TPU v7x, 32 devices: a whole 2x2x4 slice. The times are simulated.
32 devices in a mesh: rep: 4 (over y, x), fsdp: 8 (over z, core).
Axes of the slice: x: 2, y: 2, z: 4, core: 2. Of those that a mesh axis runs over, the one named last changes fastest.
Arguments:
- content_stream: bfloat16 [16384, 768], P(('rep', 'fsdp')), may hold values from -6 to 6
- query_stream: bfloat16 [16384, 768], P(('rep', 'fsdp')), may hold values from -6 to 6
- lengths: int32 [32], P(('rep', 'fsdp')), may hold values from 128 to 512, as said below
- ranking: int32 [32, 512], P(('rep', 'fsdp')), may hold values from 0 to 511, as said below
- query_weight: bfloat16 [768, 768], P('fsdp'), may hold values from -0.21875 to 0.21875
- query_bias: bfloat16 [768], P('fsdp'), may hold values from -3 to 3
- key_weight: bfloat16 [768, 768], P('fsdp'), may hold values from -0.21875 to 0.21875
- value_weight: bfloat16 [768, 768], P('fsdp'), may hold values from -0.21875 to 0.21875
- value_bias: bfloat16 [768], P('fsdp'), may hold values from -3 to 3
- output_weight: bfloat16 [768, 768], P('fsdp'), may hold values from -0.875 to 0.875
- output_bias: bfloat16 [768], P('fsdp'), may hold values from -3 to 3
- norm_gain: bfloat16 [768], P('fsdp'), may hold values from 0.5 to 1.5
- norm_shift: bfloat16 [768], P('fsdp'), may hold values from -3 to 3
- inner_weight: bfloat16 [768, 3072], P('fsdp'), may hold values from -0.21875 to 0.21875
- inner_bias: bfloat16 [3072], P('fsdp'), may hold values from -3 to 3
- outer_weight: bfloat16 [3072, 768], P('fsdp'), may hold values from -0.109375 to 0.109375
- outer_bias: bfloat16 [768], P('fsdp'), may hold values from -3 to 3
- final_gain: bfloat16 [768], P('fsdp'), may hold values from 0.5 to 1.5
- final_shift: bfloat16 [768], P('fsdp'), may hold values from -3 to 3
- bucket_bias: bfloat16 [384], P('fsdp'), may hold values from -4 to 4
- content_cotangent: bfloat16 [16384, 768], P(('rep', 'fsdp')), may hold values from -6 to 6
- query_cotangent: bfloat16 [16384, 768], P(('rep', 'fsdp')), may hold values from -6 to 6
Outputs:
- content_out: bfloat16 [16384, 768], P(('rep', 'fsdp'))
- query_out: bfloat16 [16384, 768], P(('rep', 'fsdp'))
- content_grad: float32 [16384, 768], P(('rep', 'fsdp'))
- query_grad: float32 [16384, 768], P(('rep', 'fsdp'))
- query_weight_grad: float32 [768, 768], P('fsdp')
- query_bias_grad: float32 [768], P('fsdp')
- key_weight_grad: float32 [768, 768], P('fsdp')
- value_weight_grad: float32 [768, 768], P('fsdp')
- value_bias_grad: float32 [768], P('fsdp')
- output_weight_grad: float32 [768, 768], P('fsdp')
- output_bias_grad: float32 [768], P('fsdp')
- norm_gain_grad: float32 [768], P('fsdp')
- norm_shift_grad: float32 [768], P('fsdp')
- inner_weight_grad: float32 [768, 3072], P('fsdp')
- inner_bias_grad: float32 [3072], P('fsdp')
- outer_weight_grad: float32 [3072, 768], P('fsdp')
- outer_bias_grad: float32 [768], P('fsdp')
- final_gain_grad: float32 [768], P('fsdp')
- final_shift_grad: float32 [768], P('fsdp')
- bucket_bias_grad: float32 [384], P('fsdp')
Inputs may be any that keep to these rules, and one draw needn't show every extreme that they name: `lengths`: the first sequence has all 512 slots real. `ranking`: in each sequence the slots below its length hold 0 to length - 1 once each, and the padded slots hold length to 511 once each.
All inputs are finite; a program needn't handle non-finite values.
Results may differ from a plain program's by a relative error of at most 0.019.
Values may be sent and summed in bfloat16 or wider, within the bound.
A program may use at most 256 MiB of HBM per device.

v0:
```python
import jax
import jax.numpy as jnp
from jax import lax
from jax.sharding import PartitionSpec as P

HEADS = 12
HEAD_DIM = 64
BUCKETS = 32


EPS = 1e-05
NEG = -1e30
HIGH = lax.Precision.HIGHEST
FAR_STEPS = (12, 16, 23, 32, 46, 64, 91)


def matmul(left, right):
    return jnp.dot(left, right, preferred_element_type=jnp.float32)


def matmul_tn(left, right):
    return lax.dot_general(
        left, right, (((0,), (0,)), ((), ())), preferred_element_type=jnp.float32
    )


def matmul_nt(left, right):
    return lax.dot_general(
        left, right, (((1,), (1,)), ((), ())), preferred_element_type=jnp.float32
    )


def bucket_index(seq_len):
    places = jnp.arange(seq_len, dtype=jnp.int32)
    offset = places[None, :] - places[:, None]
    distance = jnp.abs(offset)
    farther = jnp.full(distance.shape, 8, jnp.int32)
    for step_at in FAR_STEPS:
        farther = farther + (distance >= step_at).astype(jnp.int32)
    return jnp.where(distance < 8, distance, farther) + 16 * (offset > 0).astype(jnp.int32)


def visibility(length, order_rank):
    places = jnp.arange(order_rank.shape[0], dtype=jnp.int32)
    valid = places < length
    chosen = valid & (order_rank >= length - 3 * length // 20)
    open_key = valid & jnp.logical_not(chosen)
    earlier_same = order_rank[None, :] <= order_rank[:, None]
    earlier = order_rank[None, :] < order_rank[:, None]
    content_see = open_key[None, :] | chosen[None, :] & earlier_same
    query_see = open_key[None, :] | chosen[None, :] & earlier
    return (content_see, query_see)


def layer_norm(rows, gain, shift):
    mean_row = jnp.mean(rows, axis=1, keepdims=True)
    centred = rows - mean_row
    inverse = lax.rsqrt(jnp.mean(centred * centred, axis=1, keepdims=True) + EPS)
    normal = centred * inverse
    return (normal * gain + shift, normal, inverse)


def norm_back(upstream, normal, inverse, gain):
    grad_gain = jnp.sum(upstream * normal, axis=0)
    grad_shift = jnp.sum(upstream, axis=0)
    scaled = upstream * gain
    grad_rows = inverse * (
        scaled
        - jnp.mean(scaled, axis=1, keepdims=True)
        - normal * jnp.mean(scaled * normal, axis=1, keepdims=True)
    )
    return (grad_rows, grad_gain, grad_shift)


def gelu_slope(inner):
    spread = 0.5 * (1.0 + lax.erf(inner * 0.7071067811865476))
    return spread + inner * jnp.exp(-0.5 * inner * inner) * 0.3989422804014327


def scores_of(queries, key_rows, bias, visible, scale):
    raw = (
        jnp.einsum("qhe,khe->hqk", queries, key_rows, preferred_element_type=jnp.float32) * scale
        + bias
    )
    return jnp.where(visible[None], raw, NEG)


def attend_forward(items, bias, scale):
    content_q, query_q, key_rows, value_rows, length, order_rank = items
    content_see, query_see = visibility(length, order_rank)
    results = []
    for queries, visible in ((content_q, content_see), (query_q, query_see)):
        scores = scores_of(queries, key_rows, bias, visible, scale)
        row_top = jnp.max(scores, axis=2, keepdims=True)
        weights = jnp.exp(scores - row_top)
        row_total = jnp.sum(weights, axis=2, keepdims=True)
        attention_low = (weights / row_total).astype(jnp.bfloat16)
        context = jnp.einsum(
            "hqk,khe->qhe", attention_low, value_rows, preferred_element_type=jnp.float32
        )
        results.append(context.reshape(context.shape[0], -1).astype(jnp.bfloat16))
        results.append((row_top + jnp.log(row_total))[:, :, 0])
    return tuple(results)


def attend_backward(bias_total, items, bias, scale):
    content_q, query_q, key_rows, value_rows, length, order_rank, grad_cc, grad_cg, lse_c, lse_g = (
        items
    )
    content_see, query_see = visibility(length, order_rank)
    key_grad = jnp.zeros(key_rows.shape, jnp.float32)
    value_grad = jnp.zeros(value_rows.shape, jnp.float32)
    query_grads = []
    for queries, visible, grad_ctx, row_lse in (
        (content_q, content_see, grad_cc, lse_c),
        (query_q, query_see, grad_cg, lse_g),
    ):
        scores = scores_of(queries, key_rows, bias, visible, scale)
        attention = jnp.exp(scores - row_lse[:, :, None])
        grad_heads = grad_ctx.reshape(queries.shape)
        value_grad = value_grad + jnp.einsum(
            "hqk,qhe->khe",
            attention.astype(jnp.bfloat16),
            grad_heads,
            preferred_element_type=jnp.float32,
        )
        grad_attention = jnp.einsum(
            "qhe,khe->hqk", grad_heads, value_rows, preferred_element_type=jnp.float32
        )
        grad_scores = (
            attention
            * (grad_attention - jnp.sum(attention * grad_attention, axis=2, keepdims=True))
        ).astype(jnp.bfloat16)
        bias_total = bias_total + grad_scores.astype(jnp.float32)
        query_grads.append(
            jnp.einsum("hqk,khe->qhe", grad_scores, key_rows, preferred_element_type=jnp.float32)
            * scale
        )
        key_grad = (
            key_grad
            + jnp.einsum("hqk,qhe->khe", grad_scores, queries, preferred_element_type=jnp.float32)
            * scale
        )
    seq_len = key_rows.shape[0]
    return (
        bias_total,
        (
            query_grads[0].reshape(seq_len, -1),
            query_grads[1].reshape(seq_len, -1),
            key_grad.reshape(seq_len, -1),
            value_grad.reshape(seq_len, -1),
        ),
    )


def tail_forward(stream, context, weights):
    (
        w_output,
        b_output,
        gain_one,
        shift_one,
        w_inner,
        b_inner,
        w_outer,
        b_outer,
        gain_two,
        shift_two,
    ) = weights
    attended = matmul(context, w_output) + b_output
    normed, normal_one, inverse_one = layer_norm(
        stream.astype(jnp.float32) + attended, gain_one, shift_one
    )
    normed_low = normed.astype(jnp.bfloat16)
    inner = matmul(normed_low, w_inner) + b_inner
    active = jax.nn.gelu(inner, approximate=False).astype(jnp.bfloat16)
    branch = matmul(active, w_outer) + b_outer
    result, normal_two, inverse_two = layer_norm(normed + branch, gain_two, shift_two)
    return (
        result.astype(jnp.bfloat16),
        (normal_one, inverse_one, normed_low, inner, active, normal_two, inverse_two),
    )


def tail_backward(cotangent, context, kept, weights):
    w_output, gain_one, w_inner, w_outer, gain_two = weights
    normal_one, inverse_one, normed_low, inner, active, normal_two, inverse_two = kept
    grad_two, grad_gain_two, grad_shift_two = norm_back(
        cotangent.astype(jnp.float32), normal_two, inverse_two, gain_two
    )
    grad_branch = grad_two.astype(jnp.bfloat16)
    grad_outer_bias = jnp.sum(grad_branch.astype(jnp.float32), axis=0)
    grad_outer = matmul_tn(active, grad_branch)
    grad_inner_low = (matmul_nt(grad_branch, w_outer) * gelu_slope(inner)).astype(jnp.bfloat16)
    grad_inner_bias = jnp.sum(grad_inner_low.astype(jnp.float32), axis=0)
    grad_inner = matmul_tn(normed_low, grad_inner_low)
    grad_normed = grad_two + matmul_nt(grad_inner_low, w_inner)
    grad_one, grad_gain_one, grad_shift_one = norm_back(
        grad_normed, normal_one, inverse_one, gain_one
    )
    grad_attended = grad_one.astype(jnp.bfloat16)
    grad_output_bias = jnp.sum(grad_attended.astype(jnp.float32), axis=0)
    grad_output = matmul_tn(context, grad_attended)
    grad_context = matmul_nt(grad_attended, w_output).astype(jnp.bfloat16)
    return (
        grad_one,
        grad_context,
        (
            grad_output,
            grad_output_bias,
            grad_gain_one,
            grad_shift_one,
            grad_inner,
            grad_inner_bias,
            grad_outer,
            grad_outer_bias,
            grad_gain_two,
            grad_shift_two,
        ),
    )


def shards(
    content_stream,
    query_stream,
    lengths,
    ranking,
    query_weight,
    query_bias,
    key_weight,
    value_weight,
    value_bias,
    output_weight,
    output_bias,
    norm_gain,
    norm_shift,
    inner_weight,
    inner_bias,
    outer_weight,
    outer_bias,
    final_gain,
    final_shift,
    bucket_bias,
    content_cotangent,
    query_cotangent,
):
    gathered = (
        lax.all_gather(query_weight, "fsdp", axis=0, tiled=True),
        lax.all_gather(query_bias, "fsdp", axis=0, tiled=True),
        lax.all_gather(key_weight, "fsdp", axis=0, tiled=True),
        lax.all_gather(value_weight, "fsdp", axis=0, tiled=True),
        lax.all_gather(value_bias, "fsdp", axis=0, tiled=True),
        lax.all_gather(output_weight, "fsdp", axis=0, tiled=True),
        lax.all_gather(output_bias, "fsdp", axis=0, tiled=True),
        lax.all_gather(norm_gain, "fsdp", axis=0, tiled=True),
        lax.all_gather(norm_shift, "fsdp", axis=0, tiled=True),
        lax.all_gather(inner_weight, "fsdp", axis=0, tiled=True),
        lax.all_gather(inner_bias, "fsdp", axis=0, tiled=True),
        lax.all_gather(outer_weight, "fsdp", axis=0, tiled=True),
        lax.all_gather(outer_bias, "fsdp", axis=0, tiled=True),
        lax.all_gather(final_gain, "fsdp", axis=0, tiled=True),
        lax.all_gather(final_shift, "fsdp", axis=0, tiled=True),
        lax.all_gather(bucket_bias, "fsdp", axis=0, tiled=True),
    )
    (
        w_query,
        b_query,
        w_key,
        w_value,
        b_value,
        w_output,
        b_output,
        gain_one,
        shift_one,
        w_inner,
        b_inner,
        w_outer,
        b_outer,
        gain_two,
        shift_two,
        table_low,
    ) = gathered
    as_float = jnp.float32
    seq_count = lengths.shape[0]
    seq_len = ranking.shape[1]
    width = content_stream.shape[1]
    scale = HEAD_DIM ** (-0.5)
    buckets = bucket_index(seq_len)
    onehot = (
        (jnp.arange(BUCKETS, dtype=jnp.int32)[:, None, None] == buckets[None])
        .astype(jnp.bfloat16)
        .reshape(BUCKETS, seq_len * seq_len)
    )
    position_bias = matmul(table_low.reshape(HEADS, BUCKETS), onehot).reshape(
        HEADS, seq_len, seq_len
    )
    content_q = (matmul(content_stream, w_query) + b_query.astype(as_float)).astype(jnp.bfloat16)
    query_q = (matmul(query_stream, w_query) + b_query.astype(as_float)).astype(jnp.bfloat16)
    key_rows = matmul(content_stream, w_key).astype(jnp.bfloat16)
    value_rows = (matmul(content_stream, w_value) + b_value.astype(as_float)).astype(jnp.bfloat16)
    shape_four = (seq_count, seq_len, HEADS, HEAD_DIM)
    content_four = content_q.reshape(shape_four)
    query_four = query_q.reshape(shape_four)
    key_four = key_rows.reshape(shape_four)
    value_four = value_rows.reshape(shape_four)
    context_c, lse_c, context_g, lse_g = lax.map(
        lambda items: attend_forward(items, position_bias, scale),
        (content_four, query_four, key_four, value_four, lengths, ranking),
    )
    context_c = context_c.reshape(-1, width)
    context_g = context_g.reshape(-1, width)
    front = (
        w_output,
        b_output.astype(as_float),
        gain_one.astype(as_float),
        shift_one.astype(as_float),
        w_inner,
        b_inner.astype(as_float),
        w_outer,
        b_outer.astype(as_float),
        gain_two.astype(as_float),
        shift_two.astype(as_float),
    )
    content_out, kept_c = tail_forward(content_stream, context_c, front)
    query_out, kept_g = tail_forward(query_stream, context_g, front)
    (
        back_query,
        back_key,
        back_value,
        back_output,
        back_gain_one,
        back_inner,
        back_outer,
        back_gain_two,
    ) = (
        lax.all_gather(query_weight, "fsdp", axis=0, tiled=True),
        lax.all_gather(key_weight, "fsdp", axis=0, tiled=True),
        lax.all_gather(value_weight, "fsdp", axis=0, tiled=True),
        lax.all_gather(output_weight, "fsdp", axis=0, tiled=True),
        lax.all_gather(norm_gain, "fsdp", axis=0, tiled=True),
        lax.all_gather(inner_weight, "fsdp", axis=0, tiled=True),
        lax.all_gather(outer_weight, "fsdp", axis=0, tiled=True),
        lax.all_gather(final_gain, "fsdp", axis=0, tiled=True),
    )
    back_tail = (
        back_output,
        back_gain_one.astype(as_float),
        back_inner,
        back_outer,
        back_gain_two.astype(as_float),
    )
    residual_c, grad_context_c, tail_grads_c = tail_backward(
        content_cotangent, context_c, kept_c, back_tail
    )
    residual_g, grad_context_g, tail_grads_g = tail_backward(
        query_cotangent, context_g, kept_g, back_tail
    )
    tail_grads = tuple((first + second for first, second in zip(tail_grads_c, tail_grads_g)))
    (
        grad_w_output,
        grad_b_output,
        grad_gain_one,
        grad_shift_one,
        grad_w_inner,
        grad_b_inner,
        grad_w_outer,
        grad_b_outer,
        grad_gain_two,
        grad_shift_two,
    ) = tail_grads
    bias_start = jnp.zeros((HEADS, seq_len, seq_len), as_float)
    bias_total, (query_grad_c, query_grad_g, key_grad, value_grad) = lax.scan(
        lambda carry, items: attend_backward(carry, items, position_bias, scale),
        bias_start,
        (
            content_four,
            query_four,
            key_four,
            value_four,
            lengths,
            ranking,
            grad_context_c.reshape(seq_count, seq_len, width),
            grad_context_g.reshape(seq_count, seq_len, width),
            lse_c,
            lse_g,
        ),
    )
    grad_qc = query_grad_c.reshape(-1, width).astype(jnp.bfloat16)
    grad_qg = query_grad_g.reshape(-1, width).astype(jnp.bfloat16)
    grad_key = key_grad.reshape(-1, width).astype(jnp.bfloat16)
    grad_value = value_grad.reshape(-1, width).astype(jnp.bfloat16)
    grad_w_query = matmul_tn(content_stream, grad_qc) + matmul_tn(query_stream, grad_qg)
    grad_b_query = jnp.sum(grad_qc.astype(as_float), axis=0) + jnp.sum(
        grad_qg.astype(as_float), axis=0
    )
    grad_w_key = matmul_tn(content_stream, grad_key)
    grad_w_value = matmul_tn(content_stream, grad_value)
    grad_b_value = jnp.sum(grad_value.astype(as_float), axis=0)
    grad_table = lax.dot_general(
        bias_total.reshape(HEADS, -1),
        onehot.astype(as_float),
        (((1,), (1,)), ((), ())),
        precision=HIGH,
    ).reshape(-1)
    content_grad = (
        residual_c
        + matmul_nt(grad_qc, back_query)
        + matmul_nt(grad_key, back_key)
        + matmul_nt(grad_value, back_value)
    )
    query_grad = residual_g + matmul_nt(grad_qg, back_query)
    shard_grads = (
        lax.psum_scatter(grad_w_query, "fsdp", scatter_dimension=0, tiled=True),
        lax.psum_scatter(grad_b_query, "fsdp", scatter_dimension=0, tiled=True),
        lax.psum_scatter(grad_w_key, "fsdp", scatter_dimension=0, tiled=True),
        lax.psum_scatter(grad_w_value, "fsdp", scatter_dimension=0, tiled=True),
        lax.psum_scatter(grad_b_value, "fsdp", scatter_dimension=0, tiled=True),
        lax.psum_scatter(grad_w_output, "fsdp", scatter_dimension=0, tiled=True),
        lax.psum_scatter(grad_b_output, "fsdp", scatter_dimension=0, tiled=True),
        lax.psum_scatter(grad_gain_one, "fsdp", scatter_dimension=0, tiled=True),
        lax.psum_scatter(grad_shift_one, "fsdp", scatter_dimension=0, tiled=True),
        lax.psum_scatter(grad_w_inner, "fsdp", scatter_dimension=0, tiled=True),
        lax.psum_scatter(grad_b_inner, "fsdp", scatter_dimension=0, tiled=True),
        lax.psum_scatter(grad_w_outer, "fsdp", scatter_dimension=0, tiled=True),
        lax.psum_scatter(grad_b_outer, "fsdp", scatter_dimension=0, tiled=True),
        lax.psum_scatter(grad_gain_two, "fsdp", scatter_dimension=0, tiled=True),
        lax.psum_scatter(grad_shift_two, "fsdp", scatter_dimension=0, tiled=True),
        lax.psum_scatter(grad_table, "fsdp", scatter_dimension=0, tiled=True),
    )
    summed = (
        lax.psum(shard_grads[0].astype(jnp.bfloat16), "rep").astype(jnp.float32),
        lax.psum(shard_grads[1].astype(jnp.bfloat16), "rep").astype(jnp.float32),
        lax.psum(shard_grads[2].astype(jnp.bfloat16), "rep").astype(jnp.float32),
        lax.psum(shard_grads[3].astype(jnp.bfloat16), "rep").astype(jnp.float32),
        lax.psum(shard_grads[4].astype(jnp.bfloat16), "rep").astype(jnp.float32),
        lax.psum(shard_grads[5].astype(jnp.bfloat16), "rep").astype(jnp.float32),
        lax.psum(shard_grads[6].astype(jnp.bfloat16), "rep").astype(jnp.float32),
        lax.psum(shard_grads[7].astype(jnp.bfloat16), "rep").astype(jnp.float32),
        lax.psum(shard_grads[8].astype(jnp.bfloat16), "rep").astype(jnp.float32),
        lax.psum(shard_grads[9].astype(jnp.bfloat16), "rep").astype(jnp.float32),
        lax.psum(shard_grads[10].astype(jnp.bfloat16), "rep").astype(jnp.float32),
        lax.psum(shard_grads[11].astype(jnp.bfloat16), "rep").astype(jnp.float32),
        lax.psum(shard_grads[12].astype(jnp.bfloat16), "rep").astype(jnp.float32),
        lax.psum(shard_grads[13].astype(jnp.bfloat16), "rep").astype(jnp.float32),
        lax.psum(shard_grads[14].astype(jnp.bfloat16), "rep").astype(jnp.float32),
        lax.psum(shard_grads[15].astype(jnp.bfloat16), "rep").astype(jnp.float32),
    )
    return (content_out, query_out, content_grad, query_grad) + tuple(summed)


def solution(mesh):
    in_specs = (
        P(("rep", "fsdp"), None),
        P(("rep", "fsdp"), None),
        P(("rep", "fsdp")),
        P(("rep", "fsdp"), None),
        P("fsdp", None),
        P("fsdp"),
        P("fsdp", None),
        P("fsdp", None),
        P("fsdp"),
        P("fsdp", None),
        P("fsdp"),
        P("fsdp"),
        P("fsdp"),
        P("fsdp", None),
        P("fsdp"),
        P("fsdp", None),
        P("fsdp"),
        P("fsdp"),
        P("fsdp"),
        P("fsdp"),
        P(("rep", "fsdp"), None),
        P(("rep", "fsdp"), None),
    )
    out_specs = (
        P(("rep", "fsdp"), None),
        P(("rep", "fsdp"), None),
        P(("rep", "fsdp"), None),
        P(("rep", "fsdp"), None),
        P("fsdp", None),
        P("fsdp"),
        P("fsdp", None),
        P("fsdp", None),
        P("fsdp"),
        P("fsdp", None),
        P("fsdp"),
        P("fsdp"),
        P("fsdp"),
        P("fsdp", None),
        P("fsdp"),
        P("fsdp", None),
        P("fsdp"),
        P("fsdp"),
        P("fsdp"),
        P("fsdp"),
    )
    return jax.shard_map(shards, mesh=mesh, in_specs=in_specs, out_specs=out_specs, check_vma=False)
```

profile of v0, /device:TPU:0, one launch (start us, length us, event | category | flops | bytes accessed | tf_op | source)
XLA Modules:
  0.0 704.3 jit_solution(13175038152756852497)
XLA Ops:
  16.4 30.5 %all-reduce.20 = (bf16[768]{0:T(1024)(128)(2,1)S(1)}, bf16[384]{0:T(512)(128)(2,1)S(1)}, bf16[768]{0:T(1024)(128)(2,1)S(1)}, bf16[768]{0:T(1024)(128)(2,1)S(1)},...) all-reduce(bf16[768]{0:T(1024)(128)(2,1)S(1)} %dynamic-update-slice, ...), channel_id=1, replica_groups=mesh['rep'=4,'fsdp'=8] {'fsdp'}, use_global_device_ids=true, to_apply=%add | all-reduce | flops 6528 | bytes 26112
  50.5 13.2 %all-gather = bf16[8,1,384]{2,1,0:T(2,128)(2,1)S(1)} all-gather(bf16[1,1,384]{2,1,0:T(2,128)(2,1)S(1)} %reshape.452), channel_id=1, replica_groups=mesh['rep'=4,'fsdp'=8] {'fsdp'}, dimensions={0}, use_global_device_ids=true | all-gather | bytes 6912 | tf_op jit(solution)/shard_map/all_gather | solution.py:257
  65.7 5.1 fusion
  70.8 19.1 %copy.126 = f32[2,8,512,512]{3,2,1,0:T(8,128)} copy(f32[2,8,512,512]{3,1,2,0:T(8,128)S(1)} %bitcast.123) | data formatting | bytes 33554432
  90.0 10.8 %slice = f32[12,512,512]{2,1,0:T(8,128)} slice(f32[16,512,512]{2,1,0:T(8,128)} %bitcast.124), slice={[0:12], [0:512], [0:512]} | slice | bytes 25165824 | tf_op jit(solution)/shard_map/reshape | solution.py:293
  100.8 12.9 %copy.93 = f32[12,512,512]{1,2,0:T(8,128)} copy(f32[12,512,512]{2,1,0:T(8,128)} %slice) | data formatting | bytes 25165824 | tf_op jit(solution)/shard_map/reshape | solution.py:293
  117.6 3.2 add_convert_fusion.2
  125.4 3.2 convolution_convert_fusion.2
  130.1 6.6 fusion.100
  136.7 13.6 %fusion.102 = (f32[12,512]{1,0:T(8,128)S(1)}, f32[12,512,512]{1,2,0:T(8,128)}) fusion(f32[12,512,512]{1,2,0:T(8,128)} %copy.93, bf16[512,12,64]{0,2,1:T(8,128)(2,1)S(1)} %bitcast.141, bf16[512,12,64]{0,2,1:T(8,128)(2,1)S(1)} %bitcast.126, pred[512,512]{0,1:T(8,128)(4,1)S(1)} %copy-done.39), kind=kOutput, calls=%fused_computation.223 | convolution fusion | flops 415229952 | bytes 27025408 | tf_op jit(solution)/shard_map/while/body/eval_jaxpr/qhe,khe->hqk/dot_general | solution.py:82
  152.2 6.4 fusion.4
  158.6 7.7 %fusion.65 = bf16[12,64,512]{2,1,0:T(8,128)(2,1)} fusion(bf16[512,12,64]{0,2,1:T(8,128)(2,1)S(1)} %bitcast.131, f32[12,512,512]{1,2,0:T(8,128)} %get-tuple-element.255, f32[12,512]{1,0:T(8,128)S(1)} %fusion.4, f32[12,512]{1,0:T(8,128)S(1)} %get-tuple-element.254), kind=kOutput, calls=%fused_computation.155 | convolution fusion | flops 412483584 | bytes 14204928 | tf_op jit(solution)/shard_map/while/body/eval_jaxpr/hqk,khe->qhe/dot_general | solution.py:98
  166.4 2.5 fusion.64
  169.0 2.4 fusion.101
  174.2 5.3 fusion.95
  179.6 2.6 copy-done.80
  182.2 31.6 %fusion.13 = (bf16[512,3072]{1,0:T(8,128)(2,1)}, bf16[512,3072]{1,0:T(8,128)(2,1)}, f32[512,3072]{1,0:T(8,128)}) fusion(f32[3072]{0:T(1024)S(1)} %bitcast.156, f32[512,3072]{1,0:T(8,128)S(1)} %fusion.95, bf16[768,3072]{1,0:T(8,128)(2,1)S(1)} %copy-done.67, f32[512,768]{1,0:T(8,128)S(1)} %get-tuple-element.253, f32[512]{0:T(512)S(1)} %add_rsqrt_fusion.1, ...), kind=kOutput, calls=%fused_computation.32 | convolution fusion | flops 2625503232 | bytes 25188352 | tf_op jit(solution)/shard_map/dot_general | solution.py:18
  213.9 6.2 fusion.105
  220.5 2.8 fusion.104
  225.9 2.9 convert_reduce_fusion.4
  228.8 7.5 %convert_reduce_fusion.1 = (f32[3072]{0:T(1024)S(1)}, bf16[512,3072]{1,0:T(8,128)(2,1)S(1)}) fusion(f32[512,3072]{1,0:T(8,128)} %copy-done.80, f32[3072]{0:T(1024)S(1)} %bitcast.157, bf16[3072,768]{1,0:T(8,128)(2,1)S(1)} %copy-done.68, f32[512,768]{1,0:T(8,128)S(1)} %get-tuple-element.237), kind=kOutput, calls=%fused_computation.48 | convolution fusion | flops 2436756480 | bytes 15753216 | tf_op jit(solution)/shard_map/dot_general | solution.py:28
  236.4 3.1 multiply_reduce_fusion.3
  239.5 6.6 convert_reduce_fusion
  246.2 3.3 convert_reduce_fusion.7
  254.3 2.6 convolution_convert_fusion.1
  257.1 3.9 convolution_convert_fusion
  262.5 6.7 fusion.26
  269.2 6.9 convert_reduce_fusion.8
  279.2 3.1 copy.122
  282.4 9.3 %multiply_reduce_fusion.1 = (f32[12,512]{1,0:T(8,128)S(1)}, f32[12,512,512]{1,2,0:T(8,128)}) fusion(f32[12,512,512]{1,2,0:T(8,128)} %get-tuple-element.255, f32[12,512]{1,0:T(8,128)S(1)} %get-tuple-element.284, bf16[512,12,64]{0,2,1:T(8,128)(2,1)} %bitcast.138, bf16[512,12,64]{0,2,1:T(8,128)(2,1)S(1)} %bitcast.133), kind=kOutput, calls=%fused_computation.11 | convolution fusion | flops 412084224 | bytes 26787840 | tf_op jit(solution)/shard_map/while/body/eval_jaxpr/qhe,khe->hqk/dot_general | solution.py:127
  291.7 8.8 %multiply_reduce_fusion = (f32[12,512]{1,0:T(8,128)S(1)}, f32[12,512,512]{1,2,0:T(8,128)}) fusion(f32[12,512,512]{1,2,0:T(8,128)} %copy-done, f32[12,512]{1,0:T(8,128)S(1)} %get-tuple-element.283, bf16[512,12,64]{0,2,1:T(8,128)(2,1)S(1)} %bitcast.136, bf16[512,12,64]{0,2,1:T(8,128)(2,1)S(1)} %bitcast.134), kind=kOutput, calls=%fused_computation.8 | convolution fusion | flops 412084224 | bytes 26787840 | tf_op jit(solution)/shard_map/while/body/eval_jaxpr/qhe,khe->hqk/dot_general | solution.py:127
  300.5 27.2 %convert_add_fusion = (f32[12,512,512]{1,2,0:T(8,128)}, bf16[12,512,512]{1,2,0:T(8,128)(2,1)}, bf16[12,512,512]{1,2,0:T(8,128)(2,1)}) fusion(f32[12,512,512]{1,2,0:T(8,128)} %get-tuple-element.266, f32[12,512]{1,0:T(8,128)S(1)} %get-tuple-element.265, f32[12,512,512]{1,2,0:T(8,128)} %copy-done, f32[12,512]{1,0:T(8,128)S(1)} %get-tuple-element.283, ...), kind=kLoop, calls=%fused_computation.6 | loop fusion | flops 34603008 | bytes 75595776 | tf_op jit(solution)/shard_map/while/body/eval_jaxpr/add | solution.py:134
  327.7 4.9 fusion.107
  337.8 3.1 copy.120
  341.0 3.9 convert_reduce_fusion.10
  345.7 4.0 convert_reduce_fusion.9
  352.0 3.1 copy.118
  355.3 5.5 fusion.93
  360.8 5.7 convolution_add_fusion.1
  366.6 5.3 fusion.87
  371.9 5.4 convolution_add_fusion
  379.9 18.5 %copy.106 = f32[12,512,512]{2,0,1:T(8,128)} copy(f32[12,512,512]{1,2,0:T(8,128)} %get-tuple-element.220) | data formatting | bytes 25165824 | tf_op jit(solution)/shard_map/while/body/eval_jaxpr/add | solution.py:134
  403.6 10.0 %reduce-scatter.19.cloned.1.call-done = f32[96,768]{1,0:T(8,128)} async-done(((f32[768,768]{1,0:T(8,128)}), f32[96,768]{1,0:T(8,128)}) %reduce-scatter.19.cloned.1.call-update) | async-done | bytes 294928
  415.3 99.3 %reduce-scatter.15.cloned.1.call-done = f32[96,3072]{1,0:T(8,128)} async-done(((f32[768,3072]{1,0:T(8,128)}), f32[96,3072]{1,0:T(8,128)}) %reduce-scatter.15.cloned.1.call-update) | async-done | bytes 1179664 | tf_op jit(solution)/shard_map/reduce_scatter | solution.py:421
  516.8 97.9 %reduce-scatter.17.cloned.1.call-done = f32[384,768]{1,0:T(8,128)} async-done(((f32[3072,768]{1,0:T(8,128)}), f32[384,768]{1,0:T(8,128)}) %reduce-scatter.17.cloned.1.call-update) | async-done | bytes 1179664 | tf_op jit(solution)/shard_map/reduce_scatter | solution.py:423
  616.9 20.1 %fusion.68 = f32[12,32]{1,0:T(8,128)S(1)} fusion(f32[12,512,512]{2,0,1:T(8,128)} %copy.106, s32[512,512]{1,0:T(8,128)S(1)} %select_add_fusion), kind=kOutput, calls=%fused_computation.162 | convolution fusion | flops 1216348160 | bytes 13633024 | tf_op jit(solution)/shard_map/dot_general | solution.py:398
  637.4 26.4 %all-reduce.19 = (bf16[768]{0:T(1024)(128)(2,1)S(1)}, bf16[768]{0:T(1024)(128)(2,1)S(1)}, bf16[768]{0:T(1024)(128)(2,1)S(1)}, bf16[768]{0:T(1024)(128)(2,1)S(1)}...) all-reduce(f32[768]{0:T(1024)S(1)} %add.450, ...), channel_id=3, replica_groups=mesh['rep'=4,'fsdp'=8] {'fsdp'}, use_global_device_ids=true, to_apply=%region_26.27.clone | all-reduce | flops 9600 | bytes 57600
  664.5 10.0 %all-reduce.21 = (bf16[96]{0:T(256)(128)(2,1)S(1)}, bf16[96]{0:T(256)(128)(2,1)S(1)}, bf16[96]{0:T(256)(128)(2,1)S(1)}, bf16[96]{0:T(256)(128)(2,1)S(1)}, bf16[9...) all-reduce(bf16[96]{0:T(256)(128)(2,1)S(1)} %dynamic-slice.50, ...), channel_id=1, replica_groups=mesh['rep'=4,'fsdp'=8] {'rep'}, use_global_device_ids=true, to_apply=%region_27.28 | all-reduce | flops 1200 | bytes 4800 | tf_op jit(solution)/shard_map/psum | solution.py:431
  (327 shorter events, 83.9 us)
Async XLA Ops:
  7.2 7.7 %copy-start.74 = (bf16[96]{0:T(256)(128)(2,1)S(1)}, bf16[96]{0:T(256)(128)(2,1)}, u32[]{:S(2)}) copy-start(bf16[96]{0:T(256)(128)(2,1)} %param.34) | copy-start | bytes 580
  7.3 7.9 %copy-start.75 = (bf16[96]{0:T(256)(128)(2,1)S(1)}, bf16[96]{0:T(256)(128)(2,1)}, u32[]{:S(2)}) copy-start(bf16[96]{0:T(256)(128)(2,1)} %param.32) | copy-start | bytes 580
  7.3 8.1 %copy-start.76 = (bf16[96]{0:T(256)(128)(2,1)S(1)}, bf16[96]{0:T(256)(128)(2,1)}, u32[]{:S(2)}) copy-start(bf16[96]{0:T(256)(128)(2,1)} %param.27) | copy-start | bytes 580
  7.3 8.4 %copy-start.77 = (bf16[96]{0:T(256)(128)(2,1)S(1)}, bf16[96]{0:T(256)(128)(2,1)}, u32[]{:S(2)}) copy-start(bf16[96]{0:T(256)(128)(2,1)} %param.30) | copy-start | bytes 580
  7.3 8.6 %copy-start.78 = (bf16[96]{0:T(256)(128)(2,1)S(1)}, bf16[96]{0:T(256)(128)(2,1)}, u32[]{:S(2)}) copy-start(bf16[96]{0:T(256)(128)(2,1)} %param.40) | copy-start | bytes 580
  7.3 8.8 %copy-start.79 = (bf16[48]{0:T(256)(128)(2,1)S(1)}, bf16[48]{0:T(256)(128)(2,1)}, u32[]{:S(2)}) copy-start(bf16[48]{0:T(256)(128)(2,1)} %param.41) | copy-start | bytes 292
  7.3 107.7 %all-gather.8.cloned.1.call-start = ((), (), s32[]{:S(2)}) async-start(), calls=%async_computation.6 | async-start | bytes 1327104 | tf_op jit(solution)/shard_map/all_gather | solution.py:250
  8.0 109.5 %all-gather.10.cloned.1.call-start = ((), (), s32[]{:S(2)}) async-start(), calls=%async_computation.7 | async-start | bytes 1327104 | tf_op jit(solution)/shard_map/all_gather | solution.py:247
  8.8 116.6 %all-gather.12.cloned.1.call-start = ((), (), s32[]{:S(2)}) async-start(), calls=%async_computation.8 | async-start | bytes 1327104 | tf_op jit(solution)/shard_map/all_gather | solution.py:249
  9.5 159.4 %all-gather.14.cloned.1.call-start = ((), (), s32[]{:S(2)}) async-start(), calls=%async_computation.9 | async-start | bytes 1327104 | tf_op jit(solution)/shard_map/all_gather | solution.py:252
  10.1 164.1 %all-gather.16.cloned.1.call-start = ((), (), s32[]{:S(2)}) async-start(), calls=%async_computation.10 | async-start | bytes 5308416 | tf_op jit(solution)/shard_map/all_gather | solution.py:256
  10.7 203.2 %all-gather.18.cloned.1.call-start = ((), (), s32[]{:S(2)}) async-start(), calls=%async_computation.11 | async-start | bytes 5308416 | tf_op jit(solution)/shard_map/all_gather | solution.py:258
  11.3 387.1 %reduce-scatter.13.cloned.1.call-start = ((), (), s32[]{:S(2)}) async-start(), calls=%async_computation.12 | async-start | bytes 2654208 | tf_op jit(solution)/shard_map/reduce_scatter | solution.py:417
  100.7 12.9 %copy-start.52 = (s32[1,512]{1,0:T(1,128)S(1)}, s32[1,512]{1,0:T(1,128)}, u32[]{:S(2)}) copy-start(s32[1,512]{1,0:T(1,128)} %param.25) | copy-start | bytes 6148
  100.7 14.3 %copy-start.16 = (bf16[512,768]{1,0:T(8,128)(2,1)S(1)}, bf16[512,768]{1,0:T(8,128)(2,1)}, u32[]{:S(2)}) copy-start(bf16[512,768]{1,0:T(8,128)(2,1)} %param.22) | copy-start | bytes 2359300
  100.7 14.3 %copy-start.64 = (f32[768]{0:T(1024)S(1)}, f32[768]{0:T(1024)}, u32[]{:S(2)}) copy-start(f32[768]{0:T(1024)} %convert_element_type.393) | copy-start | bytes 9220
  117.5 48.8 %copy-start.6 = (bf16[512,768]{0,1:T(8,128)(2,1)}, bf16[512,768]{0,1:T(8,128)(2,1)S(1)}, u32[]{:S(2)}) copy-start(bf16[512,768]{0,1:T(8,128)(2,1)S(1)} %copy.90) | copy-start | bytes 2359300
  122.2 7.8 %copy-start.9 = (bf16[512,768]{0,1:T(8,128)(2,1)}, bf16[512,768]{0,1:T(8,128)(2,1)S(1)}, u32[]{:S(2)}) copy-start(bf16[512,768]{0,1:T(8,128)(2,1)S(1)} %copy.95) | copy-start | bytes 2359300
  125.3 11.4 %copy-start.11 = (bf16[512,768]{0,1:T(8,128)(2,1)}, bf16[512,768]{0,1:T(8,128)(2,1)S(1)}, u32[]{:S(2)}) copy-start(bf16[512,768]{0,1:T(8,128)(2,1)S(1)} %copy.91) | copy-start | bytes 2359300
  136.7 29.7 %copy-start = (f32[12,512,512]{1,2,0:T(8,128)}, f32[12,512,512]{1,2,0:T(8,128)S(1)}, u32[]{:S(2)}) copy-start(f32[12,512,512]{1,2,0:T(8,128)S(1)} %get-tuple-element.251) | copy-start | bytes 37748740
  150.4 8.2 %copy-start.47 = (f32[12,512]{1,0:T(8,128)}, f32[12,512]{1,0:T(8,128)S(1)}, u32[]{:S(2)}) copy-start(f32[12,512]{1,0:T(8,128)S(1)} %get-tuple-element.254) | copy-start | bytes 73732
  158.6 7.8 %copy-start.49 = (f32[12,512]{1,0:T(8,128)}, f32[12,512]{1,0:T(8,128)S(1)}, u32[]{:S(2)}) copy-start(f32[12,512]{1,0:T(8,128)S(1)} %fusion.4) | copy-start | bytes 73732
  174.2 8.0 %copy-start.60 = (f32[8,1,384]{2,1,0:T(1,128)S(1)}, f32[8,1,384]{2,1,0:T(1,128)}, u32[]{:S(2)}) copy-start(f32[8,1,384]{2,1,0:T(1,128)} %convert_element_type.504) | copy-start | bytes 36868
  174.2 8.0 %copy-start.67 = (bf16[768,3072]{1,0:T(8,128)(2,1)S(1)}, bf16[768,3072]{1,0:T(8,128)(2,1)}, u32[]{:S(2)}) copy-start(bf16[768,3072]{1,0:T(8,128)(2,1)} %all-gather.16.cloned.1.call-done) | copy-start | bytes 14155780
  182.2 31.7 %copy-start.61 = (f32[768]{0:T(1024)S(1)}, f32[768]{0:T(1024)}, u32[]{:S(2)}) copy-start(f32[768]{0:T(1024)} %convert_element_type.415) | copy-start | bytes 9220
  225.9 10.5 %slice-start = ((s8[4718592]{0:T(1024)(128)(4,1)}), s8[4194304]{0:T(1024)(128)(4,1)S(1)}, s32[]{:S(2)}) async-start(s8[4718592]{0:T(1024)(128)(4,1)} %bitcast.159), calls=%async_computation.19 | async-start | bytes 8388608
  228.8 7.6 %copy-start.24 = (f32[512,768]{1,0:T(8,128)}, f32[512,768]{1,0:T(8,128)S(1)}, u32[]{:S(2)}) copy-start(f32[512,768]{1,0:T(8,128)S(1)} %get-tuple-element.237) | copy-start | bytes 4718596
  228.8 17.3 %copy-start.22 = (f32[512,768]{1,0:T(8,128)}, f32[512,768]{1,0:T(8,128)S(1)}, u32[]{:S(2)}) copy-start(f32[512,768]{1,0:T(8,128)S(1)} %get-tuple-element.224) | copy-start | bytes 4718596
  228.8 7.6 %slice-start.1 = ((s8[4718592]{0:T(1024)(128)(4,1)}), s8[524288]{0:T(1024)(128)(4,1)S(1)}, s32[]{:S(2)}) async-start(s8[4718592]{0:T(1024)(128)(4,1)} %bitcast.159), calls=%async_computation.20 | async-start | bytes 1048576
  254.2 145.9 %reduce-scatter.23.cloned.1.call-start = ((), (), s32[]{:S(2)}) async-start(), calls=%async_computation.17 | async-start | bytes 2654208
  257.1 12.1 %copy-start.8 = (bf16[512,768]{0,1:T(8,128)(2,1)}, bf16[512,768]{0,1:T(8,128)(2,1)S(1)}, u32[]{:S(2)}) copy-start(bf16[512,768]{0,1:T(8,128)(2,1)S(1)} %copy.98) | copy-start | bytes 2359300
  269.2 7.8 %copy-start.18 = (bf16[512,768]{1,0:T(8,128)(2,1)S(1)}, bf16[512,768]{1,0:T(8,128)(2,1)}, u32[]{:S(2)}) copy-start(bf16[512,768]{1,0:T(8,128)(2,1)} %param.22) | copy-start | bytes 2359300
  282.4 119.5 %reduce-scatter.21.cloned.1.call-start = ((), (), s32[]{:S(2)}) async-start(), calls=%async_computation.16 | async-start | bytes 2654208
  300.5 27.2 %copy-start.12 = (bf16[512,768]{0,1:T(8,128)(2,1)S(1)}, bf16[512,768]{0,1:T(8,128)(2,1)}, u32[]{:S(2)}) copy-start(bf16[512,768]{0,1:T(8,128)(2,1)} %copy-done.11) | copy-start | bytes 2359300
  340.9 72.6 %reduce-scatter.19.cloned.1.call-start = ((), (), s32[]{:S(2)}) async-start(), calls=%async_computation.15 | async-start | bytes 2654208
  355.1 159.5 %reduce-scatter.15.cloned.1.call-start = ((), (), s32[]{:S(2)}) async-start(), calls=%async_computation.13 | async-start | bytes 10616832 | tf_op jit(solution)/shard_map/reduce_scatter | solution.py:421
  366.6 248.1 %reduce-scatter.17.cloned.1.call-start = ((), (), s32[]{:S(2)}) async-start(), calls=%async_computation.14 | async-start | bytes 10616832 | tf_op jit(solution)/shard_map/reduce_scatter | solution.py:423
  377.3 310.0 %all-reduce.25.cloned.1.call-start = ((), (), s32[]{:S(2)}) async-start(), calls=%async_computation.18 | async-start | bytes 3833856 | tf_op jit(solution)/shard_map/psum | solution.py:430
  616.8 20.4 %copy-start.58 = (f32[768]{0:T(1024)S(1)}, f32[768]{0:T(1024)}, u32[]{:S(2)}) copy-start(f32[768]{0:T(1024)} %get-tuple-element.173) | copy-start | bytes 9220
  616.8 20.4 %copy-start.59 = (f32[768]{0:T(1024)S(1)}, f32[768]{0:T(1024)}, u32[]{:S(2)}) copy-start(f32[768]{0:T(1024)} %get-tuple-element.245) | copy-start | bytes 9220
  616.8 20.4 %copy-start.56 = (f32[768]{0:T(1024)S(1)}, f32[768]{0:T(1024)}, u32[]{:S(2)}) copy-start(f32[768]{0:T(1024)} %get-tuple-element.182) | copy-start | bytes 9220
  616.8 20.4 %copy-start.57 = (f32[768]{0:T(1024)S(1)}, f32[768]{0:T(1024)}, u32[]{:S(2)}) copy-start(f32[768]{0:T(1024)} %get-tuple-element.242) | copy-start | bytes 9220
  616.9 20.5 %copy-start.53 = (f32[768]{0:T(1024)S(1)}, f32[768]{0:T(1024)}, u32[]{:S(2)}) copy-start(f32[768]{0:T(1024)} %get-tuple-element.223) | copy-start | bytes 9220
  616.9 20.5 %copy-start.54 = (f32[768]{0:T(1024)S(1)}, f32[768]{0:T(1024)}, u32[]{:S(2)}) copy-start(f32[768]{0:T(1024)} %get-tuple-element.236) | copy-start | bytes 9220
  616.9 62.9 %copy-start.21 = (bf16[12,64,512]{2,1,0:T(8,128)(2,1)S(1)}, bf16[12,64,512]{2,1,0:T(8,128)(2,1)}, u32[]{:S(2)}) copy-start(bf16[12,64,512]{2,1,0:T(8,128)(2,1)} %copy-done.20) | copy-start | bytes 2359300
  637.0 45.0 %copy-start.33 = (bf16[12,64,512]{2,1,0:T(8,128)(2,1)S(1)}, bf16[12,64,512]{2,1,0:T(8,128)(2,1)}, u32[]{:S(2)}) copy-start(bf16[12,64,512]{2,1,0:T(8,128)(2,1)} %copy-done.32) | copy-start | bytes 2359300
  674.6 7.5 %copy-start.69 = (bf16[768,768]{1,0:T(8,128)(2,1)S(1)}, bf16[768,768]{1,0:T(8,128)(2,1)}, u32[]{:S(2)}) copy-start(bf16[768,768]{1,0:T(8,128)(2,1)} %all-gather.12.cloned.1.call-done) | copy-start | bytes 3538948
  687.3 9.2 %copy-start.46 = (bf16[384,768]{1,0:T(8,128)(2,1)S(1)}, bf16[384,768]{1,0:T(8,128)(2,1)}, u32[]{:S(2)}) copy-start(bf16[384,768]{1,0:T(8,128)(2,1)} %get-tuple-element.219) | copy-start | bytes 1769476
  (49 other events, 187.7 us)
Sparse Core Ops, SparseCore 0:
  9.8 25.6 all-gather.7
  37.2 22.1 all-gather.9
  61.0 22.4 all-gather.11
  85.0 22.4 all-gather.13
  108.9 51.4 all-gather.15
  162.0 50.5 all-gather.17
  254.3 34.6 reduce-scatter.12
  291.3 35.5 reduce-scatter.22
  341.0 34.6 reduce-scatter.20
  377.9 35.5 reduce-scatter.18
  415.9 98.6 reduce-scatter.14
  516.8 97.8 reduce-scatter.16
  619.6 66.3 all-reduce.24
where the time goes:
time: 709 us; the launch traced here: 704 us
  matrix products  228 us (32%)
  waiting for transfers between devices  211 us (30%)
  local copies, waits for them, and re-layouts  99.3 us (14%)
  blocking collectives  80.1 us (11%)
  other arithmetic  65.5 us (9%)
  between operations  19.5 us (3%)
    reduce_scatter x1, waiting for transfers between devices, shards(): lax.psum_scatter(grad_w_inner, 'fsdp', scatter_dimension=0, tiled=True)  99.3 us
    reduce_scatter x1, waiting for transfers between devices, shards(): lax.psum_scatter(grad_w_outer, 'fsdp', scatter_dimension=0, tiled=True)  97.9 us
    dot_general x11, matrix products, matmul(): return jnp.dot(left, right, preferred_element_type=jnp.float32)  64.7 us
    unnamed x2, blocking collectives  56.9 us
    unnamed x210, local copies, waits for them, and re-layouts  50.6 us
    dot_general x10, matrix products, matmul_nt(): lax.dot_general(left, right, (((1,), (1,)), ((), ())), preferred_element_...  34.1 us
    dot_general x10, matrix products, matmul_tn(): lax.dot_general(left, right, (((0,), (0,)), ((), ())), preferred_element_...  32.1 us
    add x1, other arithmetic, attend_backward(): bias_total = bias_total + grad_scores.astype(jnp.float32)  27.2 us
  transfers between devices with their start and end apart: 13, of which 3 were waited for; matrix products, arithmetic and copies ran while one was open for 47% of the time, Pallas kernels for 0%

commit v1 on v0

v1 whole, which is shorter than its diff:
```python
import functools

import jax
import jax.numpy as jnp
from jax import lax
from jax.experimental import pallas as pl
from jax.experimental.pallas import tpu as pltpu
from jax.sharding import PartitionSpec as P

HEADS = 12
HEAD_DIM = 64
PAIRS = HEADS // 2
BUCKETS = 32
SEQ = 512
ROWS = 2 * SEQ
D = 768
FF = 3072
TILE = 256
TILES = FF // TILE
EPS = 1e-05
NEG = -1e30
LOG2E = 1.4426950408889634
SCALE = HEAD_DIM**-0.5
FAR_STEPS = (12, 16, 23, 32, 46, 64, 91)
F32 = jnp.float32
BF16 = jnp.bfloat16
VMEM_LIMIT = 60 * 2**20

TAIL_P = 0.28
TAIL = (
    0.11608706693762069,
    0.07021928496801585,
    0.26212226118724974,
    -0.22858899246095166,
    0.3847049667747488,
    -0.10454457204169064,
)


def mm(a, b):
    return jnp.dot(a, b, preferred_element_type=F32)


def mm_nt(a, b):
    return lax.dot_general(a, b, (((1,), (1,)), ((), ())), preferred_element_type=F32)


def mm_tn(a, b):
    return lax.dot_general(a, b, (((0,), (0,)), ((), ())), preferred_element_type=F32)


def bucket_of(offset):
    distance = jnp.abs(offset)
    farther = jnp.full(distance.shape, 8, jnp.int32)
    for step_at in FAR_STEPS:
        farther = farther + jnp.where(distance >= step_at, 1, 0)
    return jnp.where(distance < 8, distance, farther) + jnp.where(offset > 0, 16, 0)


def normal_parts(x):
    size = jnp.abs(x)
    t = 1.0 / (1.0 + TAIL_P * size)
    poly = jnp.full(x.shape, TAIL[-1], F32)
    for c in TAIL[-2::-1]:
        poly = poly * t + c
    bell = jnp.exp2(x * x * (-0.5 * LOG2E))
    tail = poly * t * bell
    return jnp.where(x < 0, tail, 1.0 - tail), bell * 0.3989422804014327


def ds(start, size):
    return pl.ds(pl.multiple_of(start, size), size)


def build_masks(len_ref, rank_ref, mask_s):
    n = len_ref[0]
    rank = rank_ref[...]
    place = lax.broadcasted_iota(jnp.int32, (1, SEQ), 1)
    valid = place < n
    chosen = valid & (rank >= n - 3 * n // 20)
    key = jnp.where(chosen, rank, jnp.where(valid, -1, 2 * SEQ)).astype(F32)
    column = jnp.broadcast_to(rank.astype(F32), (128, SEQ)).T
    for s in range(2):
        for j in range(SEQ // 128):
            seen = jnp.broadcast_to(key[:, j * 128 : (j + 1) * 128], (SEQ, 128)) <= column - s
            mask_s[s, :, j * 128 : (j + 1) * 128] = jnp.where(seen, 0.0, NEG)


def build_strip(tab_ref, strip_s):
    offset = lax.broadcasted_iota(jnp.int32, (128, 1024), 1) - 512
    bucket = lax.broadcasted_iota(jnp.int32, (128, 1024), 0)
    onehot = jnp.where(bucket_of(offset) == bucket, 1.0, 0.0).astype(BF16)
    line = mm(tab_ref[...], onehot) * LOG2E
    for h in range(HEADS):
        wide = jnp.broadcast_to(line[h : h + 1], (128, 1024))
        strip_s[h] = pltpu.roll(wide, 0, 1, stride=1, stride_axis=0)[:, 128:]


def project(x_ref, y_ref, vec_ref, w_s, q_s, k_s, v_s):
    for pair in range(0, PAIRS, 2):
        cols = slice(pair * 128, pair * 128 + 256)
        x = x_ref[...]
        parts = (
            (q_s, 0, mm(x, w_s[0, :, cols]) + vec_ref[0:1, cols]),
            (q_s, 1, mm(y_ref[...], w_s[0, :, cols]) + vec_ref[0:1, cols]),
            (k_s, None, mm(x, w_s[1, :, cols])),
            (v_s, None, mm(x, w_s[2, :, cols]) + vec_ref[1:2, cols]),
        )
        for ref, s, value in parts:
            value = value.astype(BF16)
            for e in range(2):
                piece = value[:, e * 128 : (e + 1) * 128]
                if s is None:
                    ref[pair + e] = piece
                else:
                    ref[s, pair + e] = piece


def attend(q_s, k_s, v_s, strip_s, mask_s, p_st, ctx_s, hp, slot):
    lane = lax.broadcasted_iota(jnp.int32, (SEQ, 128), 1)
    k = k_s[hp]
    v = v_s[hp]
    for s in range(2):
        q = q_s[s, hp]
        outs = []
        for e in range(2):
            own = (lane < 64) if e == 0 else (lane >= 64)
            scores = mm_nt(jnp.where(own, q, jnp.zeros_like(q)), k)
            for i in range(SEQ // 128):
                rows = slice(i * 128, (i + 1) * 128)
                blk = (
                    scores[rows] * (SCALE * LOG2E)
                    + strip_s[2 * hp + e, :, (3 - i) * 128 : (3 - i) * 128 + SEQ]
                    + mask_s[s, rows, :]
                )
                top = jnp.max(blk, axis=1, keepdims=True)
                w = jnp.exp2(blk - top)
                w = w * (1.0 / jnp.sum(w, axis=1, keepdims=True))
                p_st[slot, e, s, rows, :] = w.astype(BF16)
            outs.append(mm(p_st[slot, e, s], v))
        ctx_s[s * SEQ : (s + 1) * SEQ, ds(hp * 128, 128)] = jnp.where(
            lane < 64, outs[0], outs[1]
        ).astype(BF16)


def norm_stats(r):
    mean = jnp.mean(r, axis=1, keepdims=True)
    centred = r - mean
    inverse = lax.rsqrt(jnp.mean(centred * centred, axis=1, keepdims=True) + EPS)
    return centred * inverse, inverse


def forward_kernel(
    x_ref, y_ref, len_ref, rank_ref, vec_ref, tab_ref, wa_h, wi_h, wo_h,
    oc_ref, oq_ref, q_h, k_h, v_h, p_h, ctx_h, n1_h, inv1_h, nl_h, act_h, slope_h, n2_h, inv2_h,
    wa_s, wi_s, wo_s, q_s, k_s, v_s, ctx_s, nl_s, n1_s, br_s, inv1_s, inv2_s, w_sem, o_sem, st_sem,
):
    loads = [pltpu.make_async_copy(wa_h.at[i], wa_s.at[i], w_sem.at[i]) for i in range(4)]
    loads.append(pltpu.make_async_copy(wi_h, wi_s, w_sem.at[4]))
    loads.append(pltpu.make_async_copy(wo_h, wo_s, w_sem.at[5]))
    for c in loads:
        c.start()
    stores = []

    def keep(src, dst):
        pltpu.make_async_copy(src, dst, o_sem.at[len(stores)]).start()
        stores.append((src, dst))

    def attention(strip_s, mask_s, p_st):
        build_masks(len_ref, rank_ref, mask_s)
        build_strip(tab_ref, strip_s)
        for c in loads[:3]:
            c.wait()
        project(x_ref, y_ref, vec_ref, wa_s, q_s, k_s, v_s)
        keep(q_s, q_h)
        keep(k_s, k_h)
        keep(v_s, v_h)

        def store(hp, slot):
            return pltpu.make_async_copy(p_st.at[slot], p_h.at[hp], st_sem.at[slot])

        def step(hp, carry):
            slot = (hp % 2)

            @pl.when(hp >= 2)
            def _():
                store(hp - 2, slot).wait()

            attend(q_s, k_s, v_s, strip_s, mask_s, p_st, ctx_s, hp, slot)
            store(hp, slot).start()
            return carry

        lax.fori_loop(0, PAIRS, step, 0)
        store(PAIRS - 2, 0).wait()
        store(PAIRS - 1, 1).wait()

    pl.run_scoped(
        attention,
        pltpu.VMEM((HEADS, 128, 896), F32),
        pltpu.VMEM((2, SEQ, SEQ), F32),
        pltpu.VMEM((2, 2, 2, SEQ, SEQ), BF16),
    )
    keep(ctx_s, ctx_h)

    loads[3].wait()
    for s, in_ref in ((0, x_ref), (1, y_ref)):
        def first(i, carry, s=s, in_ref=in_ref):
            own = ds(i * 256, 256)
            rows = ds(s * SEQ + i * 256, 256)
            r = in_ref[own, :].astype(F32) + mm(ctx_s[rows, :], wa_s[3]) + vec_ref[2:3, :]
            n, inverse = norm_stats(r)
            n1_s[rows, :] = n
            inv1_s[rows, :] = jnp.broadcast_to(inverse, (256, 128))
            nl_s[rows, :] = (n * vec_ref[3:4, :] + vec_ref[4:5, :]).astype(BF16)
            return carry

        lax.fori_loop(0, SEQ // 256, first, 0)
    keep(n1_s, n1_h)
    keep(inv1_s, inv1_h)
    keep(nl_s, nl_h)

    loads[4].wait()
    loads[5].wait()
    br_s[...] = jnp.zeros_like(br_s)

    def feed(act_st, slope_st):
        def pair(t, slot):
            return (
                pltpu.make_async_copy(act_st.at[slot], act_h.at[t], st_sem.at[slot]),
                pltpu.make_async_copy(slope_st.at[slot], slope_h.at[t], st_sem.at[2 + slot]),
            )

        def step(t, carry):
            slot = (t % 2)

            @pl.when(t >= 2)
            def _():
                for c in pair(t - 2, slot):
                    c.wait()

            cols = ds(t * TILE, TILE)
            inner = mm(nl_s[...], wi_s[:, cols]) + vec_ref[pl.ds(8 + (t // 3), 1), ds((t % 3) * TILE, TILE)]
            spread, bell = normal_parts(inner)
            act = (inner * spread).astype(BF16)
            act_st[slot] = act
            slope_st[slot] = (spread + inner * bell).astype(BF16)
            br_s[...] += mm(act, wo_s[cols, :])
            for c in pair(t, slot):
                c.start()
            return carry

        lax.fori_loop(0, TILES, step, 0)
        for t in (TILES - 2, TILES - 1):
            for c in pair(t, t % 2):
                c.wait()

    pl.run_scoped(feed, pltpu.VMEM((2, ROWS, TILE), BF16), pltpu.VMEM((2, ROWS, TILE), BF16))

    for s, o_ref in ((0, oc_ref), (1, oq_ref)):
        def last(i, carry, s=s, o_ref=o_ref):
            rows = ds(s * SEQ + i * 128, 128)
            normed = n1_s[rows, :] * vec_ref[3:4, :] + vec_ref[4:5, :]
            n, inverse = norm_stats(normed + br_s[rows, :] + vec_ref[5:6, :])
            br_s[rows, :] = n
            inv2_s[rows, :] = jnp.broadcast_to(inverse, (128, 128))
            o_ref[ds(i * 128, 128), :] = (n * vec_ref[6:7, :] + vec_ref[7:8, :]).astype(BF16)
            return carry

        lax.fori_loop(0, SEQ // 128, last, 0)
    keep(br_s, n2_h)
    keep(inv2_s, inv2_h)
    for i, (src, dst) in enumerate(stores):
        pltpu.make_async_copy(src, dst, o_sem.at[i]).wait()


def call_forward(x, y, length, rank, vecs, table, wa, wi, wo):
    hbm = pl.BlockSpec(memory_space=pl.ANY)
    vmem = pl.BlockSpec(memory_space=pltpu.VMEM)
    smem = pl.BlockSpec(memory_space=pltpu.SMEM)
    shape = jax.ShapeDtypeStruct
    outs = (
        shape((SEQ, D), BF16), shape((SEQ, D), BF16),
        shape((2, PAIRS, SEQ, 128), BF16), shape((PAIRS, SEQ, 128), BF16), shape((PAIRS, SEQ, 128), BF16),
        shape((PAIRS, 2, 2, SEQ, SEQ), BF16), shape((ROWS, D), BF16),
        shape((ROWS, D), F32), shape((ROWS, 128), F32), shape((ROWS, D), BF16),
        shape((TILES, ROWS, TILE), BF16), shape((TILES, ROWS, TILE), BF16),
        shape((ROWS, D), F32), shape((ROWS, 128), F32),
    )
    return pl.pallas_call(
        forward_kernel,
        out_shape=outs,
        in_specs=[vmem, vmem, smem, vmem, vmem, vmem, hbm, hbm, hbm],
        out_specs=[vmem, vmem] + [hbm] * 12,
        scratch_shapes=[
            pltpu.VMEM((4, D, D), BF16), pltpu.VMEM((D, FF), BF16), pltpu.VMEM((FF, D), BF16),
            pltpu.VMEM((2, PAIRS, SEQ, 128), BF16), pltpu.VMEM((PAIRS, SEQ, 128), BF16), pltpu.VMEM((PAIRS, SEQ, 128), BF16),
            pltpu.VMEM((ROWS, D), BF16), pltpu.VMEM((ROWS, D), BF16), pltpu.VMEM((ROWS, D), F32), pltpu.VMEM((ROWS, D), F32),
            pltpu.VMEM((ROWS, 128), F32), pltpu.VMEM((ROWS, 128), F32),
            pltpu.SemaphoreType.DMA((6,)), pltpu.SemaphoreType.DMA((9,)), pltpu.SemaphoreType.DMA((4,)),
        ],
        compiler_params=pltpu.CompilerParams(vmem_limit_bytes=VMEM_LIMIT),
        name="forward",
    )(x, y, length, rank, vecs, table, wa, wi, wo)


def norm_grad(u, gain, n, inverse):
    ug = u * gain
    return inverse * (
        ug - jnp.mean(ug, axis=1, keepdims=True) - n * jnp.mean(ug * n, axis=1, keepdims=True)
    )


def backward_kernel(
    x_ref, y_ref, cc_ref, cq_ref, vec_ref, wa_h, wi_h, wo_h,
    q_h, k_h, v_h, p_h, ctx_h, n1_h, inv1_h, nl_h, act_h, slope_h, n2_h, inv2_h,
    gc_ref, gq_ref, ga_h, gi_h, go_h, gvec_ref, gtab_ref,
    wa_s, ctx_s, g_s, dctx_s, tr_s, st_s, l_sem, t_sem, g_sem,
):
    wload = pltpu.make_async_copy(wa_h, wa_s, l_sem.at[0])
    cload = pltpu.make_async_copy(ctx_h, ctx_s, l_sem.at[1])
    wload.start()
    cload.start()
    gvec_ref[...] = jnp.zeros_like(gvec_ref)

    def add_vec(row, value, cols=slice(None)):
        gvec_ref[row : row + 1, cols] += jnp.sum(value, axis=0, keepdims=True)

    def tail(n_s, inv_s, nl_s, db_s, act_s, slope_s, wi_s, wo_s):
        nload = pltpu.make_async_copy(n2_h, n_s, l_sem.at[2])
        iload = pltpu.make_async_copy(inv2_h, inv_s, l_sem.at[3])
        nlload = pltpu.make_async_copy(nl_h, nl_s, l_sem.at[4])
        nload.start()
        iload.start()
        nlload.start()

        def fetch(t, slot):
            return (
                pltpu.make_async_copy(act_h.at[t], act_s.at[slot], t_sem.at[slot]),
                pltpu.make_async_copy(slope_h.at[t], slope_s.at[slot], t_sem.at[2 + slot]),
                pltpu.make_async_copy(wi_h.at[:, ds(t * TILE, TILE)], wi_s.at[slot], t_sem.at[4 + slot]),
                pltpu.make_async_copy(wo_h.at[ds(t * TILE, TILE), :], wo_s.at[slot], t_sem.at[6 + slot]),
            )

        for c in fetch(0, 0):
            c.start()
        nload.wait()
        iload.wait()
        for s, cot in ((0, cc_ref), (1, cq_ref)):
            def second(i, carry, s=s, cot=cot):
                rows = ds(s * SEQ + i * 128, 128)
                u = cot[ds(i * 128, 128), :].astype(F32)
                n = n_s[rows, :]
                g = norm_grad(u, vec_ref[6:7, :], n, inv_s[rows, 0:1])
                add_vec(6, u * n)
                add_vec(7, u)
                g_s[rows, :] = g
                low = g.astype(BF16)
                db_s[rows, :] = low
                add_vec(5, low.astype(F32))
                return carry

            lax.fori_loop(0, SEQ // 128, second, 0)
        n1load = pltpu.make_async_copy(n1_h, n_s, l_sem.at[2])
        i1load = pltpu.make_async_copy(inv1_h, inv_s, l_sem.at[3])
        n1load.start()
        i1load.start()
        nlload.wait()
        tr_s[...] = nl_s[...].T

        def out_copies(t, slot):
            return (
                pltpu.make_async_copy(st_s.at[slot], go_h.at[ds(t * TILE, TILE), :], g_sem.at[slot]),
                pltpu.make_async_copy(st_s.at[2 + slot, :, :], gi_h.at[t], g_sem.at[2 + slot]),
            )

        def step(t, carry):
            slot = (t % 2)
            for c in fetch(t, slot):
                c.wait()

            @pl.when(t + 1 < TILES)
            def _():
                for c in fetch(t + 1, 1 - slot):
                    c.start()

            @pl.when(t >= 2)
            def _():
                for c in out_copies(t - 2, slot):
                    c.wait()

            db = db_s[...]
            di = (mm_nt(db, wo_s[slot]) * slope_s[slot].astype(F32)).astype(BF16)
            row, cols = (t // 3), ds((t % 3) * TILE, TILE)
            mine = lax.broadcasted_iota(jnp.int32, (8, TILE), 0) == row
            gvec_ref[8:16, cols] += jnp.where(mine, jnp.sum(di.astype(F32), axis=0, keepdims=True), 0.0)
            st_s[slot] = mm_tn(act_s[slot], db).astype(BF16)
            gin = mm(tr_s[...], di).astype(BF16)
            for j in range(3):
                st_s[2 + slot, :, j * 256 : (j + 1) * 256] = gin[j * 256 : (j + 1) * 256, :]
            g_s[...] += mm_nt(di, wi_s[slot])
            for c in out_copies(t, slot):
                c.start()
            return carry

        lax.fori_loop(0, TILES, step, 0)
        for t in (TILES - 2, TILES - 1):
            for c in out_copies(t, t % 2):
                c.wait()

        n1load.wait()
        i1load.wait()

        def first(i, carry):
            rows = ds(i * 128, 128)
            u = g_s[rows, :]
            n = n_s[rows, :]
            g = norm_grad(u, vec_ref[3:4, :], n, inv_s[rows, 0:1])
            add_vec(3, u * n)
            add_vec(4, u)
            g_s[rows, :] = g
            low = g.astype(BF16)
            db_s[rows, :] = low
            add_vec(2, low.astype(F32))
            return carry

        lax.fori_loop(0, ROWS // 128, first, 0)
        wload.wait()
        cload.wait()
        tr_s[...] = ctx_s[...].T

        def outer(j, carry):
            cols = ds(j * 256, 256)
            st_s[0, :, cols] = mm(tr_s[ds(j * 256, 256), :], db_s[...]).astype(BF16)[:, :256]
            return carry

        del outer
        for j in range(3):
            st_s[j] = mm(tr_s[j * 256 : (j + 1) * 256, :], db_s[...]).astype(BF16)
        for j in range(4):
            dctx_s[j * 256 : (j + 1) * 256, :] = mm_nt(db_s[j * 256 : (j + 1) * 256, :], wa_s[3]).astype(BF16)
        cs = [pltpu.make_async_copy(st_s.at[j], ga_h.at[3, j * 256 : (j + 1) * 256, :], g_sem.at[j]) for j in range(3)]
        for c in cs:
            c.start()
        for c in cs:
            c.wait()

    pl.run_scoped(
        tail,
        pltpu.VMEM((ROWS, D), F32),
        pltpu.VMEM((ROWS, 128), F32),
        pltpu.VMEM((ROWS, D), BF16),
        pltpu.VMEM((ROWS, D), BF16),
        pltpu.VMEM((2, ROWS, TILE), BF16),
        pltpu.VMEM((2, ROWS, TILE), BF16),
        pltpu.VMEM((2, D, TILE), BF16),
        pltpu.VMEM((2, TILE, D), BF16),
    )

    def attention(q_s, k_s, v_s, p_s, qt_s, dt_s, dq_s, dkt_s, dvt_s, far_s, bt_s):
        cs = [pltpu.make_async_copy(a, b, l_sem.at[2 + i]) for i, (a, b) in enumerate(((q_h, q_s), (k_h, k_s), (v_h, v_s)))]
        for c in cs:
            c.start()

        def fetch(hp, slot):
            return pltpu.make_async_copy(p_h.at[hp], p_s.at[slot], t_sem.at[slot])

        fetch(0, 0).start()
        for c in cs:
            c.wait()
        dt_s[...] = dctx_s[...].T
        for s in range(2):
            for hp in range(PAIRS):
                qt_s[s, hp] = q_s[s, hp].T

        def step(hp, carry):
            slot = (hp % 2)
            fetch(hp, slot).wait()

            @pl.when(hp + 1 < PAIRS)
            def _():
                fetch(hp + 1, 1 - slot).start()

            lane = lax.broadcasted_iota(jnp.int32, (SEQ, 128), 1)
            k, v = k_s[hp], v_s[hp]
            zero = jnp.zeros((SEQ, 128), BF16)
            dq = [None, None]
            for e in range(2):
                own = (lane < 64) if e == 0 else (lane >= 64)
                both = None
                dkt = dvt = None
                for s in range(2):
                    rows = slice(s * SEQ, (s + 1) * SEQ)
                    do = jnp.where(own, dctx_s[rows, ds(hp * 128, 128)], zero)
                    weight = jnp.sum(do.astype(F32) * ctx_s[rows, ds(hp * 128, 128)].astype(F32), axis=1, keepdims=True)
                    p = p_s[slot, e, s]
                    g = p.astype(F32) * (mm_nt(do, v) - weight)
                    low = g.astype(BF16)
                    both = g if both is None else both + g
                    part = mm(low, jnp.where(own, k, zero))
                    dq[s] = part if dq[s] is None else dq[s] + part
                    half = ds(hp * 128 + e * 64, 64)
                    a = mm(dt_s[half, rows], p)
                    b = mm(qt_s[s, hp, e * 64 : (e + 1) * 64, :], low)
                    dvt = a if dvt is None else dvt + a
                    dkt = b if dkt is None else dkt + b
                dvt_s[ds(hp * 128 + e * 64, 64), :] = dvt.astype(BF16)
                dkt_s[ds(hp * 128 + e * 64, 64), :] = (dkt * SCALE).astype(BF16)
                sums = [None] * 7
                for i in range(4):
                    for j in range(4):
                        blk = both[i * 128 : (i + 1) * 128, j * 128 : (j + 1) * 128]
                        at = min(max(j - i, -2), 2) + 2
                        sums[at] = blk if sums[at] is None else sums[at] + blk
                strip = jnp.concatenate([jnp.zeros((128, 128), F32), sums[1], sums[2], sums[3]], axis=1)
                flat = strip[0:8]
                for g in range(1, 16):
                    flat = flat + pltpu.roll(strip[8 * g : 8 * g + 8], 512 - 8 * g, 1)
                row = lax.broadcasted_iota(jnp.int32, (8, 512), 0)
                for bit in (1, 2, 4):
                    flat = jnp.where((row & bit) != 0, pltpu.roll(flat, 512 - bit, 1), flat)
                h = 2 * hp + e
                for ref, cols, value in (
                    (bt_s, slice(0, 512), flat),
                    (far_s, slice(0, 128), sums[0]),
                    (far_s, slice(128, 256), sums[4]),
                ):
                    line = jnp.sum(value, axis=0, keepdims=True)
                    mine = lax.broadcasted_iota(jnp.int32, (16, line.shape[1]), 0) == h
                    ref[:, cols] = jnp.where(mine, line, ref[:, cols])
            for s in range(2):
                dq_s[s * SEQ : (s + 1) * SEQ, ds(hp * 128, 128)] = (dq[s] * SCALE).astype(BF16)
            return carry

        bt_s[...] = jnp.zeros_like(bt_s)
        far_s[...] = jnp.zeros_like(far_s)
        lax.fori_loop(0, PAIRS, step, 0)

        offset = lax.broadcasted_iota(jnp.int32, (512, 128), 0) - 256
        bucket = lax.broadcasted_iota(jnp.int32, (512, 128), 1)
        near = jnp.where(bucket_of(offset) == bucket, 1.0, 0.0)
        lane = lax.broadcasted_iota(jnp.int32, (16, 128), 1)
        gtab_ref[...] = (
            lax.dot_general(bt_s[...], near, (((1,), (0,)), ((), ())), precision=lax.Precision.HIGHEST, preferred_element_type=F32)
            + jnp.where(lane == 15, jnp.sum(far_s[:, 0:128], axis=1, keepdims=True), 0.0)
            + jnp.where(lane == 31, jnp.sum(far_s[:, 128:256], axis=1, keepdims=True), 0.0)
        )

        dk = dkt_s[...].T
        dv = dvt_s[...].T
        add_vec(0, dq_s[...].astype(F32))
        add_vec(1, dv.astype(F32))
        tr_s[:, 0:SEQ] = x_ref[...].T
        tr_s[:, SEQ:] = y_ref[...].T
        slot = 0
        cs = []
        for w, grad in ((0, dq_s[...]), (1, dk), (2, dv)):
            left = tr_s[...] if w == 0 else tr_s[:, 0:SEQ]
            for j in range(3):
                if len(cs) >= 4:
                    cs[len(cs) - 4].wait()
                st_s[slot % 4] = mm(left[j * 256 : (j + 1) * 256, :], grad).astype(BF16)
                c = pltpu.make_async_copy(st_s.at[slot % 4], ga_h.at[w, j * 256 : (j + 1) * 256, :], g_sem.at[slot % 4])
                c.start()
                cs.append(c)
                slot += 1
        gc_ref[...] = g_s[0:SEQ, :] + mm_nt(dq_s[0:SEQ, :], wa_s[0]) + mm_nt(dk, wa_s[1]) + mm_nt(dv, wa_s[2])
        gq_ref[...] = g_s[SEQ:, :] + mm_nt(dq_s[SEQ:, :], wa_s[0])
        for c in cs[-4:]:
            c.wait()

    pl.run_scoped(
        attention,
        pltpu.VMEM((2, PAIRS, SEQ, 128), BF16),
        pltpu.VMEM((PAIRS, SEQ, 128), BF16),
        pltpu.VMEM((PAIRS, SEQ, 128), BF16),
        pltpu.VMEM((2, 2, 2, SEQ, SEQ), BF16),
        pltpu.VMEM((2, PAIRS, 128, SEQ), BF16),
        pltpu.VMEM((D, ROWS), BF16),
        pltpu.VMEM((ROWS, D), BF16),
        pltpu.VMEM((D, SEQ), BF16),
        pltpu.VMEM((D, SEQ), BF16),
        pltpu.VMEM((16, 256), F32),
        pltpu.VMEM((16, 512), F32),
    )


def call_backward(x, y, cc, cq, vecs, wa, wi, wo, saved):
    hbm = pl.BlockSpec(memory_space=pl.ANY)
    vmem = pl.BlockSpec(memory_space=pltpu.VMEM)
    shape = jax.ShapeDtypeStruct
    outs = (
        shape((SEQ, D), F32), shape((SEQ, D), F32),
        shape((4, D, D), BF16), shape((TILES, TILE, D), BF16), shape((FF, D), BF16),
        shape((16, D), F32), shape((16, 128), F32),
    )
    return pl.pallas_call(
        backward_kernel,
        out_shape=outs,
        in_specs=[vmem] * 5 + [hbm] * 15,
        out_specs=[vmem, vmem, hbm, hbm, hbm, vmem, vmem],
        scratch_shapes=[
            pltpu.VMEM((4, D, D), BF16), pltpu.VMEM((ROWS, D), BF16), pltpu.VMEM((ROWS, D), F32), pltpu.VMEM((ROWS, D), BF16),
            pltpu.VMEM((D, ROWS), BF16), pltpu.VMEM((4, TILE, D), BF16),
            pltpu.SemaphoreType.DMA((5,)), pltpu.SemaphoreType.DMA((8,)), pltpu.SemaphoreType.DMA((4,)),
        ],
        compiler_params=pltpu.CompilerParams(vmem_limit_bytes=VMEM_LIMIT),
        name="backward",
    )(x, y, cc, cq, vecs, wa, wi, wo, *saved)


def shards(
    content_stream, query_stream, lengths, ranking, query_weight, query_bias, key_weight, value_weight, value_bias,
    output_weight, output_bias, norm_gain, norm_shift, inner_weight, inner_bias, outer_weight, outer_bias, final_gain,
    final_shift, bucket_bias, content_cotangent, query_cotangent,
):
    def gather(a, axis=0):
        return lax.all_gather(a, "fsdp", axis=axis, tiled=True)

    wa = gather(jnp.stack([query_weight, key_weight, value_weight, output_weight]), 1)
    wi = gather(inner_weight)
    wo = gather(outer_weight)
    small = (query_bias, value_bias, output_bias, norm_gain, norm_shift, outer_bias, final_gain, final_shift)
    width = query_bias.shape[0]
    packed = jnp.concatenate([*small, inner_bias, bucket_bias])[None, :]
    packed = gather(packed)
    cuts = [packed[:, i * width : (i + 1) * width].reshape(1, D) for i in range(8)]
    at = 8 * width
    cuts.append(packed[:, at : at + inner_bias.shape[0]].reshape(4, D))
    at += inner_bias.shape[0]
    vecs = jnp.concatenate(cuts + [jnp.zeros((4, D), BF16)]).astype(F32)
    table = jnp.pad(packed[:, at:].reshape(HEADS, BUCKETS), ((0, 4), (0, 128 - BUCKETS)))

    out_c, out_q, *saved = call_forward(
        content_stream, query_stream, lengths, ranking, vecs, table, wa, wi, wo
    )
    gc, gq, ga, gi, go, gvec, gtab = call_backward(
        content_stream, query_stream, content_cotangent, query_cotangent, vecs, wa, wi, wo, saved
    )
    gi = gi.reshape(TILES, TILE, 3, TILE).transpose(2, 1, 0, 3).reshape(D, FF)

    def reduce(a, axis=0):
        a = lax.psum_scatter(a, "fsdp", scatter_dimension=axis, tiled=True)
        return lax.psum(a.astype(BF16), "rep").astype(F32)

    ga = reduce(ga, 1)
    gi = reduce(gi)
    go = reduce(go)
    count = D // width
    flat = jnp.concatenate(
        [gvec[i].reshape(count, width) for i in range(8)]
        + [gvec[8:12].reshape(count, 4 * width), gtab[:HEADS, :BUCKETS].reshape(count, -1)],
        axis=1,
    )
    flat = lax.psum_scatter(flat, "fsdp", scatter_dimension=0, tiled=True)[0]
    flat = lax.psum(flat.astype(BF16), "rep").astype(F32)
    v = [flat[i * width : (i + 1) * width] for i in range(8)]
    return (
        out_c, out_q, gc, gq, ga[0], v[0], ga[1], ga[2], v[1], ga[3], v[2], v[3], v[4], gi,
        flat[8 * width : 12 * width], go, v[5], v[6], v[7], flat[12 * width :],
    )


def solution(mesh):
    both, fsdp = ("rep", "fsdp"), "fsdp"
    row, vec = P(fsdp, None), P(fsdp)
    tokens = P(both, None)
    in_specs = (
        tokens, tokens, P(both), tokens, row, vec, row, row, vec, row, vec, vec, vec, row, vec, row, vec, vec, vec, vec,
        tokens, tokens,
    )
    out_specs = (
        tokens, tokens, tokens, tokens, row, vec, row, row, vec, row, vec, vec, vec, row, vec, row, vec, vec, vec, vec,
    )
    return jax.shard_map(shards, mesh=mesh, in_specs=in_specs, out_specs=out_specs, check_vma=False)
```

time: 709 us -> 535 us (0.75)
  matrix products: 228 us -> 0 us
  Pallas kernels: 0 us -> 120 us
  waiting for transfers between devices: 211 us -> 285 us
  local copies, waits for them, and re-layouts: 99.3 us -> 37.8 us
  other arithmetic: 65.5 us -> 7.12 us
  blocking collectives: 80.1 us -> 67.7 us
    dot_general x44 -> x0, matrix products: 228 us -> none  [the longest x11 64.7 us: matmul(): return jnp.dot(left, right, preferred_element_type=jnp.float32)]
    pallas_call x0 -> x2, Pallas kernels: none -> 120 us  [the longest x1 61.2 us: call_backward(): pl.pallas_call(backward_kernel, out_shape=outs, in_specs=[vmem] * 5 + [hb...]
    all_gather x6 -> x3, waiting for transfers between devices: 0.11 us -> 115 us  [gather(): return lax.all_gather(a, 'fsdp', axis=axis, tiled=True)]
    reduce_scatter x3, waiting for transfers between devices: 197 us -> 141 us  [reduce(): a = lax.psum_scatter(a, 'fsdp', scatter_dimension=axis, tiled=True)]
    unnamed x210 -> x10, local copies, waits for them, and re-layouts: 50.6 us -> 9.85 us
    add x12 -> x0, other arithmetic: 28.5 us -> none  [the longest x1 27.2 us: attend_backward(): bias_total = bias_total + grad_scores.astype(jnp.float32)]
    psum x1, waiting for transfers between devices: 0.01 us -> 27.2 us  [reduce(): return lax.psum(a.astype(BF16), 'rep').astype(F32)]
    reshape x4 -> x12, local copies, waits for them, and re-layouts: 23.8 us -> 0.86 us  [the longest x8 0.69 us: shards(): packed[:, i * width:(i + 1) * width].reshape(1, D)]
  transfers between devices with their start and end apart: 13 -> 7, of which waited for: 3 -> 7; matrix products, arithmetic and copies ran while one was open for 47% -> 7% of each run, Pallas kernels for 0% -> 0%
where the time goes in v1:
time: 535 us; the launch traced here: 534 us
  waiting for transfers between devices  285 us (53%)
  Pallas kernels  120 us (22%)
  blocking collectives  67.7 us (13%)
  local copies, waits for them, and re-layouts  37.8 us (7%)
  between operations  15.5 us (3%)
  other arithmetic  7.12 us (1%)
    reduce_scatter x3, waiting for transfers between devices, reduce(): a = lax.psum_scatter(a, 'fsdp', scatter_dimension=axis, tiled=True)  141 us
    all_gather x3, waiting for transfers between devices, gather(): return lax.all_gather(a, 'fsdp', axis=axis, tiled=True)  115 us
    pallas_call x1, Pallas kernels, call_backward(): pl.pallas_call(backward_kernel, out_shape=outs, in_specs=[vmem] * 5 + [hb...  61.2 us
    pallas_call x1, Pallas kernels, call_forward(): pl.pallas_call(forward_kernel, out_shape=outs, in_specs=[vmem, vmem, smem...  59.2 us
    unnamed x2, blocking collectives  57.9 us
    psum x1, waiting for transfers between devices, reduce(): return lax.psum(a.astype(BF16), 'rep').astype(F32)  27.2 us
  transfers between devices with their start and end apart: 7, of which 7 were waited for; matrix products, arithmetic and copies ran while one was open for 7% of the time, Pallas kernels for 0%

profile of v1, /device:TPU:0, one launch (start us, length us, event | category | flops | bytes accessed | tf_op | source)
XLA Modules:
  0.0 533.9 jit_solution(6840615098797034020)
XLA Ops:
  7.2 0.7 all-gather.7.cloned.1.call-update
  8.0 0.7 all-gather.9.cloned.1.call-update
  8.7 2.0 pad_maximum_fusion
  10.8 1.3 fusion.3
  12.8 6.8 %concatenate.9 = bf16[1200]{0:T(1024)(128)(2,1)S(1)} concatenate(bf16[96]{0:T(256)(128)(2,1)} %param.27, bf16[96]{0:T(256)(128)(2,1)} %param.30, bf16[96]{0:T(256)(128)(2,1)} %param.32, bf16[96]{0:T(256)(128)(2,1)} %param.33, bf16[96]{0:T(256)(128)(2,1)} %param.34, bf16[96]{0:T(256)(128)(2,1)} %param.38, bf16[96]{0:T(256)(128)(2,1)} %param.39, bf16[96]{0:T(256)(128)(2,1)} %param.40, ...), dimensions={0} | concatenate | bytes 4800 | tf_op jit(solution)/shard_map/concatenate | solution.py:624
  19.6 0.3 dynamic-update-slice
  19.9 31.5 %all-reduce.1 = bf16[9600]{0:T(1024)(128)(2,1)S(1)} all-reduce(bf16[9600]{0:T(1024)(128)(2,1)S(1)} %dynamic-update-slice), channel_id=2, replica_groups=mesh['rep'=4,'fsdp'=8] {'fsdp'}, use_global_device_ids=true, to_apply=%add.1 | all-reduce | flops 9600 | bytes 38400
  51.4 0.1 reshape.97
  52.2 0.1 reshape.92
  52.3 0.6 pad.4.tab_ref
  52.9 0.1 fusion.1
  53.0 0.1 reshape.90
  53.0 0.1 reshape.89
  53.1 0.1 reshape.88
  53.2 0.1 reshape.87
  53.3 0.1 reshape.86
  53.4 0.1 reshape.85
  53.5 0.1 reshape.84
  53.6 0.1 reshape.83
  53.7 0.1 concatenate.10
  53.7 0.6 convert_element_type.23.vec_ref
  54.4 10.2 %all-gather.7.cloned.1.call-done.wi_h = bf16[768,3072]{1,0:T(8,128)(2,1)} async-done(((bf16[96,3072]{1,0:T(8,128)(2,1)}), bf16[768,3072]{1,0:T(8,128)(2,1)}) %all-gather.7.cloned.1.call-update) | async-done | bytes 4718608 | tf_op jit(solution)/shard_map/all_gather | solution.py:617
  64.5 52.2 %all-gather.9.cloned.1.call-done.wo_h = bf16[3072,768]{1,0:T(8,128)(2,1)} async-done(((bf16[384,768]{1,0:T(8,128)(2,1)}), bf16[3072,768]{1,0:T(8,128)(2,1)}) %all-gather.9.cloned.1.call-update) | async-done | bytes 4718608 | tf_op jit(solution)/shard_map/all_gather | solution.py:617
  116.8 52.7 %all-gather.5.cloned.1.call-done.wa_h = bf16[4,768,768]{2,1,0:T(8,128)(2,1)} async-done(((bf16[4,96,768]{2,1,0:T(8,128)(2,1)}), bf16[4,768,768]{2,1,0:T(8,128)(2,1)}) %all-gather.5.cloned.1.call-update) | async-done | bytes 4718608 | tf_op jit(solution)/shard_map/all_gather | solution.py:617
  169.5 59.2 %forward.1 = (bf16[512,768]{1,0:T(8,128)(2,1)}, bf16[512,768]{1,0:T(8,128)(2,1)}, bf16[2,6,512,128]{3,2,1,0:T(8,128)(2,1)}, bf16[6,512,128]{2,1,0:T(8,128)(2,1)}...) custom-call(bf16[512,768]{1,0:T(8,128)(2,1)} %x_ref.3, ...), custom_call_target="tpu_custom_call" | custom-call | tf_op jit(solution)/shard_map/forward/pallas_call | solution.py:289
  228.7 61.2 %backward.1 = (f32[512,768]{1,0:T(8,128)}, f32[512,768]{1,0:T(8,128)}, bf16[4,768,768]{2,1,0:T(8,128)(2,1)}, bf16[12,256,768]{2,1,0:T(8,128)(2,1)}, bf16[3072,76...) custom-call(bf16[512,768]{1,0:T(8,128)(2,1)} %x_ref.3, bf16[512,768]{1,0:T(8,128)(2,1)} %y_ref.3, ...), custom_call_target="tpu_custom_call" | custom-call | tf_op jit(solution)/shard_map/backward/pallas_call | solution.py:596
  289.9 0.5 reduce-scatter.8.cloned.1.call-update
  290.5 6.9 %copy.45 = bf16[12,256,768]{1,2,0:T(8,128)(2,1)} copy(bf16[12,256,768]{2,1,0:T(8,128)(2,1)} %get-tuple-element.60) | data formatting | bytes 9437184 | tf_op jit(solution)/shard_map/backward/pallas_call | solution.py:596
  297.5 8.3 %copy.46 = bf16[3,256,12,256]{3,2,1,0:T(8,128)(2,1)} copy(bf16[3,256,12,256]{1,3,0,2:T(8,128)(2,1)} %bitcast.23) | data formatting | bytes 9437184 | tf_op jit(solution)/shard_map/transpose | solution.py:639
  305.8 8.2 %copy.47 = bf16[96,8,12,256]{3,1,2,0:T(8,128)(2,1)} copy(bf16[96,8,12,256]{3,2,1,0:T(8,128)(2,1)} %bitcast.21) | data formatting | bytes 9437184
  314.1 29.8 %reduce-scatter.4.cloned.1.call-done = bf16[4,96,768]{2,1,0:T(8,128)(2,1)} async-done(((bf16[4,768,768]{2,1,0:T(8,128)(2,1)}), bf16[4,96,768]{2,1,0:T(8,128)(2,1)}) %reduce-scatter.4.cloned.1.call-update) | async-done | bytes 589840 | tf_op jit(solution)/shard_map/reduce_scatter | solution.py:642
  343.9 55.5 %reduce-scatter.8.cloned.1.call-done = bf16[384,768]{1,0:T(8,128)(2,1)} async-done(((bf16[3072,768]{1,0:T(8,128)(2,1)}), bf16[384,768]{1,0:T(8,128)(2,1)}) %reduce-scatter.8.cloned.1.call-update) | async-done | bytes 589840 | tf_op jit(solution)/shard_map/reduce_scatter | solution.py:642
  399.3 55.5 %reduce-scatter.6.cloned.1.call-done = bf16[96,3072]{1,0:T(8,128)(2,1)} async-done(((bf16[768,3072]{1,0:T(8,128)(2,1)}), bf16[96,3072]{1,0:T(8,128)(2,1)}) %reduce-scatter.6.cloned.1.call-update) | async-done | bytes 589840 | tf_op jit(solution)/shard_map/reduce_scatter | solution.py:642
  454.9 0.1 reshape.94
  455.0 0.1 reshape_squeeze.31
  455.1 0.1 reshape_squeeze.30
  455.6 0.1 concatenate.11
  455.7 26.4 %all-reduce.2 = bf16[8,1200]{1,0:T(8,128)(2,1)S(1)} all-reduce(f32[8,1200]{1,0:T(8,128)S(1)} %concatenate.11), channel_id=4, replica_groups=mesh['rep'=4,'fsdp'=8] {'fsdp'}, use_global_device_ids=true, to_apply=%region_2.3.clone | all-reduce | flops 9600 | bytes 57600
  482.1 0.7 fusion
  482.8 9.8 %psum.29 = bf16[1200]{0:T(1024)(128)(2,1)S(1)} all-reduce(bf16[1200]{0:T(1024)(128)(2,1)S(1)} %fusion), channel_id=1, replica_groups=mesh['rep'=4,'fsdp'=8] {'rep'}, use_global_device_ids=true, to_apply=%region_3.4 | all-reduce | flops 1200 | bytes 4800 | tf_op jit(solution)/shard_map/psum | solution.py:655
  492.6 0.5 slice.159
  493.1 0.6 slice.155
  493.7 0.6 fusion.2
  494.3 27.2 %all-reduce.6.cloned.1.call-done = (bf16[4,96,768]{2,1,0:T(8,128)(2,1)}, bf16[96,3072]{1,0:T(8,128)(2,1)}, bf16[384,768]{1,0:T(8,128)(2,1)}) async-done(((bf16[4,96,768]{2,1,0:T(8,128)(2,1)}, bf16[96,3072]{1,0:T(8,128)(2,1)}, bf16[384,768]{1,0:T(8,128)(2,1)}), (bf16[4,96,768]{2,1,0:T(8,128)(2,1)}, bf16[96,3072]{1,0:T(8,128)(2,1)}, bf16[384,768]{1,0:T(8,128)(2,1)})) %all-reduce.6.cloned.1.call-update) | async-done | bytes 1769488 | tf_op jit(solution)/shard_map/psum | solution.py:643
  521.5 1.2 convert_element_type.24
  522.7 1.0 slice_bitcast_fusion
  523.7 2.2 convert_element_type.28
  525.9 1.1 convert_element_type.29
  (31 shorter events, 0.9 us)
Async XLA Ops:
  7.2 57.3 %all-gather.7.cloned.1.call-start = ((), (), s32[]{:S(2)}) async-start(), calls=%async_computation.4 | async-start | bytes 5308416 | tf_op jit(solution)/shard_map/all_gather | solution.py:617
  7.9 108.9 %all-gather.9.cloned.1.call-start = ((), (), s32[]{:S(2)}) async-start(), calls=%async_computation.5 | async-start | bytes 5308416 | tf_op jit(solution)/shard_map/all_gather | solution.py:617
  8.7 160.8 %all-gather.5.cloned.1.call-start = ((), (), s32[]{:S(2)}) async-start(), calls=%async_computation.3 | async-start | bytes 5308416 | tf_op jit(solution)/shard_map/all_gather | solution.py:617
  10.8 333.1 %reduce-scatter.4.cloned.1.call-start = ((), (), s32[]{:S(2)}) async-start(), calls=%async_computation.6 | async-start | bytes 5308416 | tf_op jit(solution)/shard_map/reduce_scatter | solution.py:642
  289.9 109.5 %reduce-scatter.8.cloned.1.call-start = ((), (), s32[]{:S(2)}) async-start(), calls=%async_computation.8 | async-start | bytes 5308416 | tf_op jit(solution)/shard_map/reduce_scatter | solution.py:642
  290.5 164.4 %reduce-scatter.6.cloned.1.call-start = ((), (), s32[]{:S(2)}) async-start(), calls=%async_computation.7 | async-start | bytes 5308416 | tf_op jit(solution)/shard_map/reduce_scatter | solution.py:642
  314.0 140.9 %copy-start.2 = (f32[16,128]{1,0:T(8,128)S(1)}, f32[16,128]{1,0:T(8,128)}, u32[]{:S(2)}) copy-start(f32[16,128]{1,0:T(8,128)} %get-tuple-element.59) | copy-start | bytes 24580
  314.0 141.0 %copy-start.1 = (f32[16,768]{1,0:T(8,128)S(1)}, f32[16,768]{1,0:T(8,128)}, u32[]{:S(2)}) copy-start(f32[16,768]{1,0:T(8,128)} %get-tuple-element.58) | copy-start | bytes 147460
  314.0 207.5 %all-reduce.6.cloned.1.call-start = ((), (), s32[]{:S(2)}) async-start(), calls=%async_computation.9 | async-start | bytes 3538944 | tf_op jit(solution)/shard_map/psum | solution.py:643
  521.5 4.4 copy-start
Sparse Core Ops, SparseCore 0:
  9.7 54.8 all-gather.6
  66.2 50.5 all-gather.8
  119.0 50.4 all-gather.4
  290.0 53.8 reduce-scatter.3
  346.0 53.2 reduce-scatter.7
  401.5 53.3 reduce-scatter.5
  458.3 63.1 all-reduce.5

commit v2 on v1

--- a/solution.py
+++ b/solution.py
@@ -72,6 +72,149 @@
     return pl.ds(pl.multiple_of(start, size), size)
 
 
+def places():
+    f = lax.axis_index("fsdp")
+    return lax.axis_index("rep"), f // 2, f % 2
+
+
+def hop(i, k):
+    if k == 0:
+        return i
+    if k == 1:
+        return i + 1 - 2 * (i % 2)
+    return (i + 2) % 4 if k == 2 else 3 - i
+
+
+def remote(src, dst, send, recv, device):
+    return pltpu.make_async_remote_copy(
+        src_ref=src, dst_ref=dst, send_sem=send, recv_sem=recv, device_id=device, device_id_type=pl.DeviceIdType.MESH
+    )
+
+
+def greet(devices):
+    barrier = pltpu.get_barrier_semaphore()
+    for device in devices:
+        pl.semaphore_signal(barrier, inc=1, device_id=device, device_id_type=pl.DeviceIdType.MESH)
+    pl.semaphore_wait(barrier, len(devices))
+
+
+class Gather:
+    def __init__(self, refs, sems):
+        self.wa, self.wi, self.wo, self.small = refs
+        self.l_sem, self.zs, self.zr, self.xs, self.xr, self.cs, self.cr, self.vs, self.vr = sems
+        self.r, self.z, self.c = places()
+
+    def block(self, t, r, z, c):
+        if t == 2:
+            return self.wo.at[z, pl.ds(pl.multiple_of(c * 384 + r * 96, 96), 96), :]
+        return (self.wa, self.wi)[t].at[r, z, ds(c * 96, 96), :]
+
+    def slab(self, t, r, c):
+        if t == 2:
+            return self.wo.at[:, pl.ds(pl.multiple_of(c * 384 + r * 96, 96), 96), :]
+        return (self.wa, self.wi)[t].at[r, :, ds(c * 96, 96), :]
+
+    def own(self, shards):
+        *square, inner, outer = shards
+        z, c = self.z, self.c
+        copies = [
+            [pltpu.make_async_copy(square[m], self.block(0, m, z, c), self.l_sem.at[0, m]) for m in range(4)],
+            [
+                pltpu.make_async_copy(inner.at[:, m * D : (m + 1) * D], self.block(1, m, z, c), self.l_sem.at[1, m])
+                for m in range(4)
+            ],
+            [pltpu.make_async_copy(outer, self.wo.at[z, ds(c * 384, 384), :], self.l_sem.at[2, 0])],
+        ]
+        return copies
+
+    def small_copy(self, k):
+        f = 2 * self.z + self.c
+        return remote(
+            self.small.at[f], self.small.at[f], self.vs.at[k - 1], self.vr.at[k - 1], (self.r, (f + k) % 8)
+        )
+
+    def small_come(self, k):
+        f = (2 * self.z + self.c + 8 - k) % 8
+        return remote(self.small.at[f], self.small.at[f], self.vs.at[k - 1], self.vr.at[k - 1], (self.r, f))
+
+    def z_copy(self, t, k, come=False):
+        far = hop(self.z, k)
+        ref = self.block(t, self.r, far if come else self.z, self.c)
+        return remote(ref, ref, self.zs.at[t, k - 1], self.zr.at[t, k - 1], (self.r, 2 * far + self.c))
+
+    def x_copy(self, t, k, m, come=False):
+        far = hop(self.r, m)
+        ref = self.block(t, far if come else self.r, hop(self.z, k), self.c)
+        at = 3 * (k - 1) + m - 1
+        return remote(ref, ref, self.xs.at[t, at], self.xr.at[t, at], (far, 2 * self.z + self.c))
+
+    def c_copy(self, t, m, come=False):
+        ref = self.slab(t, hop(self.r, m), 1 - self.c if come else self.c)
+        return remote(ref, ref, self.cs.at[t, m], self.cr.at[t, m], (self.r, 2 * self.z + 1 - self.c))
+
+    def start_z(self, t):
+        for k in (1, 2, 3):
+            self.z_copy(t, k).start()
+
+    def pass_on(self, t):
+        for k in (1, 2, 3):
+            self.z_copy(t, k, True).wait_recv()
+            for m in (1, 2, 3):
+                self.x_copy(t, k, m).start()
+
+    def share(self, t):
+        for m in range(4):
+            if m:
+                for k in (1, 2, 3):
+                    self.x_copy(t, k, m, True).wait_recv()
+            self.c_copy(t, m).start()
+
+    def finish(self, t):
+        for m in range(4):
+            self.c_copy(t, m, True).wait_recv()
+
+    def drain(self):
+        for k in range(1, 8):
+            self.small_copy(k).wait_send()
+        for t in range(3):
+            for k in (1, 2, 3):
+                self.z_copy(t, k).wait_send()
+                for m in (1, 2, 3):
+                    self.x_copy(t, k, m).wait_send()
+            for m in range(4):
+                self.c_copy(t, m).wait_send()
+
+
+def unpack_small(small_s, vec_s):
+    blocks = [small_s[f] for f in range(8)]
+    at = lax.broadcasted_iota(jnp.int32, (1024, D), 0)
+    want = lax.broadcasted_iota(jnp.int32, (1024, D), 1)
+    spread = jnp.where((at % 128 < 96) & (want == (at // 128) * 96 + at % 128), 1.0, 0.0).astype(BF16)
+    vec_s[...] = mm(jnp.concatenate(blocks, axis=1), spread)
+    wide = [b.astype(F32) for b in blocks]
+    for m in range(4):
+        for j in range(6):
+            vec_s[8 + m : 9 + m, j * 128 : (j + 1) * 128] = wide[2 * m + j // 3][8 + j % 3 : 9 + j % 3]
+    return [w[11:12] for w in wide]
+
+
+def lines_of(rows):
+    bucket = bucket_of(lax.broadcasted_iota(jnp.int32, (128, 1024), 1) - 512)
+    entry = lax.broadcasted_iota(jnp.int32, (128, 1024), 0)
+
+    def pick(first, shift):
+        inside = (entry >= first) & (entry < 48)
+        return jnp.where(inside & (bucket == entry + shift), 1.0, 0.0).astype(BF16)
+
+    table = jnp.concatenate(rows, axis=0).astype(BF16)
+    a0, a1, b1, b2 = (mm(table, pick(*p)) for p in ((0, 0), (32, -32), (0, 16), (16, -16)))
+    lines = []
+    for m in range(4):
+        i, j = 2 * m, 2 * m + 1
+        lines += [a0[i : i + 1], a1[i : i + 1] + b1[j : j + 1], b2[j : j + 1]]
+    return [line * LOG2E for line in lines]
+
+
 def build_masks(len_ref, rank_ref, mask_s):
     n = len_ref[0]
     rank = rank_ref[...]
@@ -86,14 +229,23 @@
             mask_s[s, :, j * 128 : (j + 1) * 128] = jnp.where(seen, 0.0, NEG)
 
 
-def build_strip(tab_ref, strip_s):
+def lines_of_table(tab_ref):
     offset = lax.broadcasted_iota(jnp.int32, (128, 1024), 1) - 512
     bucket = lax.broadcasted_iota(jnp.int32, (128, 1024), 0)
     onehot = jnp.where(bucket_of(offset) == bucket, 1.0, 0.0).astype(BF16)
     line = mm(tab_ref[...], onehot) * LOG2E
+    return [line[h : h + 1] for h in range(HEADS)]
+
+
+def build_strip(lines, strip_s):
     for h in range(HEADS):
-        wide = jnp.broadcast_to(line[h : h + 1], (128, 1024))
+        wide = jnp.broadcast_to(lines[h], (128, 1024))
         strip_s[h] = pltpu.roll(wide, 0, 1, stride=1, stride_axis=0)[:, 128:]
+
+
+def square(w_s, m, cols=slice(None)):
+    block = w_s[m, :, :, cols]
+    return block.reshape(D, block.shape[-1])
 
 
 def project(x_ref, y_ref, vec_ref, w_s, q_s, k_s, v_s):
@@ -101,10 +253,10 @@
         cols = slice(pair * 128, pair * 128 + 256)
         x = x_ref[...]
         parts = (
-            (q_s, 0, mm(x, w_s[0, :, cols]) + vec_ref[0:1, cols]),
-            (q_s, 1, mm(y_ref[...], w_s[0, :, cols]) + vec_ref[0:1, cols]),
-            (k_s, None, mm(x, w_s[1, :, cols])),
-            (v_s, None, mm(x, w_s[2, :, cols]) + vec_ref[1:2, cols]),
+            (q_s, 0, mm(x, square(w_s, 0, cols)) + vec_ref[0:1, cols]),
+            (q_s, 1, mm(y_ref[...], square(w_s, 0, cols)) + vec_ref[0:1, cols]),
+            (k_s, None, mm(x, square(w_s, 1, cols))),
+            (v_s, None, mm(x, square(w_s, 2, cols)) + vec_ref[1:2, cols]),
         )
         for ref, s, value in parts:
             value = value.astype(BF16)
@@ -150,16 +302,50 @@
     return centred * inverse, inverse
 
 
-def forward_kernel(
-    x_ref, y_ref, len_ref, rank_ref, vec_ref, tab_ref, wa_h, wi_h, wo_h,
-    oc_ref, oq_ref, q_h, k_h, v_h, p_h, ctx_h, n1_h, inv1_h, nl_h, act_h, slope_h, n2_h, inv2_h,
-    wa_s, wi_s, wo_s, q_s, k_s, v_s, ctx_s, nl_s, n1_s, br_s, inv1_s, inv2_s, w_sem, o_sem, st_sem,
-):
-    loads = [pltpu.make_async_copy(wa_h.at[i], wa_s.at[i], w_sem.at[i]) for i in range(4)]
-    loads.append(pltpu.make_async_copy(wi_h, wi_s, w_sem.at[4]))
-    loads.append(pltpu.make_async_copy(wo_h, wo_s, w_sem.at[5]))
-    for c in loads:
-        c.start()
+NETWORK = {
+    0: (("pass_on", 1), ("start_z", 2)),
+    2: (("share", 1),),
+    3: (("pass_on", 2),),
+    5: (("share", 2),),
+}
+
+
+def forward_kernel(linked, *refs):
+    refs = list(refs)
+    take = lambda n: [refs.pop(0) for _ in range(n)]
+    x_ref, y_ref, len_ref, rank_ref = take(4)
+    if linked:
+        (small_ref,) = take(1)
+        shards = take(6)
+    else:
+        vec_ref, tab_ref, *weights = take(5)
+    oc_ref, oq_ref, q_h, k_h, v_h, p_h, ctx_h, n1_h, inv1_h, nl_h, act_h, slope_h, n2_h, inv2_h = take(14)
+    if linked:
+        vec_h, *weights = take(4)
+    wa_s, wi_s, wo_s, q_s, k_s, v_s, ctx_s, nl_s, n1_s, br_s, inv1_s, inv2_s, o_sem, st_sem, w_sem = take(15)
+    copies = (wa_s, wi_s, wo_s)
+    if linked:
+        small_s, vec_ref, *sems = take(10)
+        net = Gather((wa_s, wi_s, wo_s, small_s), (w_sem, *sems))
+        r, z, c = places()
+        f = 2 * z + c
+        own = net.own(shards)
+        for batch in own:
+            for copy in batch:
+                copy.start()
+        small_s[f] = small_ref[...]
+        greet(
+            [(hop(r, m), f) for m in (1, 2, 3)] + [(r, (f + k) % 8) for k in range(1, 8)]
+        )
+        for k in range(1, 8):
+            net.small_copy(k).start()
+        for copy in own[0]:
+            copy.wait()
+        net.start_z(0)
+    else:
+        loads = [pltpu.make_async_copy(src, dst, w_sem.at[i, 0]) for i, (src, dst) in enumerate(zip(weights, copies))]
+        for copy in loads:
+            copy.start()
     stores = []
 
     def keep(src, dst):
@@ -168,9 +354,21 @@
 
     def attention(strip_s, mask_s, p_st):
         build_masks(len_ref, rank_ref, mask_s)
-        build_strip(tab_ref, strip_s)
-        for c in loads[:3]:
-            c.wait()
+        if linked:
+            for k in range(1, 8):
+                net.small_come(k).wait_recv()
+            build_strip(lines_of(unpack_small(small_s, vec_ref)), strip_s)
+            net.pass_on(0)
+            for copy in own[1] + own[2]:
+                copy.wait()
+            net.start_z(1)
+            net.share(0)
+            net.finish(0)
+            keep(vec_ref, vec_h)
+            keep(wa_s, weights[0])
+        else:
+            build_strip(lines_of_table(tab_ref), strip_s)
+            loads[0].wait()
         project(x_ref, y_ref, vec_ref, wa_s, q_s, k_s, v_s)
         keep(q_s, q_h)
         keep(k_s, k_h)
@@ -185,6 +383,13 @@
             @pl.when(hp >= 2)
             def _():
                 store(hp - 2, slot).wait()
+
+            if linked:
+                for at, moves in NETWORK.items():
+                    @pl.when(hp == at)
+                    def _(moves=moves):
+                        for name, t in moves:
+                            getattr(net, name)(t)
 
             attend(q_s, k_s, v_s, strip_s, mask_s, p_st, ctx_s, hp, slot)
             store(hp, slot).start()
@@ -202,12 +407,11 @@
     )
     keep(ctx_s, ctx_h)
 
-    loads[3].wait()
     for s, in_ref in ((0, x_ref), (1, y_ref)):
         def first(i, carry, s=s, in_ref=in_ref):
             own = ds(i * 256, 256)
             rows = ds(s * SEQ + i * 256, 256)
-            r = in_ref[own, :].astype(F32) + mm(ctx_s[rows, :], wa_s[3]) + vec_ref[2:3, :]
+            r = in_ref[own, :].astype(F32) + mm(ctx_s[rows, :], square(wa_s, 3)) + vec_ref[2:3, :]
             n, inverse = norm_stats(r)
             n1_s[rows, :] = n
             inv1_s[rows, :] = jnp.broadcast_to(inverse, (256, 128))
@@ -219,8 +423,14 @@
     keep(inv1_s, inv1_h)
     keep(nl_s, nl_h)
 
-    loads[4].wait()
-    loads[5].wait()
+    if linked:
+        net.finish(1)
+        net.finish(2)
+        keep(wi_s, weights[1])
+        keep(wo_s, weights[2])
+    else:
+        loads[1].wait()
+        loads[2].wait()
     br_s[...] = jnp.zeros_like(br_s)
 
     def feed(act_st, slope_st):
@@ -238,13 +448,13 @@
                 for c in pair(t - 2, slot):
                     c.wait()
 
-            cols = ds(t * TILE, TILE)
-            inner = mm(nl_s[...], wi_s[:, cols]) + vec_ref[pl.ds(8 + (t // 3), 1), ds((t % 3) * TILE, TILE)]
+            part = ds((t % 3) * TILE, TILE)
+            inner = mm(nl_s[...], square(wi_s, t // 3, part)) + vec_ref[pl.ds(8 + (t // 3), 1), ds((t % 3) * TILE, TILE)]
             spread, bell = normal_parts(inner)
             act = (inner * spread).astype(BF16)
             act_st[slot] = act
             slope_st[slot] = (spread + inner * bell).astype(BF16)
-            br_s[...] += mm(act, wo_s[cols, :])
+            br_s[...] += mm(act, wo_s[t // 3, part, :])
             for c in pair(t, slot):
                 c.start()
             return carry
@@ -271,36 +481,54 @@
     keep(inv2_s, inv2_h)
     for i, (src, dst) in enumerate(stores):
         pltpu.make_async_copy(src, dst, o_sem.at[i]).wait()
-
-
-def call_forward(x, y, length, rank, vecs, table, wa, wi, wo):
+    if linked:
+        net.drain()
+
+
+WEIGHTS = ((4, 4, 192, D), (4, 4, 192, D), (4, D, D))
+
+
+def call_forward(linked, *args):
     hbm = pl.BlockSpec(memory_space=pl.ANY)
     vmem = pl.BlockSpec(memory_space=pltpu.VMEM)
     smem = pl.BlockSpec(memory_space=pltpu.SMEM)
+    dma = pltpu.SemaphoreType.DMA
     shape = jax.ShapeDtypeStruct
-    outs = (
+    outs = [
         shape((SEQ, D), BF16), shape((SEQ, D), BF16),
         shape((2, PAIRS, SEQ, 128), BF16), shape((PAIRS, SEQ, 128), BF16), shape((PAIRS, SEQ, 128), BF16),
         shape((PAIRS, 2, 2, SEQ, SEQ), BF16), shape((ROWS, D), BF16),
         shape((ROWS, D), F32), shape((ROWS, 128), F32), shape((ROWS, D), BF16),
         shape((TILES, ROWS, TILE), BF16), shape((TILES, ROWS, TILE), BF16),
         shape((ROWS, D), F32), shape((ROWS, 128), F32),
-    )
+    ]
+    scratch = [pltpu.VMEM(w, BF16) for w in WEIGHTS] + [
+        pltpu.VMEM((2, PAIRS, SEQ, 128), BF16), pltpu.VMEM((PAIRS, SEQ, 128), BF16), pltpu.VMEM((PAIRS, SEQ, 128), BF16),
+        pltpu.VMEM((ROWS, D), BF16), pltpu.VMEM((ROWS, D), BF16), pltpu.VMEM((ROWS, D), F32), pltpu.VMEM((ROWS, D), F32),
+        pltpu.VMEM((ROWS, 128), F32), pltpu.VMEM((ROWS, 128), F32),
+        dma((13,)), dma((4,)), dma((3, 4)),
+    ]
+    in_specs = [vmem, vmem, smem, vmem]
+    if linked:
+        in_specs += [vmem] + [hbm] * 6
+        outs += [shape((16, D), F32)] + [shape(w, BF16) for w in WEIGHTS]
+        scratch += [
+            pltpu.VMEM((8, 16, 128), BF16), pltpu.VMEM((16, D), F32),
+            dma((3, 3)), dma((3, 3)), dma((3, 9)), dma((3, 9)), dma((3, 4)), dma((3, 4)), dma((7,)), dma((7,)),
+        ]
+        params = pltpu.CompilerParams(vmem_limit_bytes=VMEM_LIMIT, collective_id=1, has_side_effects=True)
+    else:
+        in_specs += [vmem, vmem] + [hbm] * 3
+        params = pltpu.CompilerParams(vmem_limit_bytes=VMEM_LIMIT)
     return pl.pallas_call(
-        forward_kernel,
+        functools.partial(forward_kernel, linked),
         out_shape=outs,
-        in_specs=[vmem, vmem, smem, vmem, vmem, vmem, hbm, hbm, hbm],
-        out_specs=[vmem, vmem] + [hbm] * 12,
-        scratch_shapes=[
-            pltpu.VMEM((4, D, D), BF16), pltpu.VMEM((D, FF), BF16), pltpu.VMEM((FF, D), BF16),
-            pltpu.VMEM((2, PAIRS, SEQ, 128), BF16), pltpu.VMEM((PAIRS, SEQ, 128), BF16), pltpu.VMEM((PAIRS, SEQ, 128), BF16),
-            pltpu.VMEM((ROWS, D), BF16), pltpu.VMEM((ROWS, D), BF16), pltpu.VMEM((ROWS, D), F32), pltpu.VMEM((ROWS, D), F32),
-            pltpu.VMEM((ROWS, 128), F32), pltpu.VMEM((ROWS, 128), F32),
-            pltpu.SemaphoreType.DMA((6,)), pltpu.SemaphoreType.DMA((9,)), pltpu.SemaphoreType.DMA((4,)),
-        ],
-        compiler_params=pltpu.CompilerParams(vmem_limit_bytes=VMEM_LIMIT),
+        in_specs=in_specs,
+        out_specs=[vmem, vmem] + [hbm] * (len(outs) - 2),
+        scratch_shapes=scratch,
+        compiler_params=params,
         name="forward",
-    )(x, y, length, rank, vecs, table, wa, wi, wo)
+    )(*args)
 
 
 def norm_grad(u, gain, n, inverse):
@@ -337,8 +565,8 @@
             return (
                 pltpu.make_async_copy(act_h.at[t], act_s.at[slot], t_sem.at[slot]),
                 pltpu.make_async_copy(slope_h.at[t], slope_s.at[slot], t_sem.at[2 + slot]),
-                pltpu.make_async_copy(wi_h.at[:, ds(t * TILE, TILE)], wi_s.at[slot], t_sem.at[4 + slot]),
-                pltpu.make_async_copy(wo_h.at[ds(t * TILE, TILE), :], wo_s.at[slot], t_sem.at[6 + slot]),
+                pltpu.make_async_copy(wi_h.at[t // 3, :, :, ds((t % 3) * TILE, TILE)], wi_s.at[slot], t_sem.at[4 + slot]),
+                pltpu.make_async_copy(wo_h.at[t // 3, ds((t % 3) * TILE, TILE), :], wo_s.at[slot], t_sem.at[6 + slot]),
             )
 
         for c in fetch(0, 0):
@@ -397,7 +625,7 @@
             gin = mm(tr_s[...], di).astype(BF16)
             for j in range(3):
                 st_s[2 + slot, :, j * 256 : (j + 1) * 256] = gin[j * 256 : (j + 1) * 256, :]
-            g_s[...] += mm_nt(di, wi_s[slot])
+            g_s[...] += mm_nt(di, wi_s[slot].reshape(D, TILE))
             for c in out_copies(t, slot):
                 c.start()
             return carry
@@ -437,7 +665,7 @@
         for j in range(3):
             st_s[j] = mm(tr_s[j * 256 : (j + 1) * 256, :], db_s[...]).astype(BF16)
         for j in range(4):
-            dctx_s[j * 256 : (j + 1) * 256, :] = mm_nt(db_s[j * 256 : (j + 1) * 256, :], wa_s[3]).astype(BF16)
+            dctx_s[j * 256 : (j + 1) * 256, :] = mm_nt(db_s[j * 256 : (j + 1) * 256, :], square(wa_s, 3)).astype(BF16)
         cs = [pltpu.make_async_copy(st_s.at[j], ga_h.at[3, j * 256 : (j + 1) * 256, :], g_sem.at[j]) for j in range(3)]
         for c in cs:
             c.start()
@@ -452,7 +680,7 @@
         pltpu.VMEM((ROWS, D), BF16),
         pltpu.VMEM((2, ROWS, TILE), BF16),
         pltpu.VMEM((2, ROWS, TILE), BF16),
-        pltpu.VMEM((2, D, TILE), BF16),
+        pltpu.VMEM((2, 4, 192, TILE), BF16),
         pltpu.VMEM((2, TILE, D), BF16),
     )
 
@@ -563,8 +791,8 @@
                 c.start()
                 cs.append(c)
                 slot += 1
-        gc_ref[...] = g_s[0:SEQ, :] + mm_nt(dq_s[0:SEQ, :], wa_s[0]) + mm_nt(dk, wa_s[1]) + mm_nt(dv, wa_s[2])
-        gq_ref[...] = g_s[SEQ:, :] + mm_nt(dq_s[SEQ:, :], wa_s[0])
+        gc_ref[...] = g_s[0:SEQ, :] + mm_nt(dq_s[0:SEQ, :], square(wa_s, 0)) + mm_nt(dk, square(wa_s, 1)) + mm_nt(dv, square(wa_s, 2))
+        gq_ref[...] = g_s[SEQ:, :] + mm_nt(dq_s[SEQ:, :], square(wa_s, 0))
         for c in cs[-4:]:
             c.wait()
 
@@ -599,7 +827,7 @@
         in_specs=[vmem] * 5 + [hbm] * 15,
         out_specs=[vmem, vmem, hbm, hbm, hbm, vmem, vmem],
         scratch_shapes=[
-            pltpu.VMEM((4, D, D), BF16), pltpu.VMEM((ROWS, D), BF16), pltpu.VMEM((ROWS, D), F32), pltpu.VMEM((ROWS, D), BF16),
+            pltpu.VMEM(WEIGHTS[0], BF16), pltpu.VMEM((ROWS, D), BF16), pltpu.VMEM((ROWS, D), F32), pltpu.VMEM((ROWS, D), BF16),
             pltpu.VMEM((D, ROWS), BF16), pltpu.VMEM((4, TILE, D), BF16),
             pltpu.SemaphoreType.DMA((5,)), pltpu.SemaphoreType.DMA((8,)), pltpu.SemaphoreType.DMA((4,)),
         ],
@@ -613,26 +841,30 @@
     output_weight, output_bias, norm_gain, norm_shift, inner_weight, inner_bias, outer_weight, outer_bias, final_gain,
     final_shift, bucket_bias, content_cotangent, query_cotangent,
 ):
-    def gather(a, axis=0):
-        return lax.all_gather(a, "fsdp", axis=axis, tiled=True)
-
-    wa = gather(jnp.stack([query_weight, key_weight, value_weight, output_weight]), 1)
-    wi = gather(inner_weight)
-    wo = gather(outer_weight)
     small = (query_bias, value_bias, output_bias, norm_gain, norm_shift, outer_bias, final_gain, final_shift)
     width = query_bias.shape[0]
-    packed = jnp.concatenate([*small, inner_bias, bucket_bias])[None, :]
-    packed = gather(packed)
-    cuts = [packed[:, i * width : (i + 1) * width].reshape(1, D) for i in range(8)]
-    at = 8 * width
-    cuts.append(packed[:, at : at + inner_bias.shape[0]].reshape(4, D))
-    at += inner_bias.shape[0]
-    vecs = jnp.concatenate(cuts + [jnp.zeros((4, D), BF16)]).astype(F32)
-    table = jnp.pad(packed[:, at:].reshape(HEADS, BUCKETS), ((0, 4), (0, 128 - BUCKETS)))
-
-    out_c, out_q, *saved = call_forward(
-        content_stream, query_stream, lengths, ranking, vecs, table, wa, wi, wo
-    )
+    linked = width * 8 == D and lax.axis_size("rep") == 4
+    front = (content_stream, query_stream, lengths, ranking)
+    if linked:
+        rows = jnp.pad(jnp.stack(small), ((0, 0), (0, 128 - width)))
+        rest = jnp.pad(bucket_bias, (0, 128 - bucket_bias.shape[0])).reshape(1, 128)
+        packed = jnp.concatenate([rows, inner_bias.reshape(3, 128), rest, jnp.zeros((4, 128), BF16)])
+        out_c, out_q, *saved, vecs, wa, wi, wo = call_forward(
+            True, *front, packed, query_weight, key_weight, value_weight, output_weight, inner_weight, outer_weight
+        )
+    else:
+        def gather(a, axis=0):
+            return lax.all_gather(a, "fsdp", axis=axis, tiled=True)
+
+        wa = gather(jnp.stack([query_weight, key_weight, value_weight, output_weight]), 1).reshape(WEIGHTS[0])
+        wi = gather(inner_weight).reshape(D, 4, D).transpose(1, 0, 2).reshape(WEIGHTS[1])
+        wo = gather(outer_weight).reshape(WEIGHTS[2])
+        packed = gather(jnp.concatenate([*small, inner_bias, bucket_bias])[None, :])
+        cuts = [packed[:, i * width : (i + 1) * width].reshape(1, D) for i in range(8)]
+        cuts.append(packed[:, 8 * width : 12 * width].reshape(4, D))
+        vecs = jnp.concatenate(cuts + [jnp.zeros((4, D), BF16)]).astype(F32)
+        table = jnp.pad(packed[:, 12 * width :].reshape(HEADS, BUCKETS), ((0, 4), (0, 128 - BUCKETS)))
+        out_c, out_q, *saved = call_forward(False, *front, vecs, table, wa, wi, wo)
     gc, gq, ga, gi, go, gvec, gtab = call_backward(
         content_stream, query_stream, content_cotangent, query_cotangent, vecs, wa, wi, wo, saved
     )

time: 535 us -> 446 us (0.83)
  waiting for transfers between devices: 285 us -> 166 us
  Pallas kernels: 120 us -> 191 us
  blocking collectives: 67.7 us -> 36.4 us
  local copies, waits for them, and re-layouts: 37.8 us -> 31.5 us
    all_gather x3 -> x0, waiting for transfers between devices: 115 us -> none  [gather(): return lax.all_gather(a, 'fsdp', axis=axis, tiled=True)]
    pallas_call x1, Pallas kernels: 59.2 us -> 129 us  [call_forward(): pl.pallas_call(functools.partial(forward_kernel, linked), out_shape=outs,...]
    unnamed x2 -> x1, blocking collectives: 57.9 us -> 26.5 us
    concatenate x2 -> x1, local copies, waits for them, and re-layouts: 6.86 us -> 0.08 us  [shards(): jnp.concatenate([rows, inner_bias.reshape(3, 128), rest, jnp.zeros((4, 12...]
  transfers between devices with their start and end apart: 7 -> 4, of which waited for: 7 -> 4; matrix products, arithmetic and copies ran while one was open for 7% -> 6% of each run, Pallas kernels for 0% -> 0%
where the time goes in v2:
time: 446 us; the launch traced here: 445 us
  Pallas kernels  191 us (43%)
  waiting for transfers between devices  166 us (37%)
  blocking collectives  36.4 us (8%)
  local copies, waits for them, and re-layouts  31.5 us (7%)
  between operations  14.5 us (3%)
  other arithmetic  5.83 us (1%)
    reduce_scatter x3, waiting for transfers between devices, reduce(): a = lax.psum_scatter(a, 'fsdp', scatter_dimension=axis, tiled=True)  139 us
    pallas_call x1, Pallas kernels, call_forward(): pl.pallas_call(functools.partial(forward_kernel, linked), out_shape=outs,...  129 us
    pallas_call x1, Pallas kernels, call_backward(): pl.pallas_call(backward_kernel, out_shape=outs, in_specs=[vmem] * 5 + [hb...  61.5 us
    unnamed x1, blocking collectives  26.5 us
    psum x1, waiting for transfers between devices, reduce(): return lax.psum(a.astype(BF16), 'rep').astype(F32)  26.1 us
    unnamed x16, local copies, waits for them, and re-layouts  10.6 us
    psum x1, blocking collectives, shards(): flat = lax.psum(flat.astype(BF16), 'rep').astype(F32)  9.89 us
  transfers between devices with their start and end apart: 4, of which 4 were waited for; matrix products, arithmetic and copies ran while one was open for 6% of the time, Pallas kernels for 0%

profile of v2, /device:TPU:0, one launch (start us, length us, event | category | flops | bytes accessed | tf_op | source)
XLA Modules:
  0.0 445.3 jit_solution(4391090923580519502)
XLA Ops:
  7.2 0.0 reduce-scatter.4.cloned.1.call-start
  7.9 0.7 pad_bitcast_fusion
  8.5 0.1 pad.13.clone
  8.6 0.8 stack.35
  9.4 1.3 fusion.4.refs_4_
  10.8 129.2 %forward.1 = (bf16[512,768]{1,0:T(8,128)(2,1)}, bf16[512,768]{1,0:T(8,128)(2,1)}, bf16[2,6,512,128]{3,2,1,0:T(8,128)(2,1)}, bf16[6,512,128]{2,1,0:T(8,128)(2,1)}...) custom-call(bf16[512,768]{1,0:T(8,128)(2,1)} %x_ref.1, ...), custom_call_target="tpu_custom_call" | custom-call | tf_op jit(solution)/shard_map/forward/pallas_call | solution.py:523
  140.0 61.5 %backward.1 = (f32[512,768]{1,0:T(8,128)}, f32[512,768]{1,0:T(8,128)}, bf16[4,768,768]{2,1,0:T(8,128)(2,1)}, bf16[12,256,768]{2,1,0:T(8,128)(2,1)}, bf16[3072,76...) custom-call(bf16[512,768]{1,0:T(8,128)(2,1)} %x_ref.1, bf16[512,768]{1,0:T(8,128)(2,1)} %y_ref.1, ...), custom_call_target="tpu_custom_call" | custom-call | tf_op jit(solution)/shard_map/backward/pallas_call | solution.py:824
  201.5 0.0 reduce-scatter.4.cloned.1.call-update
  201.5 0.0 reduce-scatter.6.cloned.1.call-start
  201.6 6.9 %copy.45 = bf16[12,256,768]{1,2,0:T(8,128)(2,1)} copy(bf16[12,256,768]{2,1,0:T(8,128)(2,1)} %get-tuple-element.68) | data formatting | bytes 9437184 | tf_op jit(solution)/shard_map/backward/pallas_call | solution.py:824
  208.5 8.3 %copy.46 = bf16[3,256,12,256]{3,2,1,0:T(8,128)(2,1)} copy(bf16[3,256,12,256]{1,3,0,2:T(8,128)(2,1)} %bitcast.29) | data formatting | bytes 9437184 | tf_op jit(solution)/shard_map/transpose | solution.py:871
  216.8 8.2 %copy.47 = bf16[96,8,12,256]{3,1,2,0:T(8,128)(2,1)} copy(bf16[96,8,12,256]{3,2,1,0:T(8,128)(2,1)} %bitcast.27) | data formatting | bytes 9437184
  225.0 0.0 reduce-scatter.6.cloned.1.call-update
  225.0 0.0 reduce-scatter.8.cloned.1.call-start
  225.1 0.7 reduce-scatter.8.cloned.1.call-update
  225.8 0.0 all-reduce.6.cloned.1.call-start
  225.8 27.9 %reduce-scatter.4.cloned.1.call-done = bf16[4,96,768]{2,1,0:T(8,128)(2,1)} async-done(((bf16[4,768,768]{2,1,0:T(8,128)(2,1)}), bf16[4,96,768]{2,1,0:T(8,128)(2,1)}) %reduce-scatter.4.cloned.1.call-update) | async-done | bytes 589840 | tf_op jit(solution)/shard_map/reduce_scatter | solution.py:874
  253.7 55.7 %reduce-scatter.6.cloned.1.call-done = bf16[96,3072]{1,0:T(8,128)(2,1)} async-done(((bf16[768,3072]{1,0:T(8,128)(2,1)}), bf16[96,3072]{1,0:T(8,128)(2,1)}) %reduce-scatter.6.cloned.1.call-update) | async-done | bytes 589840 | tf_op jit(solution)/shard_map/reduce_scatter | solution.py:874
  309.4 55.7 %reduce-scatter.8.cloned.1.call-done = bf16[384,768]{1,0:T(8,128)(2,1)} async-done(((bf16[3072,768]{1,0:T(8,128)(2,1)}), bf16[384,768]{1,0:T(8,128)(2,1)}) %reduce-scatter.8.cloned.1.call-update) | async-done | bytes 589840 | tf_op jit(solution)/shard_map/reduce_scatter | solution.py:874
  365.0 0.0 all-reduce.6.cloned.1.call-update
  365.1 0.1 slice_reduce_fusion
  365.2 0.1 reshape_squeeze.24
  365.2 0.1 reshape_squeeze.25
  365.3 0.1 reshape_squeeze.26
  365.4 0.1 reshape_squeeze.27
  365.4 0.1 reshape_squeeze.28
  365.5 0.1 reshape_squeeze.29
  365.6 0.1 reshape_squeeze.30
  365.7 0.1 reshape_squeeze.31
  365.8 0.0 copy-done.4
  365.8 0.1 reshape.62
  365.8 0.0 copy-done.5
  365.8 0.6 dynamic-slice
  366.4 0.1 concatenate.7
  366.5 26.5 %all-reduce.2 = bf16[8,1200]{1,0:T(8,128)(2,1)S(1)} all-reduce(f32[8,1200]{1,0:T(8,128)S(1)} %concatenate.7), channel_id=3, replica_groups=mesh['rep'=4,'fsdp'=8] {'fsdp'}, use_global_device_ids=true, to_apply=%region_2.3.clone | all-reduce | flops 9600 | bytes 57600
  393.0 0.7 fusion.1
  393.7 9.9 %psum.29 = bf16[1200]{0:T(1024)(128)(2,1)S(1)} all-reduce(bf16[1200]{0:T(1024)(128)(2,1)S(1)} %fusion.1), channel_id=1, replica_groups=mesh['rep'=4,'fsdp'=8] {'rep'}, use_global_device_ids=true, to_apply=%region_3.4 | all-reduce | flops 1200 | bytes 4800 | tf_op jit(solution)/shard_map/psum | solution.py:887
  403.6 0.6 slice.105
  404.2 0.5 slice.109
  404.7 0.6 fusion.5
  405.3 26.1 %all-reduce.6.cloned.1.call-done = (bf16[4,96,768]{2,1,0:T(8,128)(2,1)}, bf16[96,3072]{1,0:T(8,128)(2,1)}, bf16[384,768]{1,0:T(8,128)(2,1)}) async-done(((bf16[4,96,768]{2,1,0:T(8,128)(2,1)}, bf16[96,3072]{1,0:T(8,128)(2,1)}, bf16[384,768]{1,0:T(8,128)(2,1)}), (bf16[4,96,768]{2,1,0:T(8,128)(2,1)}, bf16[96,3072]{1,0:T(8,128)(2,1)}, bf16[384,768]{1,0:T(8,128)(2,1)})) %all-reduce.6.cloned.1.call-update) | async-done | bytes 1769488 | tf_op jit(solution)/shard_map/psum | solution.py:875
  431.4 1.2 convert_element_type.22
  432.7 1.0 slice_bitcast_fusion
  433.7 2.2 convert_element_type.26
  435.9 0.0 copy-done.2
  435.9 1.1 convert_element_type.27
  437.0 0.9 copy.54
  437.8 0.9 copy.55
  (12 shorter events, 0.0 us)
Async XLA Ops:
  7.2 246.5 %reduce-scatter.4.cloned.1.call-start = ((), (), s32[]{:S(2)}) async-start(), calls=%async_computation.3 | async-start | bytes 5308416 | tf_op jit(solution)/shard_map/reduce_scatter | solution.py:874
  201.5 107.8 %reduce-scatter.6.cloned.1.call-start = ((), (), s32[]{:S(2)}) async-start(), calls=%async_computation.4 | async-start | bytes 5308416 | tf_op jit(solution)/shard_map/reduce_scatter | solution.py:874
  225.0 140.1 %copy-start.3 = (f32[16,768]{1,0:T(8,128)S(1)}, f32[16,768]{1,0:T(8,128)}, u32[]{:S(2)}) copy-start(f32[16,768]{1,0:T(8,128)} %get-tuple-element.66) | copy-start | bytes 147460
  225.0 140.8 %copy-start.4 = (f32[16,128]{1,0:T(8,128)S(1)}, f32[16,128]{1,0:T(8,128)}, u32[]{:S(2)}) copy-start(f32[16,128]{1,0:T(8,128)} %get-tuple-element.67) | copy-start | bytes 24580
  225.0 140.8 %copy-start.5 = (u32[32]{0:T(128)S(1)}, u32[32]{0:T(128)}, u32[]{:S(2)}) copy-start(u32[32]{0:T(128)} %constant.12) | copy-start | bytes 388
  225.0 140.0 %reduce-scatter.8.cloned.1.call-start = ((), (), s32[]{:S(2)}) async-start(), calls=%async_computation.5 | async-start | bytes 5308416 | tf_op jit(solution)/shard_map/reduce_scatter | solution.py:874
  225.8 205.7 %all-reduce.6.cloned.1.call-start = ((), (), s32[]{:S(2)}) async-start(), calls=%async_computation.6 | async-start | bytes 3538944 | tf_op jit(solution)/shard_map/psum | solution.py:875
  365.0 71.9 %copy-start.1 = (bf16[512,768]{1,0:T(8,128)(2,1)S(1)}, bf16[512,768]{1,0:T(8,128)(2,1)}, u32[]{:S(2)}) copy-start(bf16[512,768]{1,0:T(8,128)(2,1)} %get-tuple-element.113) | copy-start | bytes 2359300
  366.4 71.4 %copy-start = (bf16[512,768]{1,0:T(8,128)(2,1)S(1)}, bf16[512,768]{1,0:T(8,128)(2,1)}, u32[]{:S(2)}) copy-start(bf16[512,768]{1,0:T(8,128)(2,1)} %get-tuple-element.114) | copy-start | bytes 2359300
  431.4 4.4 copy-start.2
Sparse Core Ops, SparseCore 0:
  201.6 52.0 reduce-scatter.3
  256.0 53.3 reduce-scatter.5
  311.7 53.3 reduce-scatter.7
  368.3 63.0 all-reduce.5

commit v3 on v2

--- a/solution.py
+++ b/solution.py
@@ -24,7 +24,7 @@
 FAR_STEPS = (12, 16, 23, 32, 46, 64, 91)
 F32 = jnp.float32
 BF16 = jnp.bfloat16
-VMEM_LIMIT = 60 * 2**20
+VMEM_LIMIT = 62 * 2**20
 
 TAIL_P = 0.28
 TAIL = (
@@ -98,21 +98,29 @@
     pl.semaphore_wait(barrier, len(devices))
 
 
+def block_of(buffers, t, r, z, c):
+    if t == 2:
+        return buffers[2].at[z, pl.ds(pl.multiple_of(c * 384 + r * 96, 96), 96), :]
+    return buffers[t].at[r, z, ds(c * 96, 96), :]
+
+
+def slab_of(buffers, t, r, c):
+    if t == 2:
+        return buffers[2].at[:, pl.ds(pl.multiple_of(c * 384 + r * 96, 96), 96), :]
+    return buffers[t].at[r, :, ds(c * 96, 96), :]
+
+
 class Gather:
     def __init__(self, refs, sems):
-        self.wa, self.wi, self.wo, self.small = refs
+        *self.w, self.small = refs
         self.l_sem, self.zs, self.zr, self.xs, self.xr, self.cs, self.cr, self.vs, self.vr = sems
         self.r, self.z, self.c = places()
 
     def block(self, t, r, z, c):
-        if t == 2:
-            return self.wo.at[z, pl.ds(pl.multiple_of(c * 384 + r * 96, 96), 96), :]
-        return (self.wa, self.wi)[t].at[r, z, ds(c * 96, 96), :]
+        return block_of(self.w, t, r, z, c)
 
     def slab(self, t, r, c):
-        if t == 2:
-            return self.wo.at[:, pl.ds(pl.multiple_of(c * 384 + r * 96, 96), 96), :]
-        return (self.wa, self.wi)[t].at[r, :, ds(c * 96, 96), :]
+        return slab_of(self.w, t, r, c)
 
     def own(self, shards):
         *square, inner, outer = shards
@@ -123,7 +131,7 @@
                 pltpu.make_async_copy(inner.at[:, m * D : (m + 1) * D], self.block(1, m, z, c), self.l_sem.at[1, m])
                 for m in range(4)
             ],
-            [pltpu.make_async_copy(outer, self.wo.at[z, ds(c * 384, 384), :], self.l_sem.at[2, 0])],
+            [pltpu.make_async_copy(outer, self.w[2].at[z, ds(c * 384, 384), :], self.l_sem.at[2, 0])],
         ]
         return copies
 
@@ -531,6 +539,222 @@
     )(*args)
 
 
+class Reduce:
+    def __init__(self, refs, sems):
+        self.g, (self.cr1, self.cr2, self.xr0, self.xr, self.zr0, self.zr, self.tt, self.yr, self.res) = refs
+        self.cs, self.cr, self.credit, self.xs, self.xd, self.zs, self.zd, self.ys, self.yd, self.as_, self.ad = sems
+        self.r, self.z, self.c = places()
+        self.f = 2 * self.z + self.c
+        x, y = self.r % 2, self.r // 2
+        self.keep, self.give = (x, 2 + y), (1 - x, 3 - y)
+
+    def block(self, t, q, z):
+        return block_of(self.g, t, q, z, self.c)
+
+    def core(self, t, i):
+        if t == 2:
+            src, dst = self.g[2].at[i, ds((1 - self.c) * 384, 384), :], self.cr2.at[i]
+        else:
+            src, dst = slab_of(self.g, t, i, 1 - self.c), self.cr1.at[i]
+        return remote(src, dst, self.cs.at[t, i], self.cr.at[t, i], (self.r, 2 * self.z + 1 - self.c))
+
+    def start_core(self, t, i):
+        self.core(t, i).start()
+
+    def across(self, t, m):
+        if t == 0:
+            to = hop(self.r, m + 1)
+            return remote(slab_of(self.g, 0, to, self.c), self.xr0.at[m], self.xs.at[0, m], self.xd.at[0, m], (to, self.f))
+        src = slab_of(self.g, t, self.give[m], self.c)
+        return remote(src, self.xr.at[t - 1, m], self.xs.at[t, m], self.xd.at[t, m], (hop(self.r, m + 1), self.f))
+
+    def along(self, t, k, m):
+        to = hop(self.z, k + 1)
+        device = (self.r, 2 * to + self.c)
+        if t == 0:
+            return remote(self.block(0, self.r, to), self.zr0.at[k], self.zs.at[0, k], self.zd.at[0, k], device)
+        at = 2 * k + m
+        src = self.block(t, self.keep[m], to)
+        return remote(src, self.zr.at[t - 1, k, m], self.zs.at[t, at], self.zd.at[t, at], device)
+
+    def complete(self, t, m):
+        src, dst = self.tt.at[t - 1, m], self.yr.at[t - 1, m]
+        return remote(src, dst, self.ys.at[t - 1, m], self.yd.at[t - 1, m], (hop(self.r, 2 - m), self.f))
+
+    def spread(self, t, m, come=False):
+        far = hop(self.r, m + 1)
+        if t == 0:
+            ref = self.res.at[0, far if come else self.r]
+        else:
+            ref = self.res.at[t, self.give[m] if come else self.keep[m]]
+        return remote(ref, ref, self.as_.at[t, m], self.ad.at[t, m], (far, self.f))
+
+    def cores(self, t):
+        for i in range(4):
+            self.core(t, i).wait_recv()
+
+        def add(i, carry):
+            if t == 2:
+                rows = ds(self.c * 384, 384)
+                total = self.g[2][i, rows, :].astype(F32) + self.cr2[i].astype(F32)
+                self.g[2][i, rows, :] = total.astype(BF16)
+            else:
+                rows = ds(self.c * 96, 96)
+                total = self.g[t][i, :, rows, :].astype(F32) + self.cr1[i].astype(F32)
+                self.g[t][i, :, rows, :] = total.astype(BF16)
+            return carry
+
+        lax.fori_loop(0, 4, add, 0)
+        if t == 1:
+            pl.semaphore_signal(
+                self.credit, inc=1, device_id=(self.r, 2 * self.z + 1 - self.c), device_id_type=pl.DeviceIdType.MESH
+            )
+        for m in range(3 if t == 0 else 2):
+            self.across(t, m).start()
+
+    def replicas(self, t):
+        for m in range(3 if t == 0 else 2):
+            self.across(t, m).wait_recv()
+
+        def add(i, carry):
+            if t == 0:
+                ref = self.block(0, self.r, i)
+                total = ref[...].astype(F32)
+                for m in range(3):
+                    total = total + self.xr0[m, i].astype(F32)
+                ref[...] = total.astype(BF16)
+            else:
+                for m in range(2):
+                    ref = self.block(t, self.keep[m], i)
+                    ref[...] = (ref[...].astype(F32) + self.xr[t - 1, m, i].astype(F32)).astype(BF16)
+            return carry
+
+        lax.fori_loop(0, 4, add, 0)
+        for k in range(3):
+            for m in range(1 if t == 0 else 2):
+                self.along(t, k, m).start()
+
+    def owners(self, t):
+        for k in range(3):
+            for m in range(1 if t == 0 else 2):
+                self.along(t, k, m).wait_recv()
+        if t == 0:
+            total = self.block(0, self.r, self.z)[...].astype(F32)
+            for k in range(3):
+                total = total + self.zr0[k].astype(F32)
+            self.res[0, self.r] = total.astype(BF16)
+            for m in range(3):
+                self.spread(0, m).start()
+            return
+        for m in range(2):
+            total = self.block(t, self.keep[m], self.z)[...].astype(F32)
+            for k in range(3):
+                total = total + self.zr[t - 1, k, m].astype(F32)
+            self.tt[t - 1, m] = total.astype(BF16)
+            self.complete(t, m).start()
+
+    def ends(self, t):
+        for m in range(2):
+            self.complete(t, m).wait_recv()
+            total = self.tt[t - 1, m].astype(F32) + self.yr[t - 1, m].astype(F32)
+            self.res[t, self.keep[m]] = total.astype(BF16)
+            self.spread(t, m).start()
+
+    def finish(self, t):
+        for m in range(3 if t == 0 else 2):
+            self.spread(t, m, True).wait_recv()
+
+    def drain(self):
+        for t in range(3):
+            for i in range(4):
+                self.core(t, i).wait_send()
+            for m in range(3 if t == 0 else 2):
+                self.across(t, m).wait_send()
+                self.spread(t, m).wait_send()
+            for k in range(3):
+                for m in range(1 if t == 0 else 2):
+                    self.along(t, k, m).wait_send()
+            if t:
+                for m in range(2):
+                    self.complete(t, m).wait_send()
+
+
+class SmallReduce:
+    def __init__(self, refs, sems):
+        self.out, self.got, self.sums = refs
+        self.vs, self.vd, self.ws, self.wd = sems
+        self.r, z, c = places()
+        self.f = 2 * z + c
+
+    def first(self, k):
+        to = (self.f + k) % 8
+        return remote(self.out.at[to], self.got.at[self.f], self.vs.at[k - 1], self.vd.at[k - 1], (self.r, to))
+
+    def first_come(self, k):
+        back = (self.f + 8 - k) % 8
+        return remote(self.out.at[back], self.got.at[back], self.vs.at[k - 1], self.vd.at[k - 1], (self.r, back))
+
+    def second(self, m, come=False):
+        far = hop(self.r, m)
+        ref = self.sums.at[far if come else self.r]
+        return remote(ref, ref, self.ws.at[m - 1], self.wd.at[m - 1], (far, self.f))
+
+    def start(self, vec, table):
+        pack_small(vec, table, self.out)
+        self.got[self.f] = self.out[self.f]
+        for k in range(1, 8):
+            self.first(k).start()
+
+    def middle(self):
+        for k in range(1, 8):
+            self.first_come(k).wait_recv()
+        total = self.got[0]
+        for f in range(1, 8):
+            total = total + self.got[f]
+        self.sums[self.r] = total
+        for m in (1, 2, 3):
+            self.second(m).start()
+
+    def finish(self):
+        for m in (1, 2, 3):
+            self.second(m, True).wait_recv()
+        total = self.sums[0]
+        for r in range(1, 4):
+            total = total + self.sums[r]
+        return total
+
+    def drain(self):
+        for k in range(1, 8):
+            self.first(k).wait_send()
+        for m in (1, 2, 3):
+            self.second(m).wait_send()
+
+
+def pack_small(vec_ref, table, out_ref):
+    want = lax.broadcasted_iota(jnp.int32, (D, 1024), 0)
+    at = lax.broadcasted_iota(jnp.int32, (D, 1024), 1)
+    gathered = jnp.where((at % 128 < 96) & (want == (at // 128) * 96 + at % 128), 1.0, 0.0)
+    vec = vec_ref[...]
+    rows = lax.dot_general(
+        vec[0:8], gathered, (((1,), (0,)), ((), ())), precision=lax.Precision.HIGHEST, preferred_element_type=F32
+    )
+    lane = lax.broadcasted_iota(jnp.int32, (1, 128), 1)
+    for f in range(8):
+        m = f // 2
+        out_ref[f, 0:8, :] = rows[:, f * 128 : (f + 1) * 128]
+        for j in range(3):
+            col = (f % 2) * 384 + j * 128
+            out_ref[f, 8 + j : 9 + j, :] = vec[8 + m : 9 + m, col : col + 128]
+        head = 3 * m + f % 2
+        a, b = table[head : head + 1], table[head + 1 : head + 2]
+        if f % 2 == 0:
+            line = jnp.where(lane < 32, a, jnp.where(lane < 48, pltpu.roll(b, 32, 1), 0.0))
+        else:
+            line = jnp.where(lane < 16, pltpu.roll(a, 112, 1), jnp.where(lane < 48, pltpu.roll(b, 16, 1), 0.0))
+        out_ref[f, 11:12, :] = line
+        out_ref[f, 12:16, :] = jnp.zeros((4, 128), F32)
+
+
 def norm_grad(u, gain, n, inverse):
     ug = u * gain
     return inverse * (
@@ -538,28 +762,52 @@
     )
 
 
-def backward_kernel(
-    x_ref, y_ref, cc_ref, cq_ref, vec_ref, wa_h, wi_h, wo_h,
-    q_h, k_h, v_h, p_h, ctx_h, n1_h, inv1_h, nl_h, act_h, slope_h, n2_h, inv2_h,
-    gc_ref, gq_ref, ga_h, gi_h, go_h, gvec_ref, gtab_ref,
-    wa_s, ctx_s, g_s, dctx_s, tr_s, st_s, l_sem, t_sem, g_sem,
-):
-    wload = pltpu.make_async_copy(wa_h, wa_s, l_sem.at[0])
+BACK_NETWORK = {
+    1: (("replicas", 2),),
+    3: (("replicas", 1),),
+    4: (("owners", 2),),
+    5: (("ends", 2),),
+}
+
+
+def backward_kernel(linked, *refs):
+    refs = list(refs)
+    take = lambda n: [refs.pop(0) for _ in range(n)]
+    x_h, y_h, cc_h, cq_h, vec_ref, wa_h, wi_h, wo_h = take(8)
+    q_h, k_h, v_h, p_h, ctx_h, n1_h, inv1_h, nl_h, act_h, slope_h, n2_h, inv2_h = take(12)
+    gc_h, gq_h = take(2)
+    if linked:
+        res_ref, small_ref = take(2)
+    else:
+        *grads_h, gvec_ref, gtab_ref = take(5)
+    ctx_s, g_s, dctx_s, tr_s, l_sem, t_sem = take(6)
+    ga_s, gi_s, go_s = grads = take(3)
+    if linked:
+        gvec_ref, *more = take(10)
+        sum_refs = take(3)
+        sems = take(11)
+        sum_sems = take(4)
+        net = Reduce((grads, more[:9]), sems)
+        sums = SmallReduce(sum_refs, sum_sems)
+        r, z, c = places()
+        f = 2 * z + c
+        res_s = more[8]
     cload = pltpu.make_async_copy(ctx_h, ctx_s, l_sem.at[1])
-    wload.start()
     cload.start()
     gvec_ref[...] = jnp.zeros_like(gvec_ref)
 
     def add_vec(row, value, cols=slice(None)):
         gvec_ref[row : row + 1, cols] += jnp.sum(value, axis=0, keepdims=True)
 
-    def tail(n_s, inv_s, nl_s, db_s, act_s, slope_s, wi_s, wo_s):
+    def tail(n_s, inv_s, nl_s, db_s, act_s, slope_s, wi_s, wo_s, cot_s, wt_s):
+        wload = pltpu.make_async_copy(wa_h.at[3], wt_s, l_sem.at[0])
+        wload.start()
         nload = pltpu.make_async_copy(n2_h, n_s, l_sem.at[2])
         iload = pltpu.make_async_copy(inv2_h, inv_s, l_sem.at[3])
         nlload = pltpu.make_async_copy(nl_h, nl_s, l_sem.at[4])
-        nload.start()
-        iload.start()
-        nlload.start()
+        cots = [pltpu.make_async_copy(ref, cot_s.at[s], l_sem.at[5 + s]) for s, ref in enumerate((cc_h, cq_h))]
+        for copy in (nload, iload, *cots, nlload):
+            copy.start()
 
         def fetch(t, slot):
             return (
@@ -569,71 +817,70 @@
                 pltpu.make_async_copy(wo_h.at[t // 3, ds((t % 3) * TILE, TILE), :], wo_s.at[slot], t_sem.at[6 + slot]),
             )
 
-        for c in fetch(0, 0):
-            c.start()
-        nload.wait()
-        iload.wait()
-        for s, cot in ((0, cc_ref), (1, cq_ref)):
-            def second(i, carry, s=s, cot=cot):
-                rows = ds(s * SEQ + i * 128, 128)
-                u = cot[ds(i * 128, 128), :].astype(F32)
-                n = n_s[rows, :]
-                g = norm_grad(u, vec_ref[6:7, :], n, inv_s[rows, 0:1])
-                add_vec(6, u * n)
-                add_vec(7, u)
-                g_s[rows, :] = g
-                low = g.astype(BF16)
-                db_s[rows, :] = low
-                add_vec(5, low.astype(F32))
-                return carry
-
-            lax.fori_loop(0, SEQ // 128, second, 0)
+        for copy in fetch(0, 0):
+            copy.start()
+        if linked:
+            greet([(hop(r, m), f) for m in (1, 2, 3)] + [(r, (f + k) % 8) for k in range(1, 8)])
+        for copy in (nload, iload, *cots):
+            copy.wait()
+
+        def second(i, carry):
+            rows = ds(i * 128, 128)
+            u = cot_s[i // 4, ds((i % 4) * 128, 128), :].astype(F32)
+            n = n_s[rows, :]
+            g = norm_grad(u, vec_ref[6:7, :], n, inv_s[rows, 0:1])
+            add_vec(6, u * n)
+            add_vec(7, u)
+            g_s[rows, :] = g
+            low = g.astype(BF16)
+            db_s[rows, :] = low
+            add_vec(5, low.astype(F32))
+            return carry
+
+        lax.fori_loop(0, ROWS // 128, second, 0)
         n1load = pltpu.make_async_copy(n1_h, n_s, l_sem.at[2])
         i1load = pltpu.make_async_copy(inv1_h, inv_s, l_sem.at[3])
         n1load.start()
         i1load.start()
         nlload.wait()
         tr_s[...] = nl_s[...].T
-
-        def out_copies(t, slot):
-            return (
-                pltpu.make_async_copy(st_s.at[slot], go_h.at[ds(t * TILE, TILE), :], g_sem.at[slot]),
-                pltpu.make_async_copy(st_s.at[2 + slot, :, :], gi_h.at[t], g_sem.at[2 + slot]),
-            )
+        xyloads = [
+            pltpu.make_async_copy(ref, nl_s.at[s * SEQ : (s + 1) * SEQ, :], l_sem.at[5 + s])
+            for s, ref in enumerate((x_h, y_h))
+        ]
+        for copy in xyloads:
+            copy.start()
 
         def step(t, carry):
-            slot = (t % 2)
-            for c in fetch(t, slot):
-                c.wait()
+            slot = t % 2
+            for copy in fetch(t, slot):
+                copy.wait()
 
             @pl.when(t + 1 < TILES)
             def _():
-                for c in fetch(t + 1, 1 - slot):
-                    c.start()
-
-            @pl.when(t >= 2)
-            def _():
-                for c in out_copies(t - 2, slot):
-                    c.wait()
+                for copy in fetch(t + 1, 1 - slot):
+                    copy.start()
 
             db = db_s[...]
             di = (mm_nt(db, wo_s[slot]) * slope_s[slot].astype(F32)).astype(BF16)
-            row, cols = (t // 3), ds((t % 3) * TILE, TILE)
-            mine = lax.broadcasted_iota(jnp.int32, (8, TILE), 0) == row
-            gvec_ref[8:16, cols] += jnp.where(mine, jnp.sum(di.astype(F32), axis=0, keepdims=True), 0.0)
-            st_s[slot] = mm_tn(act_s[slot], db).astype(BF16)
-            gin = mm(tr_s[...], di).astype(BF16)
-            for j in range(3):
-                st_s[2 + slot, :, j * 256 : (j + 1) * 256] = gin[j * 256 : (j + 1) * 256, :]
+            i, part = t // 3, ds((t % 3) * TILE, TILE)
+            mine = lax.broadcasted_iota(jnp.int32, (8, TILE), 0) == i
+            gvec_ref[8:16, part] += jnp.where(mine, jnp.sum(di.astype(F32), axis=0, keepdims=True), 0.0)
+            go_s[i, part, :] = mm_tn(act_s[slot], db).astype(BF16)
+            gi_s[i, :, :, part] = mm(tr_s[...], di).astype(BF16).reshape(4, 192, TILE)
             g_s[...] += mm_nt(di, wi_s[slot].reshape(D, TILE))
-            for c in out_copies(t, slot):
-                c.start()
+            if linked:
+                @pl.when(t % 3 == 2)
+                def _():
+                    net.start_core(2, i)
+                    net.start_core(1, i)
+
             return carry
 
         lax.fori_loop(0, TILES, step, 0)
-        for t in (TILES - 2, TILES - 1):
-            for c in out_copies(t, t % 2):
-                c.wait()
+        if linked:
+            net.cores(2)
+            net.cores(1)
 
         n1load.wait()
         i1load.wait()
@@ -655,22 +902,15 @@
         wload.wait()
         cload.wait()
         tr_s[...] = ctx_s[...].T
-
-        def outer(j, carry):
-            cols = ds(j * 256, 256)
-            st_s[0, :, cols] = mm(tr_s[ds(j * 256, 256), :], db_s[...]).astype(BF16)[:, :256]
-            return carry
-
-        del outer
-        for j in range(3):
-            st_s[j] = mm(tr_s[j * 256 : (j + 1) * 256, :], db_s[...]).astype(BF16)
+        ga_s[3] = mm(tr_s[...], db_s[...]).astype(BF16).reshape(4, 192, D)
+        if linked:
+            pl.semaphore_wait(net.credit, 1)
+            net.start_core(0, 3)
         for j in range(4):
-            dctx_s[j * 256 : (j + 1) * 256, :] = mm_nt(db_s[j * 256 : (j + 1) * 256, :], square(wa_s, 3)).astype(BF16)
-        cs = [pltpu.make_async_copy(st_s.at[j], ga_h.at[3, j * 256 : (j + 1) * 256, :], g_sem.at[j]) for j in range(3)]
-        for c in cs:
-            c.start()
-        for c in cs:
-            c.wait()
+            dctx_s[j * 256 : (j + 1) * 256, :] = mm_nt(db_s[j * 256 : (j + 1) * 256, :], wt_s[...].reshape(D, D)).astype(BF16)
+        for copy in xyloads:
+            copy.wait()
+        tr_s[...] = nl_s[...].T
 
     pl.run_scoped(
         tail,
@@ -682,36 +922,50 @@
         pltpu.VMEM((2, ROWS, TILE), BF16),
         pltpu.VMEM((2, 4, 192, TILE), BF16),
         pltpu.VMEM((2, TILE, D), BF16),
+        pltpu.VMEM((2, SEQ, D), BF16),
+        pltpu.VMEM(WEIGHTS[0][1:], BF16),
     )
 
-    def attention(q_s, k_s, v_s, p_s, qt_s, dt_s, dq_s, dkt_s, dvt_s, far_s, bt_s):
-        cs = [pltpu.make_async_copy(a, b, l_sem.at[2 + i]) for i, (a, b) in enumerate(((q_h, q_s), (k_h, k_s), (v_h, v_s)))]
-        for c in cs:
-            c.start()
+    def attention(q_s, k_s, v_s, p_s, dq_s, dkt_s, dvt_s, far_s, bt_s, wa_s):
+        wload = pltpu.make_async_copy(wa_h.at[0:3], wa_s, l_sem.at[0])
+        wload.start()
+        loads = [(q_h, q_s), (k_h, k_s), (v_h, v_s)]
+        loads = [pltpu.make_async_copy(a, b, l_sem.at[2 + i]) for i, (a, b) in enumerate(loads)]
+        for copy in loads:
+            copy.start()
 
         def fetch(hp, slot):
             return pltpu.make_async_copy(p_h.at[hp], p_s.at[slot], t_sem.at[slot])
 
         fetch(0, 0).start()
-        for c in cs:
-            c.wait()
-        dt_s[...] = dctx_s[...].T
-        for s in range(2):
-            for hp in range(PAIRS):
-                qt_s[s, hp] = q_s[s, hp].T
+        for copy in loads:
+            copy.wait()
 
         def step(hp, carry):
-            slot = (hp % 2)
+            slot = hp % 2
             fetch(hp, slot).wait()
 
             @pl.when(hp + 1 < PAIRS)
             def _():
                 fetch(hp + 1, 1 - slot).start()
 
+            if linked:
+                for at, moves in BACK_NETWORK.items():
+                    @pl.when(hp == at)
+                    def _(moves=moves):
+                        for name, t in moves:
+                            getattr(net, name)(t)
+
+            attend_back(hp, slot)
+            return carry
+
+        def attend_back(hp, slot):
             lane = lax.broadcasted_iota(jnp.int32, (SEQ, 128), 1)
             k, v = k_s[hp], v_s[hp]
             zero = jnp.zeros((SEQ, 128), BF16)
             dq = [None, None]
+            qt = [q_s[s, hp].T for s in range(2)]
+            dt = [dctx_s[s * SEQ : (s + 1) * SEQ, ds(hp * 128, 128)].T for s in range(2)]
             for e in range(2):
                 own = (lane < 64) if e == 0 else (lane >= 64)
                 both = None
@@ -726,20 +980,20 @@
                     both = g if both is None else both + g
                     part = mm(low, jnp.where(own, k, zero))
                     dq[s] = part if dq[s] is None else dq[s] + part
-                    half = ds(hp * 128 + e * 64, 64)
-                    a = mm(dt_s[half, rows], p)
-                    b = mm(qt_s[s, hp, e * 64 : (e + 1) * 64, :], low)
+                    half = slice(e * 64, (e + 1) * 64)
+                    a = mm(dt[s][half], p)
+                    b = mm(qt[s][half], low)
                     dvt = a if dvt is None else dvt + a
                     dkt = b if dkt is None else dkt + b
                 dvt_s[ds(hp * 128 + e * 64, 64), :] = dvt.astype(BF16)
                 dkt_s[ds(hp * 128 + e * 64, 64), :] = (dkt * SCALE).astype(BF16)
-                sums = [None] * 7
+                parts = [None] * 5
                 for i in range(4):
                     for j in range(4):
                         blk = both[i * 128 : (i + 1) * 128, j * 128 : (j + 1) * 128]
                         at = min(max(j - i, -2), 2) + 2
-                        sums[at] = blk if sums[at] is None else sums[at] + blk
-                strip = jnp.concatenate([jnp.zeros((128, 128), F32), sums[1], sums[2], sums[3]], axis=1)
+                        parts[at] = blk if parts[at] is None else parts[at] + blk
+                strip = jnp.concatenate([jnp.zeros((128, 128), F32), parts[1], parts[2], parts[3]], axis=1)
                 flat = strip[0:8]
                 for g in range(1, 16):
                     flat = flat + pltpu.roll(strip[8 * g : 8 * g + 8], 512 - 8 * g, 1)
@@ -749,52 +1003,75 @@
                 h = 2 * hp + e
                 for ref, cols, value in (
                     (bt_s, slice(0, 512), flat),
-                    (far_s, slice(0, 128), sums[0]),
-                    (far_s, slice(128, 256), sums[4]),
+                    (far_s, slice(0, 128), parts[0]),
+                    (far_s, slice(128, 256), parts[4]),
                 ):
                     line = jnp.sum(value, axis=0, keepdims=True)
                     mine = lax.broadcasted_iota(jnp.int32, (16, line.shape[1]), 0) == h
                     ref[:, cols] = jnp.where(mine, line, ref[:, cols])
             for s in range(2):
                 dq_s[s * SEQ : (s + 1) * SEQ, ds(hp * 128, 128)] = (dq[s] * SCALE).astype(BF16)
-            return carry
 
         bt_s[...] = jnp.zeros_like(bt_s)
         far_s[...] = jnp.zeros_like(far_s)
         lax.fori_loop(0, PAIRS, step, 0)
+
+        dk = dkt_s[...].T
+        dv = dvt_s[...].T
+        for w, left, grad in ((1, slice(0, SEQ), dk), (2, slice(0, SEQ), dv), (0, slice(0, ROWS), dq_s[...])):
+            ga_s[w] = mm(tr_s[:, left], grad).astype(BF16).reshape(4, 192, D)
+            if linked:
+                net.start_core(0, w)
 
         offset = lax.broadcasted_iota(jnp.int32, (512, 128), 0) - 256
         bucket = lax.broadcasted_iota(jnp.int32, (512, 128), 1)
         near = jnp.where(bucket_of(offset) == bucket, 1.0, 0.0)
         lane = lax.broadcasted_iota(jnp.int32, (16, 128), 1)
-        gtab_ref[...] = (
+        table = (
             lax.dot_general(bt_s[...], near, (((1,), (0,)), ((), ())), precision=lax.Precision.HIGHEST, preferred_element_type=F32)
             + jnp.where(lane == 15, jnp.sum(far_s[:, 0:128], axis=1, keepdims=True), 0.0)
             + jnp.where(lane == 31, jnp.sum(far_s[:, 128:256], axis=1, keepdims=True), 0.0)
         )
-
-        dk = dkt_s[...].T
-        dv = dvt_s[...].T
         add_vec(0, dq_s[...].astype(F32))
         add_vec(1, dv.astype(F32))
-        tr_s[:, 0:SEQ] = x_ref[...].T
-        tr_s[:, SEQ:] = y_ref[...].T
-        slot = 0
-        cs = []
-        for w, grad in ((0, dq_s[...]), (1, dk), (2, dv)):
-            left = tr_s[...] if w == 0 else tr_s[:, 0:SEQ]
-            for j in range(3):
-                if len(cs) >= 4:
-                    cs[len(cs) - 4].wait()
-                st_s[slot % 4] = mm(left[j * 256 : (j + 1) * 256, :], grad).astype(BF16)
-                c = pltpu.make_async_copy(st_s.at[slot % 4], ga_h.at[w, j * 256 : (j + 1) * 256, :], g_sem.at[slot % 4])
-                c.start()
-                cs.append(c)
-                slot += 1
-        gc_ref[...] = g_s[0:SEQ, :] + mm_nt(dq_s[0:SEQ, :], square(wa_s, 0)) + mm_nt(dk, square(wa_s, 1)) + mm_nt(dv, square(wa_s, 2))
-        gq_ref[...] = g_s[SEQ:, :] + mm_nt(dq_s[SEQ:, :], square(wa_s, 0))
-        for c in cs[-4:]:
-            c.wait()
+        if linked:
+            net.cores(0)
+            sums.start(gvec_ref, table)
+            net.owners(1)
+        else:
+            gtab_ref[...] = table
+
+        wload.wait()
+        g_s[0:SEQ, :] += mm_nt(dq_s[0:SEQ, :], square(wa_s, 0)) + mm_nt(dk, square(wa_s, 1)) + mm_nt(dv, square(wa_s, 2))
+        g_s[SEQ:, :] += mm_nt(dq_s[SEQ:, :], square(wa_s, 0))
+        outs = [
+            pltpu.make_async_copy(g_s.at[s * SEQ : (s + 1) * SEQ, :], ref, l_sem.at[2 + s])
+            for s, ref in enumerate((gc_h, gq_h))
+        ]
+        for copy in outs:
+            copy.start()
+        if linked:
+            sums.middle()
+            net.replicas(0)
+            net.ends(1)
+            net.finish(2)
+            net.finish(1)
+            small_ref[...] = sums.finish()
+            res_ref[1] = res_s[1]
+            res_ref[2] = res_s[2]
+            net.owners(0)
+            net.finish(0)
+            res_ref[0] = res_s[0]
+            net.drain()
+            sums.drain()
+        else:
+            writes = [pltpu.make_async_copy(a, b, t_sem.at[i]) for i, (a, b) in enumerate(zip(grads, grads_h))]
+            for copy in writes:
+                copy.start()
+            for copy in writes:
+                copy.wait()
+        for copy in outs:
+            copy.wait()
 
     pl.run_scoped(
         attention,
@@ -802,36 +1079,53 @@
         pltpu.VMEM((PAIRS, SEQ, 128), BF16),
         pltpu.VMEM((PAIRS, SEQ, 128), BF16),
         pltpu.VMEM((2, 2, 2, SEQ, SEQ), BF16),
-        pltpu.VMEM((2, PAIRS, 128, SEQ), BF16),
-        pltpu.VMEM((D, ROWS), BF16),
         pltpu.VMEM((ROWS, D), BF16),
         pltpu.VMEM((D, SEQ), BF16),
         pltpu.VMEM((D, SEQ), BF16),
         pltpu.VMEM((16, 256), F32),
         pltpu.VMEM((16, 512), F32),
+        pltpu.VMEM((3, *WEIGHTS[0][1:]), BF16),
     )
 
 
-def call_backward(x, y, cc, cq, vecs, wa, wi, wo, saved):
+def call_backward(linked, x, y, cc, cq, vecs, wa, wi, wo, saved):
     hbm = pl.BlockSpec(memory_space=pl.ANY)
     vmem = pl.BlockSpec(memory_space=pltpu.VMEM)
+    dma = pltpu.SemaphoreType.DMA
     shape = jax.ShapeDtypeStruct
-    outs = (
-        shape((SEQ, D), F32), shape((SEQ, D), F32),
-        shape((4, D, D), BF16), shape((TILES, TILE, D), BF16), shape((FF, D), BF16),
-        shape((16, D), F32), shape((16, 128), F32),
-    )
+    outs = [shape((SEQ, D), F32), shape((SEQ, D), F32)]
+    out_specs = [hbm, hbm]
+    scratch = [
+        pltpu.VMEM((ROWS, D), BF16), pltpu.VMEM((ROWS, D), F32), pltpu.VMEM((ROWS, D), BF16),
+        pltpu.VMEM((D, ROWS), BF16), dma((7,)), dma((8,)),
+    ] + [pltpu.VMEM(w, BF16) for w in WEIGHTS]
+    if linked:
+        outs += [shape((3, 4, 96, D), BF16), shape((16, 128), F32)]
+        out_specs += [vmem, vmem]
+        scratch += [pltpu.VMEM((16, D), F32)] + [
+            pltpu.VMEM(s, BF16)
+            for s in (
+                (4, 4, 96, D), (4, 384, D), (3, 4, 96, D), (2, 2, 4, 96, D), (3, 96, D), (2, 3, 2, 96, D), (2, 2, 96, D),
+                (2, 2, 96, D), (3, 4, 96, D),
+            )
+        ]
+        scratch += [pltpu.VMEM((n, 16, 128), F32) for n in (8, 8, 4)]
+        scratch += [
+            dma((3, 4)), dma((3, 4)), pltpu.SemaphoreType.REGULAR, dma((3, 3)), dma((3, 3)), dma((3, 6)), dma((3, 6)),
+            dma((2, 2)), dma((2, 2)), dma((3, 3)), dma((3, 3)), dma((7,)), dma((7,)), dma((3,)), dma((3,)),
+        ]
+        params = pltpu.CompilerParams(vmem_limit_bytes=VMEM_LIMIT, collective_id=2, has_side_effects=True)
+    else:
+        outs += [shape(w, BF16) for w in WEIGHTS] + [shape((16, D), F32), shape((16, 128), F32)]
+        out_specs += [hbm] * 3 + [vmem, vmem]
+        params = pltpu.CompilerParams(vmem_limit_bytes=VMEM_LIMIT)
     return pl.pallas_call(
-        backward_kernel,
+        functools.partial(backward_kernel, linked),
         out_shape=outs,
-        in_specs=[vmem] * 5 + [hbm] * 15,
-        out_specs=[vmem, vmem, hbm, hbm, hbm, vmem, vmem],
-        scratch_shapes=[
-            pltpu.VMEM(WEIGHTS[0], BF16), pltpu.VMEM((ROWS, D), BF16), pltpu.VMEM((ROWS, D), F32), pltpu.VMEM((ROWS, D), BF16),
-            pltpu.VMEM((D, ROWS), BF16), pltpu.VMEM((4, TILE, D), BF16),
-            pltpu.SemaphoreType.DMA((5,)), pltpu.SemaphoreType.DMA((8,)), pltpu.SemaphoreType.DMA((4,)),
-        ],
-        compiler_params=pltpu.CompilerParams(vmem_limit_bytes=VMEM_LIMIT),
+        in_specs=[hbm] * 4 + [vmem] + [hbm] * 15,
+        out_specs=out_specs,
+        scratch_shapes=scratch,
+        compiler_params=params,
         name="backward",
     )(x, y, cc, cq, vecs, wa, wi, wo, *saved)
 
@@ -865,30 +1159,37 @@
         vecs = jnp.concatenate(cuts + [jnp.zeros((4, D), BF16)]).astype(F32)
         table = jnp.pad(packed[:, 12 * width :].reshape(HEADS, BUCKETS), ((0, 4), (0, 128 - BUCKETS)))
         out_c, out_q, *saved = call_forward(False, *front, vecs, table, wa, wi, wo)
-    gc, gq, ga, gi, go, gvec, gtab = call_backward(
-        content_stream, query_stream, content_cotangent, query_cotangent, vecs, wa, wi, wo, saved
-    )
-    gi = gi.reshape(TILES, TILE, 3, TILE).transpose(2, 1, 0, 3).reshape(D, FF)
-
-    def reduce(a, axis=0):
-        a = lax.psum_scatter(a, "fsdp", scatter_dimension=axis, tiled=True)
-        return lax.psum(a.astype(BF16), "rep").astype(F32)
-
-    ga = reduce(ga, 1)
-    gi = reduce(gi)
-    go = reduce(go)
-    count = D // width
-    flat = jnp.concatenate(
-        [gvec[i].reshape(count, width) for i in range(8)]
-        + [gvec[8:12].reshape(count, 4 * width), gtab[:HEADS, :BUCKETS].reshape(count, -1)],
-        axis=1,
-    )
-    flat = lax.psum_scatter(flat, "fsdp", scatter_dimension=0, tiled=True)[0]
-    flat = lax.psum(flat.astype(BF16), "rep").astype(F32)
-    v = [flat[i * width : (i + 1) * width] for i in range(8)]
+    streams = (content_stream, query_stream, content_cotangent, query_cotangent)
+    gc, gq, *grads = call_backward(linked, *streams, vecs, wa, wi, wo, saved)
+    if linked:
+        res, flat = grads
+        res = res.astype(F32)
+        ga, go = res[0], res[2].reshape(4 * width, D)
+        gi = res[1].transpose(1, 0, 2).reshape(width, FF)
+        v = [flat[i, :width] for i in range(8)]
+        inner, table = flat[8:11].reshape(4 * width), flat[11, : bucket_bias.shape[0]]
+    else:
+        def reduce(a, axis=0):
+            a = lax.psum_scatter(a, "fsdp", scatter_dimension=axis, tiled=True)
+            return lax.psum(a.astype(BF16), "rep").astype(F32)
+
+        ga, gi, go, gvec, gtab = grads
+        ga = reduce(ga.reshape(4, D, D), 1)
+        gi = reduce(gi.reshape(4, D, D).transpose(1, 0, 2).reshape(D, FF))
+        go = reduce(go.reshape(FF, D))
+        count = D // width
+        flat = jnp.concatenate(
+            [gvec[i].reshape(count, width) for i in range(8)]
+            + [gvec[8:12].reshape(count, 4 * width), gtab[:HEADS, :BUCKETS].reshape(count, -1)],
+            axis=1,
+        )
+        flat = lax.psum_scatter(flat, "fsdp", scatter_dimension=0, tiled=True)[0]
+        flat = lax.psum(flat.astype(BF16), "rep").astype(F32)
+        v = [flat[i * width : (i + 1) * width] for i in range(8)]
+        inner, table = flat[8 * width : 12 * width], flat[12 * width :]
     return (
         out_c, out_q, gc, gq, ga[0], v[0], ga[1], ga[2], v[1], ga[3], v[2], v[3], v[4], gi,
-        flat[8 * width : 12 * width], go, v[5], v[6], v[7], flat[12 * width :],
+        inner, go, v[5], v[6], v[7], table,
     )
 
 

time: 446 us -> 293 us (0.66)
  waiting for transfers between devices: 166 us -> 0 us
  Pallas kernels: 191 us -> 273 us
  blocking collectives: 36.4 us -> 0 us
  local copies, waits for them, and re-layouts: 31.5 us -> 15.2 us
  between operations: 14.5 us -> 1.35 us
    reduce_scatter x3 -> x0, waiting for transfers between devices: 139 us -> none  [reduce(): a = lax.psum_scatter(a, 'fsdp', scatter_dimension=axis, tiled=True)]
    pallas_call x1, Pallas kernels: 61.5 us -> 144 us  [call_backward(): pl.pallas_call(functools.partial(backward_kernel, linked), out_shape=outs...]
    unnamed x1 -> x0, blocking collectives: 26.5 us -> none
    psum x1 -> x0, waiting for transfers between devices: 26.1 us -> none  [reduce(): return lax.psum(a.astype(BF16), 'rep').astype(F32)]
    psum x1 -> x0, blocking collectives: 9.89 us -> none  [shards(): flat = lax.psum(flat.astype(BF16), 'rep').astype(F32)]
    transpose x1 -> x0, local copies, waits for them, and re-layouts: 8.27 us -> none  [shards(): gi = gi.reshape(TILES, TILE, 3, TILE).transpose(2, 1, 0, 3).reshape(D, FF)]
    pallas_call x1 -> x0, local copies, waits for them, and re-layouts: 6.92 us -> none  [call_backward(): pl.pallas_call(backward_kernel, out_shape=outs, in_specs=[vmem] * 5 + [hb...]
    unnamed x16 -> x15, local copies, waits for them, and re-layouts: 10.6 us -> 5.21 us
  transfers between devices with their start and end apart: 4 -> 0, of which waited for: 4 -> 0; matrix products, arithmetic and copies ran while one was open for 6% -> 0% of each run, Pallas kernels for 0% -> 0%
where the time goes in v3:
time: 293 us; the launch traced here: 291 us
  Pallas kernels  273 us (93%)
  local copies, waits for them, and re-layouts  15.2 us (5%)
    pallas_call x1, Pallas kernels, call_backward(): pl.pallas_call(functools.partial(backward_kernel, linked), out_shape=outs...  144 us
    pallas_call x1, Pallas kernels, call_forward(): pl.pallas_call(functools.partial(forward_kernel, linked), out_shape=outs,...  129 us

profile of v3, /device:TPU:0, one launch (start us, length us, event | category | flops | bytes accessed | tf_op | source)
XLA Modules:
  0.0 291.4 jit_solution(1864095686025826805)
XLA Ops:
  1.3 0.7 pad_bitcast_fusion
  2.0 0.1 pad.13.clone
  2.0 0.8 stack.35
  2.8 1.3 fusion.3.refs_4_
  4.2 129.2 %forward.1 = (bf16[512,768]{1,0:T(8,128)(2,1)}, bf16[512,768]{1,0:T(8,128)(2,1)}, bf16[2,6,512,128]{3,2,1,0:T(8,128)(2,1)}, bf16[6,512,128]{2,1,0:T(8,128)(2,1)}...) custom-call(bf16[512,768]{1,0:T(8,128)(2,1)} %refs_0_.3, ...), custom_call_target="tpu_custom_call" | custom-call | tf_op jit(solution)/shard_map/forward/pallas_call | solution.py:531
  133.4 144.1 %backward.1 = (f32[512,768]{1,0:T(8,128)}, f32[512,768]{1,0:T(8,128)}, bf16[3,4,96,768]{3,2,1,0:T(8,128)(2,1)}, f32[16,128]{1,0:T(8,128)}) custom-call(bf16[512,768]{1,0:T(8,128)(2,1)} %refs_0_.3, bf16[512,768]{1,0:T(8,128)(2,1)} %refs_1_.3, bf16[512,768]{1,0:T(8,128)(2,1)} %refs_2_.2, bf16[512,768]{1,0:T(8,128)(2,1)} %refs_3_.3, ...), custom_call_target="tpu_custom_call" | custom-call | tf_op jit(solution)/shard_map/backward/pallas_call | solution.py:1122
  277.4 0.0 copy-start
  277.4 1.3 slice_bitcast_fusion.6
  278.8 1.3 slice_bitcast_fusion.5
  280.0 1.5 slice_bitcast_fusion.7
  281.5 2.2 slice.78
  283.7 0.0 copy-done
  283.7 0.3 convert_element_type.7
  284.1 0.1 slice_bitcast_fusion
  284.2 1.0 slice_bitcast_fusion.1
  285.2 0.0 copy-start.4
  285.2 0.0 copy-start.3
  285.2 1.1 copy.43
  286.3 0.0 copy-start.2
  286.3 0.2 copy-done.4
  286.6 0.9 copy.49
  287.4 0.0 copy-done.3
  287.4 0.9 copy.50
  288.3 0.0 copy-done.2
  288.3 0.0 copy-start.1
  288.3 1.1 copy.51
  289.5 0.8 copy-done.1
  290.3 1.1 copy.52
  (1 shorter events, 0.0 us)
Async XLA Ops:
  277.4 6.3 %copy-start = (bf16[3,4,96,768]{3,2,1,0:T(8,128)(2,1)S(1)}, bf16[3,4,96,768]{3,2,1,0:T(8,128)(2,1)}, u32[]{:S(2)}) copy-start(bf16[3,4,96,768]{3,2,1,0:T(8,128)(2,1)} %get-tuple-element.62) | copy-start | bytes 5308420
  285.2 1.4 copy-start.4
  285.2 2.2 copy-start.3
  286.3 2.0 copy-start.2
  288.3 2.0 copy-start.1

commit v4 on v3

--- a/solution.py
+++ b/solution.py
@@ -98,16 +98,31 @@
     pl.semaphore_wait(barrier, len(devices))
 
 
+PIECES = 3
+
+
 def block_of(buffers, t, r, z, c):
     if t == 2:
         return buffers[2].at[z, pl.ds(pl.multiple_of(c * 384 + r * 96, 96), 96), :]
-    return buffers[t].at[r, z, ds(c * 96, 96), :]
-
-
-def slab_of(buffers, t, r, c):
-    if t == 2:
-        return buffers[2].at[:, pl.ds(pl.multiple_of(c * 384 + r * 96, 96), 96), :]
-    return buffers[t].at[r, :, ds(c * 96, 96), :]
+    return buffers[1].at[r, z, ds(c * 96, 96), :]
+
+
+def quarter(u, r, c):
+    rows = pl.ds(pl.multiple_of(c * 96 + (r // 2) * 48, 48), 48)
+    if isinstance(u, int) and u == PIECES:
+        return rows, ds((r % 2) * 384, 384)
+    return rows, pl.ds(pl.multiple_of(u * 256 + (r % 2) * 128, 128), 128)
+
+
+def matrices(u):
+    return 3 if isinstance(u, int) and u == PIECES else slice(0, 3)
+
+
+def columns(u):
+    return slice(0, D) if isinstance(u, int) and u == PIECES else ds(u * 256, 256)
+
+
+ALL = slice(0, 4)
 
 
 class Gather:
@@ -116,19 +131,20 @@
         self.l_sem, self.zs, self.zr, self.xs, self.xr, self.cs, self.cr, self.vs, self.vr = sems
         self.r, self.z, self.c = places()
 
-    def block(self, t, r, z, c):
-        return block_of(self.w, t, r, z, c)
-
-    def slab(self, t, r, c):
-        return slab_of(self.w, t, r, c)
+    def block(self, u, r, z, c):
+        if isinstance(u, int) and u > PIECES:
+            return block_of(self.w, u - PIECES, r, z, c)
+        rows, cols = quarter(u, r, c)
+        return self.w[0].at[matrices(u), z, rows, cols]
 
     def own(self, shards):
         *square, inner, outer = shards
         z, c = self.z, self.c
+        rows = ds(c * 96, 96)
         copies = [
-            [pltpu.make_async_copy(square[m], self.block(0, m, z, c), self.l_sem.at[0, m]) for m in range(4)],
+            [pltpu.make_async_copy(square[m], self.w[0].at[m, z, rows, :], self.l_sem.at[0, m]) for m in range(4)],
             [
-                pltpu.make_async_copy(inner.at[:, m * D : (m + 1) * D], self.block(1, m, z, c), self.l_sem.at[1, m])
+                pltpu.make_async_copy(inner.at[:, m * D : (m + 1) * D], self.block(4, m, z, c), self.l_sem.at[1, m])
                 for m in range(4)
             ],
             [pltpu.make_async_copy(outer, self.w[2].at[z, ds(c * 384, 384), :], self.l_sem.at[2, 0])],
@@ -145,52 +161,68 @@
         f = (2 * self.z + self.c + 8 - k) % 8
         return remote(self.small.at[f], self.small.at[f], self.vs.at[k - 1], self.vr.at[k - 1], (self.r, f))
 
-    def z_copy(self, t, k, come=False):
+    def z_copy(self, u, k, come=False):
         far = hop(self.z, k)
-        ref = self.block(t, self.r, far if come else self.z, self.c)
-        return remote(ref, ref, self.zs.at[t, k - 1], self.zr.at[t, k - 1], (self.r, 2 * far + self.c))
-
-    def x_copy(self, t, k, m, come=False):
+        ref = self.block(u, self.r, far if come else self.z, self.c)
+        return remote(ref, ref, self.zs.at[u, k - 1], self.zr.at[u, k - 1], (self.r, 2 * far + self.c))
+
+    def x_copy(self, u, k, m, come=False):
         far = hop(self.r, m)
-        ref = self.block(t, far if come else self.r, hop(self.z, k), self.c)
+        ref = self.block(u, far if come else self.r, hop(self.z, k), self.c)
         at = 3 * (k - 1) + m - 1
-        return remote(ref, ref, self.xs.at[t, at], self.xr.at[t, at], (far, 2 * self.z + self.c))
-
-    def c_copy(self, t, m, come=False):
-        ref = self.slab(t, hop(self.r, m), 1 - self.c if come else self.c)
-        return remote(ref, ref, self.cs.at[t, m], self.cr.at[t, m], (self.r, 2 * self.z + 1 - self.c))
-
-    def start_z(self, t):
+        return remote(ref, ref, self.xs.at[u, at], self.xr.at[u, at], (far, 2 * self.z + self.c))
+
+    def c_copy(self, u, m, come=False):
+        c = 1 - self.c if come else self.c
+        if isinstance(u, int) and u > PIECES:
+            ref = self.block(u, hop(self.r, m), ALL, c)
+        else:
+            ref = self.w[0].at[matrices(u), ALL, ds(c * 96, 96), columns(u)]
+        return remote(ref, ref, self.cs.at[u, m], self.cr.at[u, m], (self.r, 2 * self.z + 1 - self.c))
+
+    def parts(self, u):
+        return 4 if isinstance(u, int) and u > PIECES else 1
+
+    def start_z(self, u):
         for k in (1, 2, 3):
-            self.z_copy(t, k).start()
-
-    def pass_on(self, t):
+            self.z_copy(u, k).start()
+
+    def pass_on(self, u):
         for k in (1, 2, 3):
-            self.z_copy(t, k, True).wait_recv()
+            self.z_copy(u, k, True).wait_recv()
             for m in (1, 2, 3):
-                self.x_copy(t, k, m).start()
-
-    def share(self, t):
+                self.x_copy(u, k, m).start()
+
+    def share(self, u):
+        parts = self.parts(u)
         for m in range(4):
             if m:
                 for k in (1, 2, 3):
-                    self.x_copy(t, k, m, True).wait_recv()
-            self.c_copy(t, m).start()
-
-    def finish(self, t):
-        for m in range(4):
-            self.c_copy(t, m, True).wait_recv()
+                    self.x_copy(u, k, m, True).wait_recv()
+            if parts == 4:
+                self.c_copy(u, m).start()
+        if parts == 1:
+            self.c_copy(u, 0).start()
+
+    def finish(self, u):
+        for m in range(self.parts(u)):
+            self.c_copy(u, m, True).wait_recv()
 
     def drain(self):
         for k in range(1, 8):
             self.small_copy(k).wait_send()
-        for t in range(3):
+
+        def sent(u):
             for k in (1, 2, 3):
-                self.z_copy(t, k).wait_send()
+                self.z_copy(u, k).wait_send()
                 for m in (1, 2, 3):
-                    self.x_copy(t, k, m).wait_send()
-            for m in range(4):
-                self.c_copy(t, m).wait_send()
+                    self.x_copy(u, k, m).wait_send()
+            for m in range(self.parts(u)):
+                self.c_copy(u, m).wait_send()
+
+        lax.fori_loop(0, PIECES, lambda u, carry: (sent(u), carry)[1], 0)
+        for u in (3, 4, 5):
+            sent(u)
 
 
 def unpack_small(small_s, vec_s):
@@ -256,24 +288,23 @@
     return block.reshape(D, block.shape[-1])
 
 
-def project(x_ref, y_ref, vec_ref, w_s, q_s, k_s, v_s):
-    for pair in range(0, PAIRS, 2):
-        cols = slice(pair * 128, pair * 128 + 256)
-        x = x_ref[...]
-        parts = (
-            (q_s, 0, mm(x, square(w_s, 0, cols)) + vec_ref[0:1, cols]),
-            (q_s, 1, mm(y_ref[...], square(w_s, 0, cols)) + vec_ref[0:1, cols]),
-            (k_s, None, mm(x, square(w_s, 1, cols))),
-            (v_s, None, mm(x, square(w_s, 2, cols)) + vec_ref[1:2, cols]),
-        )
-        for ref, s, value in parts:
-            value = value.astype(BF16)
-            for e in range(2):
-                piece = value[:, e * 128 : (e + 1) * 128]
-                if s is None:
-                    ref[pair + e] = piece
-                else:
-                    ref[s, pair + e] = piece
+def project(x_ref, y_ref, vec_ref, w_s, q_s, k_s, v_s, p):
+    cols = ds(p * 256, 256)
+    x = x_ref[...]
+    parts = (
+        (q_s, 0, mm(x, square(w_s, 0, cols)) + vec_ref[0:1, cols]),
+        (q_s, 1, mm(y_ref[...], square(w_s, 0, cols)) + vec_ref[0:1, cols]),
+        (k_s, None, mm(x, square(w_s, 1, cols))),
+        (v_s, None, mm(x, square(w_s, 2, cols)) + vec_ref[1:2, cols]),
+    )
+    for ref, s, value in parts:
+        value = value.astype(BF16)
+        for e in range(2):
+            piece = value[:, e * 128 : (e + 1) * 128]
+            if s is None:
+                ref[2 * p + e] = piece
+            else:
+                ref[s, 2 * p + e] = piece
 
 
 def attend(q_s, k_s, v_s, strip_s, mask_s, p_st, ctx_s, hp, slot):
@@ -311,10 +342,12 @@
 
 
 NETWORK = {
-    0: (("pass_on", 1), ("start_z", 2)),
-    2: (("share", 1),),
-    3: (("pass_on", 2),),
-    5: (("share", 2),),
+    (0, 0): (("pass_on", 2), ("start_z", 3), ("start_z", 4)),
+    (0, 1): (("share", 1),),
+    (1, 0): (("pass_on", 3), ("start_z", 5)),
+    (1, 1): (("share", 2), ("pass_on", 4)),
+    (2, 0): (("share", 3),),
+    (2, 1): (("pass_on", 5),),
 }
 
 
@@ -349,7 +382,8 @@
             net.small_copy(k).start()
         for copy in own[0]:
             copy.wait()
-        net.start_z(0)
+        for u in range(PIECES):
+            net.start_z(u)
     else:
         loads = [pltpu.make_async_copy(src, dst, w_sem.at[i, 0]) for i, (src, dst) in enumerate(zip(weights, copies))]
         for copy in loads:
@@ -367,45 +401,48 @@
                 net.small_come(k).wait_recv()
             build_strip(lines_of(unpack_small(small_s, vec_ref)), strip_s)
             net.pass_on(0)
+            net.pass_on(1)
             for copy in own[1] + own[2]:
                 copy.wait()
-            net.start_z(1)
             net.share(0)
-            net.finish(0)
             keep(vec_ref, vec_h)
-            keep(wa_s, weights[0])
         else:
             build_strip(lines_of_table(tab_ref), strip_s)
             loads[0].wait()
-        project(x_ref, y_ref, vec_ref, wa_s, q_s, k_s, v_s)
+
+        def store(hp, slot):
+            return pltpu.make_async_copy(p_st.at[slot], p_h.at[hp], st_sem.at[slot])
+
+        def hooks(p, part):
+            for (at, when), moves in NETWORK.items():
+                if when == part:
+                    @pl.when(p == at)
+                    def _(moves=moves):
+                        for name, u in moves:
+                            getattr(net, name)(u)
+
+        def step(p, carry):
+            if linked:
+                net.finish(p)
+            project(x_ref, y_ref, vec_ref, wa_s, q_s, k_s, v_s, p)
+            for part in range(2):
+                if linked:
+                    hooks(p, part)
+
+                @pl.when(p >= 1)
+                def _():
+                    store(2 * p - 2 + part, part).wait()
+
+                attend(q_s, k_s, v_s, strip_s, mask_s, p_st, ctx_s, 2 * p + part, part)
+                store(2 * p + part, part).start()
+            return carry
+
+        lax.fori_loop(0, PIECES, step, 0)
+        for part in range(2):
+            store(PAIRS - 2 + part, part).wait()
         keep(q_s, q_h)
         keep(k_s, k_h)
         keep(v_s, v_h)
-
-        def store(hp, slot):
-            return pltpu.make_async_copy(p_st.at[slot], p_h.at[hp], st_sem.at[slot])
-
-        def step(hp, carry):
-            slot = (hp % 2)
-
-            @pl.when(hp >= 2)
-            def _():
-                store(hp - 2, slot).wait()
-
-            if linked:
-                for at, moves in NETWORK.items():
-                    @pl.when(hp == at)
-                    def _(moves=moves):
-                        for name, t in moves:
-                            getattr(net, name)(t)
-
-            attend(q_s, k_s, v_s, strip_s, mask_s, p_st, ctx_s, hp, slot)
-            store(hp, slot).start()
-            return carry
-
-        lax.fori_loop(0, PAIRS, step, 0)
-        store(PAIRS - 2, 0).wait()
-        store(PAIRS - 1, 1).wait()
 
     pl.run_scoped(
         attention,
@@ -414,6 +451,9 @@
         pltpu.VMEM((2, 2, 2, SEQ, SEQ), BF16),
     )
     keep(ctx_s, ctx_h)
+    if linked:
+        net.finish(3)
+        keep(wa_s, weights[0])
 
     for s, in_ref in ((0, x_ref), (1, y_ref)):
         def first(i, carry, s=s, in_ref=in_ref):
@@ -432,47 +472,61 @@
     keep(nl_s, nl_h)
 
     if linked:
-        net.finish(1)
-        net.finish(2)
+        net.share(4)
+        net.finish(4)
         keep(wi_s, weights[1])
-        keep(wo_s, weights[2])
     else:
         loads[1].wait()
         loads[2].wait()
-    br_s[...] = jnp.zeros_like(br_s)
-
-    def feed(act_st, slope_st):
+
+    def feed(act_s, slope_st):
+        def part(t):
+            return ds(t * TILE, TILE)
+
         def pair(t, slot):
             return (
-                pltpu.make_async_copy(act_st.at[slot], act_h.at[t], st_sem.at[slot]),
-                pltpu.make_async_copy(slope_st.at[slot], slope_h.at[t], st_sem.at[2 + slot]),
+                pltpu.make_async_copy(act_s.at[:, part(t)], act_h.at[:, part(t)], st_sem.at[slot]),
+                pltpu.make_async_copy(slope_st.at[slot], slope_h.at[:, part(t)], st_sem.at[2 + slot]),
             )
 
         def step(t, carry):
-            slot = (t % 2)
+            slot = t % 2
 
             @pl.when(t >= 2)
             def _():
                 for c in pair(t - 2, slot):
                     c.wait()
 
-            part = ds((t % 3) * TILE, TILE)
-            inner = mm(nl_s[...], square(wi_s, t // 3, part)) + vec_ref[pl.ds(8 + (t // 3), 1), ds((t % 3) * TILE, TILE)]
+            if linked:
+                @pl.when(t == 9)
+                def _():
+                    net.share(5)
+
+            cols = ds((t % 3) * TILE, TILE)
+            inner = mm(nl_s[...], square(wi_s, t // 3, cols)) + vec_ref[pl.ds(8 + (t // 3), 1), cols]
             spread, bell = normal_parts(inner)
-            act = (inner * spread).astype(BF16)
-            act_st[slot] = act
+            act_s[:, part(t)] = (inner * spread).astype(BF16)
             slope_st[slot] = (spread + inner * bell).astype(BF16)
-            br_s[...] += mm(act, wo_s[t // 3, part, :])
             for c in pair(t, slot):
                 c.start()
             return carry
 
         lax.fori_loop(0, TILES, step, 0)
+        if linked:
+            net.finish(5)
+            keep(wo_s, weights[2])
+
+        def outer(i, carry):
+            rows = ds(i * 256, 256)
+            br_s[rows, :] = mm(act_s[rows, :], wo_s[...].reshape(FF, D))
+            return carry
+
+        lax.fori_loop(0, ROWS // 256, outer, 0)
         for t in (TILES - 2, TILES - 1):
             for c in pair(t, t % 2):
                 c.wait()
 
-    pl.run_scoped(feed, pltpu.VMEM((2, ROWS, TILE), BF16), pltpu.VMEM((2, ROWS, TILE), BF16))
+    pl.run_scoped(feed, pltpu.VMEM((ROWS, FF), BF16), pltpu.VMEM((2, ROWS, TILE), BF16))
 
     for s, o_ref in ((0, oc_ref), (1, oq_ref)):
         def last(i, carry, s=s, o_ref=o_ref):
@@ -507,7 +561,7 @@
         shape((2, PAIRS, SEQ, 128), BF16), shape((PAIRS, SEQ, 128), BF16), shape((PAIRS, SEQ, 128), BF16),
         shape((PAIRS, 2, 2, SEQ, SEQ), BF16), shape((ROWS, D), BF16),
         shape((ROWS, D), F32), shape((ROWS, 128), F32), shape((ROWS, D), BF16),
-        shape((TILES, ROWS, TILE), BF16), shape((TILES, ROWS, TILE), BF16),
+        shape((ROWS, FF), BF16), shape((ROWS, FF), BF16),
         shape((ROWS, D), F32), shape((ROWS, 128), F32),
     ]
     scratch = [pltpu.VMEM(w, BF16) for w in WEIGHTS] + [
@@ -522,7 +576,7 @@
         outs += [shape((16, D), F32)] + [shape(w, BF16) for w in WEIGHTS]
         scratch += [
             pltpu.VMEM((8, 16, 128), BF16), pltpu.VMEM((16, D), F32),
-            dma((3, 3)), dma((3, 3)), dma((3, 9)), dma((3, 9)), dma((3, 4)), dma((3, 4)), dma((7,)), dma((7,)),
+            dma((6, 3)), dma((6, 3)), dma((6, 9)), dma((6, 9)), dma((6, 4)), dma((6, 4)), dma((7,)), dma((7,)),
         ]
         params = pltpu.CompilerParams(vmem_limit_bytes=VMEM_LIMIT, collective_id=1, has_side_effects=True)
     else:
@@ -541,142 +595,231 @@
 
 class Reduce:
     def __init__(self, refs, sems):
-        self.g, (self.cr1, self.cr2, self.xr0, self.xr, self.zr0, self.zr, self.tt, self.yr, self.res) = refs
+        self.g, more = refs
+        self.cr1, self.cr2, self.xr0, self.xr3, self.xr1, self.xr2, self.zr0, self.zr3, self.zr1, self.zr2 = more[:10]
+        self.tt, self.yr, self.res = (more[10], more[11]), (more[12], more[13]), more[14]
         self.cs, self.cr, self.credit, self.xs, self.xd, self.zs, self.zd, self.ys, self.yd, self.as_, self.ad = sems
         self.r, self.z, self.c = places()
         self.f = 2 * self.z + self.c
-        x, y = self.r % 2, self.r // 2
-        self.keep, self.give = (x, 2 + y), (1 - x, 3 - y)
-
-    def block(self, t, q, z):
-        return block_of(self.g, t, q, z, self.c)
+        self.side = (self.r % 2, self.r // 2)
+
+
+    def part(self, u, r, z):
+        rows, cols = quarter(u, r, self.c)
+        return self.g[0].at[matrices(u), z, rows, cols]
+
+    def core0(self, u):
+        src = self.g[0].at[matrices(u), ALL, ds((1 - self.c) * 96, 96), columns(u)]
+        dst = self.cr1.at[matrices(u), ALL, :, columns(u)]
+        return remote(src, dst, self.cs.at[0, u], self.cr.at[0, u], (self.r, 2 * self.z + 1 - self.c))
+
+    def across0(self, u, m):
+        to = hop(self.r, m + 1)
+        dst = self.xr3.at[m] if isinstance(u, int) and u == PIECES else self.xr0.at[u, m]
+        return remote(self.part(u, to, ALL), dst, self.xs.at[0, 3 * u + m], self.xd.at[0, 3 * u + m], (to, self.f))
+
+    def along0(self, u, k):
+        to = hop(self.z, k + 1)
+        dst = self.zr3.at[k] if isinstance(u, int) and u == PIECES else self.zr0.at[u, k]
+        device = (self.r, 2 * to + self.c)
+        return remote(self.part(u, self.r, to), dst, self.zs.at[0, 3 * u + k], self.zd.at[0, 3 * u + k], device)
+
+    def result(self, u, r):
+        rows, cols = quarter(u, r, 0)
+        return self.res.at[0, matrices(u), rows, cols]
+
+    def spread0(self, u, m, come=False):
+        far = hop(self.r, m + 1)
+        ref = self.result(u, far if come else self.r)
+        return remote(ref, ref, self.as_.at[0, 3 * u + m], self.ad.at[0, 3 * u + m], (far, self.f))
+
+    def start0(self, u):
+        self.core0(u).start()
+
+    def cores0(self, u):
+        self.core0(u).wait_recv()
+
+        def add(i, carry):
+            rows = ds(self.c * 96, 96)
+            total = self.g[0][matrices(u), i, rows, columns(u)].astype(F32)
+            total = total + self.cr1[matrices(u), i, :, columns(u)].astype(F32)
+            self.g[0][matrices(u), i, rows, columns(u)] = total.astype(BF16)
+            return carry
+
+        lax.fori_loop(0, 4, add, 0)
+        for m in range(3):
+            self.across0(u, m).start()
+
+    def replicas0(self, u):
+        last = isinstance(u, int) and u == PIECES
+        ref = self.part(u, self.r, ALL)
+        total = ref[...].astype(F32)
+        for m in range(3):
+            self.across0(u, m).wait_recv()
+            total = total + (self.xr3[m] if last else self.xr0[u, m]).astype(F32)
+        ref[...] = total.astype(BF16)
+        for k in range(3):
+            self.along0(u, k).start()
+
+    def owners0(self, u):
+        last = isinstance(u, int) and u == PIECES
+        total = self.part(u, self.r, self.z)[...].astype(F32)
+        for k in range(3):
+            self.along0(u, k).wait_recv()
+            total = total + (self.zr3[k] if last else self.zr0[u, k]).astype(F32)
+        self.result(u, self.r)[...] = total.astype(BF16)
+        for m in range(3):
+            self.spread0(u, m).start()
+
+    def finish0(self, u):
+        for m in range(3):
+            self.spread0(u, m, True).wait_recv()
+
+
+    def part1(self, i, m, z, give=False):
+        side = 1 - self.side[m] if give else self.side[m]
+        rows = pl.ds(pl.multiple_of(self.c * 96 + m * 48, 48), 48)
+        return self.g[1].at[i, z, rows, ds(side * 384, 384)]
+
+    def part2(self, m, z, give=False):
+        side = 1 - self.side[m] if give else self.side[m]
+        return block_of(self.g, 2, 2 * m + side, z, self.c)
 
     def core(self, t, i):
         if t == 2:
             src, dst = self.g[2].at[i, ds((1 - self.c) * 384, 384), :], self.cr2.at[i]
         else:
-            src, dst = slab_of(self.g, t, i, 1 - self.c), self.cr1.at[i]
+            src, dst = block_of(self.g, 1, i, ALL, 1 - self.c), self.cr1.at[i]
         return remote(src, dst, self.cs.at[t, i], self.cr.at[t, i], (self.r, 2 * self.z + 1 - self.c))
 
-    def start_core(self, t, i):
-        self.core(t, i).start()
-
-    def across(self, t, m):
-        if t == 0:
-            to = hop(self.r, m + 1)
-            return remote(slab_of(self.g, 0, to, self.c), self.xr0.at[m], self.xs.at[0, m], self.xd.at[0, m], (to, self.f))
-        src = slab_of(self.g, t, self.give[m], self.c)
-        return remote(src, self.xr.at[t - 1, m], self.xs.at[t, m], self.xd.at[t, m], (hop(self.r, m + 1), self.f))
-
-    def along(self, t, k, m):
-        to = hop(self.z, k + 1)
-        device = (self.r, 2 * to + self.c)
-        if t == 0:
-            return remote(self.block(0, self.r, to), self.zr0.at[k], self.zs.at[0, k], self.zd.at[0, k], device)
-        at = 2 * k + m
-        src = self.block(t, self.keep[m], to)
-        return remote(src, self.zr.at[t - 1, k, m], self.zs.at[t, at], self.zd.at[t, at], device)
+    def across(self, t, i, m):
+        at, device = 2 * i + m, (hop(self.r, m + 1), self.f)
+        if t == 1:
+            src, dst = self.part1(i, m, ALL, True), self.xr1.at[m, i]
+        else:
+            src, dst = self.part2(m, i, True), self.xr2.at[m, i]
+        return remote(src, dst, self.xs.at[t, at], self.xd.at[t, at], device)
+
+    def along1(self, i, k, m, come=False):
+        far = hop(self.z, k)
+        src, dst = self.part1(i, m, far), self.zr1.at[k - 1, m, i]
+        at = 8 * (k - 1) + 2 * i + m
+        return remote(src, dst, self.zs.at[1, at], self.zd.at[1, at], (self.r, 2 * far + self.c))
+
+    def along2(self, to, m):
+        src, dst = self.part2(m, to), self.zr2.at[self.z, m]
+        return remote(
+            src, dst, self.zs.at[2, 2 * to + m], self.zd.at[2, 2 * self.z + m], (self.r, 2 * to + self.c)
+        )
+
+    def along2_come(self, back, m):
+        src, dst = self.part2(m, back), self.zr2.at[back, m]
+        return remote(src, dst, self.zs.at[2, 2 * back + m], self.zd.at[2, 2 * back + m], (self.r, 2 * back + self.c))
 
     def complete(self, t, m):
-        src, dst = self.tt.at[t - 1, m], self.yr.at[t - 1, m]
+        src, dst = self.tt[t - 1].at[m], self.yr[t - 1].at[m]
         return remote(src, dst, self.ys.at[t - 1, m], self.yd.at[t - 1, m], (hop(self.r, 2 - m), self.f))
 
+    def result_of(self, t, m, give=False):
+        side = 1 - self.side[m] if give else self.side[m]
+        if t == 1:
+            return self.res.at[1, :, m * 48 : (m + 1) * 48, ds(side * 384, 384)]
+        return self.res.at[2, 2 * m + side]
+
     def spread(self, t, m, come=False):
-        far = hop(self.r, m + 1)
-        if t == 0:
-            ref = self.res.at[0, far if come else self.r]
-        else:
-            ref = self.res.at[t, self.give[m] if come else self.keep[m]]
-        return remote(ref, ref, self.as_.at[t, m], self.ad.at[t, m], (far, self.f))
-
-    def cores(self, t):
-        for i in range(4):
-            self.core(t, i).wait_recv()
-
-        def add(i, carry):
-            if t == 2:
-                rows = ds(self.c * 384, 384)
-                total = self.g[2][i, rows, :].astype(F32) + self.cr2[i].astype(F32)
-                self.g[2][i, rows, :] = total.astype(BF16)
+        ref = self.result_of(t, m, come)
+        return remote(ref, ref, self.as_.at[t, m], self.ad.at[t, m], (hop(self.r, m + 1), self.f))
+
+    def start(self, i):
+        self.core(2, i).start()
+        self.core(1, i).start()
+
+    def cores(self, i):
+        rows = ds(self.c * 384, 384)
+        self.core(2, i).wait_recv()
+        self.g[2][i, rows, :] = (self.g[2][i, rows, :].astype(F32) + self.cr2[i].astype(F32)).astype(BF16)
+        for m in range(2):
+            self.across(2, i, m).start()
+        rows = ds(self.c * 96, 96)
+        self.core(1, i).wait_recv()
+        self.g[1][i, :, rows, :] = (self.g[1][i, :, rows, :].astype(F32) + self.cr1[i].astype(F32)).astype(BF16)
+        for m in range(2):
+            self.across(1, i, m).start()
+
+    def allow0(self):
+        pl.semaphore_signal(
+            self.credit, inc=1, device_id=(self.r, 2 * self.z + 1 - self.c), device_id_type=pl.DeviceIdType.MESH
+        )
+
+    def replicas(self, i):
+        for m in range(2):
+            self.across(2, i, m).wait_recv()
+            ref = self.part2(m, i)
+            ref[...] = (ref[...].astype(F32) + self.xr2[m, i].astype(F32)).astype(BF16)
+
+            @pl.when(self.z != i)
+            def _(m=m):
+                self.along2(i, m).start()
+
+        for m in range(2):
+            self.across(1, i, m).wait_recv()
+            ref = self.part1(i, m, ALL)
+            ref[...] = (ref[...].astype(F32) + self.xr1[m, i].astype(F32)).astype(BF16)
+            for k in (1, 2, 3):
+                self.along1(i, k, m).start()
+
+    def owners(self, t):
+        for m in range(2):
+            if t == 1:
+                for i in range(4):
+                    total = self.part1(i, m, self.z)[...].astype(F32)
+                    for k in (1, 2, 3):
+                        self.along1(i, k, m).wait_recv()
+                        total = total + self.zr1[k - 1, m, i].astype(F32)
+                    self.tt[0][m, i] = total.astype(BF16)
             else:
-                rows = ds(self.c * 96, 96)
-                total = self.g[t][i, :, rows, :].astype(F32) + self.cr1[i].astype(F32)
-                self.g[t][i, :, rows, :] = total.astype(BF16)
-            return carry
-
-        lax.fori_loop(0, 4, add, 0)
-        if t == 1:
-            pl.semaphore_signal(
-                self.credit, inc=1, device_id=(self.r, 2 * self.z + 1 - self.c), device_id_type=pl.DeviceIdType.MESH
-            )
-        for m in range(3 if t == 0 else 2):
-            self.across(t, m).start()
-
-    def replicas(self, t):
-        for m in range(3 if t == 0 else 2):
-            self.across(t, m).wait_recv()
-
-        def add(i, carry):
-            if t == 0:
-                ref = self.block(0, self.r, i)
-                total = ref[...].astype(F32)
-                for m in range(3):
-                    total = total + self.xr0[m, i].astype(F32)
-                ref[...] = total.astype(BF16)
-            else:
-                for m in range(2):
-                    ref = self.block(t, self.keep[m], i)
-                    ref[...] = (ref[...].astype(F32) + self.xr[t - 1, m, i].astype(F32)).astype(BF16)
-            return carry
-
-        lax.fori_loop(0, 4, add, 0)
-        for k in range(3):
-            for m in range(1 if t == 0 else 2):
-                self.along(t, k, m).start()
-
-    def owners(self, t):
-        for k in range(3):
-            for m in range(1 if t == 0 else 2):
-                self.along(t, k, m).wait_recv()
-        if t == 0:
-            total = self.block(0, self.r, self.z)[...].astype(F32)
-            for k in range(3):
-                total = total + self.zr0[k].astype(F32)
-            self.res[0, self.r] = total.astype(BF16)
-            for m in range(3):
-                self.spread(0, m).start()
-            return
-        for m in range(2):
-            total = self.block(t, self.keep[m], self.z)[...].astype(F32)
-            for k in range(3):
-                total = total + self.zr[t - 1, k, m].astype(F32)
-            self.tt[t - 1, m] = total.astype(BF16)
+                total = self.part2(m, self.z)[...].astype(F32)
+                for k in (1, 2, 3):
+                    back = hop(self.z, k)
+                    self.along2_come(back, m).wait_recv()
+                    total = total + self.zr2[back, m].astype(F32)
+                self.tt[1][m] = total.astype(BF16)
             self.complete(t, m).start()
 
     def ends(self, t):
         for m in range(2):
             self.complete(t, m).wait_recv()
-            total = self.tt[t - 1, m].astype(F32) + self.yr[t - 1, m].astype(F32)
-            self.res[t, self.keep[m]] = total.astype(BF16)
+            total = self.tt[t - 1][m].astype(F32) + self.yr[t - 1][m].astype(F32)
+            self.result_of(t, m)[...] = total.astype(BF16)
             self.spread(t, m).start()
 
     def finish(self, t):
-        for m in range(3 if t == 0 else 2):
+        for m in range(2):
             self.spread(t, m, True).wait_recv()
 
     def drain(self):
-        for t in range(3):
+        def sent(u):
+            self.core0(u).wait_send()
+            for m in range(3):
+                self.across0(u, m).wait_send()
+                self.along0(u, m).wait_send()
+                self.spread0(u, m).wait_send()
+
+        lax.fori_loop(0, PIECES, lambda u, carry: (sent(u), carry)[1], 0)
+        sent(PIECES)
+        for m in range(2):
+            for t in (1, 2):
+                for i in range(4):
+                    self.across(t, i, m).wait_send()
+                self.complete(t, m).wait_send()
+                self.spread(t, m).wait_send()
+            for k in (1, 2, 3):
+                self.along2(hop(self.z, k), m).wait_send()
+                for i in range(4):
+                    self.along1(i, k, m).wait_send()
+        for t in (1, 2):
             for i in range(4):
                 self.core(t, i).wait_send()
-            for m in range(3 if t == 0 else 2):
-                self.across(t, m).wait_send()
-                self.spread(t, m).wait_send()
-            for k in range(3):
-                for m in range(1 if t == 0 else 2):
-                    self.along(t, k, m).wait_send()
-            if t:
-                for m in range(2):
-                    self.complete(t, m).wait_send()
 
 
 class SmallReduce:
@@ -763,10 +906,11 @@
 
 
 BACK_NETWORK = {
-    1: (("replicas", 2),),
-    3: (("replicas", 1),),
-    4: (("owners", 2),),
-    5: (("ends", 2),),
+    (0, 0): (("replicas", 3),),
+    (0, 1): (("replicas0", 3),),
+    (1, 1): (("cores0", 0), ("owners", 2)),
+    (2, 0): (("replicas0", 0), ("owners0", 3)),
+    (2, 1): (("cores0", 1), ("ends", 2)),
 }
 
 
@@ -783,15 +927,15 @@
     ctx_s, g_s, dctx_s, tr_s, l_sem, t_sem = take(6)
     ga_s, gi_s, go_s = grads = take(3)
     if linked:
-        gvec_ref, *more = take(10)
+        gvec_ref, *more = take(16)
         sum_refs = take(3)
         sems = take(11)
         sum_sems = take(4)
-        net = Reduce((grads, more[:9]), sems)
+        net = Reduce((grads, more), sems)
         sums = SmallReduce(sum_refs, sum_sems)
         r, z, c = places()
         f = 2 * z + c
-        res_s = more[8]
+        res_s = more[-1]
     cload = pltpu.make_async_copy(ctx_h, ctx_s, l_sem.at[1])
     cload.start()
     gvec_ref[...] = jnp.zeros_like(gvec_ref)
@@ -811,8 +955,8 @@
 
         def fetch(t, slot):
             return (
-                pltpu.make_async_copy(act_h.at[t], act_s.at[slot], t_sem.at[slot]),
-                pltpu.make_async_copy(slope_h.at[t], slope_s.at[slot], t_sem.at[2 + slot]),
+                pltpu.make_async_copy(act_h.at[:, ds(t * TILE, TILE)], act_s.at[slot], t_sem.at[slot]),
+                pltpu.make_async_copy(slope_h.at[:, ds(t * TILE, TILE)], slope_s.at[slot], t_sem.at[2 + slot]),
                 pltpu.make_async_copy(wi_h.at[t // 3, :, :, ds((t % 3) * TILE, TILE)], wi_s.at[slot], t_sem.at[4 + slot]),
                 pltpu.make_async_copy(wo_h.at[t // 3, ds((t % 3) * TILE, TILE), :], wo_s.at[slot], t_sem.at[6 + slot]),
             )
@@ -861,6 +1005,15 @@
                 for copy in fetch(t + 1, 1 - slot):
                     copy.start()
 
+            if linked:
+                @pl.when((t % 3 == 1) & (t >= 4))
+                def _():
+                    net.cores(t // 3 - 1)
+
+                @pl.when((t % 3 == 1) & (t >= 7))
+                def _():
+                    net.replicas(t // 3 - 2)
+
             db = db_s[...]
             di = (mm_nt(db, wo_s[slot]) * slope_s[slot].astype(F32)).astype(BF16)
             i, part = t // 3, ds((t % 3) * TILE, TILE)
@@ -872,16 +1025,11 @@
             if linked:
                 @pl.when(t % 3 == 2)
                 def _():
-                    net.start_core(2, i)
-                    net.start_core(1, i)
+                    net.start(i)
 
             return carry
 
         lax.fori_loop(0, TILES, step, 0)
-        if linked:
-            net.cores(2)
-            net.cores(1)
-
         n1load.wait()
         i1load.wait()
 
@@ -901,13 +1049,19 @@
         lax.fori_loop(0, ROWS // 128, first, 0)
         wload.wait()
         cload.wait()
+        if linked:
+            net.cores(3)
+            net.allow0()
+            net.replicas(2)
         tr_s[...] = ctx_s[...].T
         ga_s[3] = mm(tr_s[...], db_s[...]).astype(BF16).reshape(4, 192, D)
         if linked:
             pl.semaphore_wait(net.credit, 1)
-            net.start_core(0, 3)
+            net.start0(PIECES)
         for j in range(4):
             dctx_s[j * 256 : (j + 1) * 256, :] = mm_nt(db_s[j * 256 : (j + 1) * 256, :], wt_s[...].reshape(D, D)).astype(BF16)
+        if linked:
+            net.cores0(PIECES)
         for copy in xyloads:
             copy.wait()
         tr_s[...] = nl_s[...].T
@@ -926,7 +1080,7 @@
         pltpu.VMEM(WEIGHTS[0][1:], BF16),
     )
 
-    def attention(q_s, k_s, v_s, p_s, dq_s, dkt_s, dvt_s, far_s, bt_s, wa_s):
+    def attention(q_s, k_s, v_s, p_s, dq_s, dk_s, dv_s, dkt_s, dvt_s, far_s, bt_s, wa_s):
         wload = pltpu.make_async_copy(wa_h.at[0:3], wa_s, l_sem.at[0])
         wload.start()
         loads = [(q_h, q_s), (k_h, k_s), (v_h, v_s)]
@@ -941,22 +1095,35 @@
         for copy in loads:
             copy.wait()
 
-        def step(hp, carry):
-            slot = hp % 2
-            fetch(hp, slot).wait()
-
-            @pl.when(hp + 1 < PAIRS)
-            def _():
-                fetch(hp + 1, 1 - slot).start()
-
+        def hooks(p, part):
+            for (at, when), moves in BACK_NETWORK.items():
+                if when == part:
+                    @pl.when(p == at)
+                    def _(moves=moves):
+                        for name, u in moves:
+                            getattr(net, name)(u)
+
+        def step(p, carry):
+            for part in range(2):
+                hp = 2 * p + part
+                if part == 0:
+                    fetch(hp + 1, 1).start()
+                else:
+                    @pl.when(p + 1 < PIECES)
+                    def _():
+                        fetch(hp + 1, 0).start()
+
+                if linked:
+                    hooks(p, part)
+                fetch(hp, part).wait()
+                attend_back(hp, part)
+            cols = ds(p * 256, 256)
+            dk_s[:, cols] = dkt_s[cols, :].T
+            dv_s[:, cols] = dvt_s[cols, :].T
+            for w, left, grad in ((1, slice(0, SEQ), dk_s), (2, slice(0, SEQ), dv_s), (0, slice(0, ROWS), dq_s)):
+                ga_s[w, :, :, cols] = mm(tr_s[:, left], grad[:, cols]).astype(BF16).reshape(4, 192, 256)
             if linked:
-                for at, moves in BACK_NETWORK.items():
-                    @pl.when(hp == at)
-                    def _(moves=moves):
-                        for name, t in moves:
-                            getattr(net, name)(t)
-
-            attend_back(hp, slot)
+                net.start0(p)
             return carry
 
         def attend_back(hp, slot):
@@ -1014,14 +1181,7 @@
 
         bt_s[...] = jnp.zeros_like(bt_s)
         far_s[...] = jnp.zeros_like(far_s)
-        lax.fori_loop(0, PAIRS, step, 0)
-
-        dk = dkt_s[...].T
-        dv = dvt_s[...].T
-        for w, left, grad in ((1, slice(0, SEQ), dk), (2, slice(0, SEQ), dv), (0, slice(0, ROWS), dq_s[...])):
-            ga_s[w] = mm(tr_s[:, left], grad).astype(BF16).reshape(4, 192, D)
-            if linked:
-                net.start_core(0, w)
+        lax.fori_loop(0, PIECES, step, 0)
 
         offset = lax.broadcasted_iota(jnp.int32, (512, 128), 0) - 256
         bucket = lax.broadcasted_iota(jnp.int32, (512, 128), 1)
@@ -1033,16 +1193,24 @@
             + jnp.where(lane == 31, jnp.sum(far_s[:, 128:256], axis=1, keepdims=True), 0.0)
         )
         add_vec(0, dq_s[...].astype(F32))
-        add_vec(1, dv.astype(F32))
+        add_vec(1, dv_s[...].astype(F32))
         if linked:
-            net.cores(0)
+            net.cores0(2)
             sums.start(gvec_ref, table)
-            net.owners(1)
+            net.replicas0(1)
+            net.owners0(0)
         else:
             gtab_ref[...] = table
 
         wload.wait()
-        g_s[0:SEQ, :] += mm_nt(dq_s[0:SEQ, :], square(wa_s, 0)) + mm_nt(dk, square(wa_s, 1)) + mm_nt(dv, square(wa_s, 2))
+        g_s[0:SEQ, :] += mm_nt(dq_s[0:SEQ, :], square(wa_s, 0))
+        g_s[0:SEQ, :] += mm_nt(dk_s[...], square(wa_s, 1))
+        if linked:
+            net.replicas0(2)
+            net.owners0(1)
+            net.owners(1)
+            sums.middle()
+        g_s[0:SEQ, :] += mm_nt(dv_s[...], square(wa_s, 2))
         g_s[SEQ:, :] += mm_nt(dq_s[SEQ:, :], square(wa_s, 0))
         outs = [
             pltpu.make_async_copy(g_s.at[s * SEQ : (s + 1) * SEQ, :], ref, l_sem.at[2 + s])
@@ -1051,16 +1219,15 @@
         for copy in outs:
             copy.start()
         if linked:
-            sums.middle()
-            net.replicas(0)
             net.ends(1)
+            net.owners0(2)
             net.finish(2)
             net.finish(1)
             small_ref[...] = sums.finish()
             res_ref[1] = res_s[1]
             res_ref[2] = res_s[2]
-            net.owners(0)
-            net.finish(0)
+            for u in range(PIECES + 1):
+                net.finish0(u)
             res_ref[0] = res_s[0]
             net.drain()
             sums.drain()
@@ -1080,6 +1247,8 @@
         pltpu.VMEM((PAIRS, SEQ, 128), BF16),
         pltpu.VMEM((2, 2, 2, SEQ, SEQ), BF16),
         pltpu.VMEM((ROWS, D), BF16),
+        pltpu.VMEM((SEQ, D), BF16),
+        pltpu.VMEM((SEQ, D), BF16),
         pltpu.VMEM((D, SEQ), BF16),
         pltpu.VMEM((D, SEQ), BF16),
         pltpu.VMEM((16, 256), F32),
@@ -1105,14 +1274,15 @@
         scratch += [pltpu.VMEM((16, D), F32)] + [
             pltpu.VMEM(s, BF16)
             for s in (
-                (4, 4, 96, D), (4, 384, D), (3, 4, 96, D), (2, 2, 4, 96, D), (3, 96, D), (2, 3, 2, 96, D), (2, 2, 96, D),
-                (2, 2, 96, D), (3, 4, 96, D),
+                (4, 4, 96, D), (4, 384, D), (3, 3, 3, 4, 48, 128), (3, 4, 48, 384), (2, 4, 4, 48, 384), (2, 4, 96, D),
+                (3, 3, 3, 48, 128), (3, 48, 384), (3, 2, 4, 48, 384), (4, 2, 96, D), (2, 4, 48, 384), (2, 96, D),
+                (2, 4, 48, 384), (2, 96, D), (3, 4, 96, D),
             )
         ]
         scratch += [pltpu.VMEM((n, 16, 128), F32) for n in (8, 8, 4)]
         scratch += [
-            dma((3, 4)), dma((3, 4)), pltpu.SemaphoreType.REGULAR, dma((3, 3)), dma((3, 3)), dma((3, 6)), dma((3, 6)),
-            dma((2, 2)), dma((2, 2)), dma((3, 3)), dma((3, 3)), dma((7,)), dma((7,)), dma((3,)), dma((3,)),
+            dma((3, 4)), dma((3, 4)), pltpu.SemaphoreType.REGULAR, dma((3, 12)), dma((3, 12)), dma((3, 24)), dma((3, 24)),
+            dma((2, 2)), dma((2, 2)), dma((3, 12)), dma((3, 12)), dma((7,)), dma((7,)), dma((3,)), dma((3,)),
         ]
         params = pltpu.CompilerParams(vmem_limit_bytes=VMEM_LIMIT, collective_id=2, has_side_effects=True)
     else:

time: 293 us -> 230 us (0.78)
  Pallas kernels: 273 us -> 211 us
    pallas_call x1, Pallas kernels: 129 us -> 90.9 us  [call_forward(): pl.pallas_call(functools.partial(forward_kernel, linked), out_shape=outs,...]
    pallas_call x1, Pallas kernels: 144 us -> 120 us  [call_backward(): pl.pallas_call(functools.partial(backward_kernel, linked), out_shape=outs...]
where the time goes in v4:
time: 230 us; the launch traced here: 229 us
  Pallas kernels  211 us (92%)
  local copies, waits for them, and re-layouts  15.2 us (7%)
    pallas_call x1, Pallas kernels, call_backward(): pl.pallas_call(functools.partial(backward_kernel, linked), out_shape=outs...  120 us
    pallas_call x1, Pallas kernels, call_forward(): pl.pallas_call(functools.partial(forward_kernel, linked), out_shape=outs,...  90.9 us
    unnamed x15, local copies, waits for them, and re-layouts  5.21 us

profile of v4, /device:TPU:0, one launch (start us, length us, event | category | flops | bytes accessed | tf_op | source)
XLA Modules:
  0.0 228.9 jit_solution(10636348629837481333)
XLA Ops:
  1.3 0.7 pad_bitcast_fusion
  2.0 0.1 pad.13.clone
  2.0 0.8 stack.35
  2.8 1.3 fusion.3.refs_4_
  4.2 90.9 %forward.1 = (bf16[512,768]{1,0:T(8,128)(2,1)}, bf16[512,768]{1,0:T(8,128)(2,1)}, bf16[2,6,512,128]{3,2,1,0:T(8,128)(2,1)}, bf16[6,512,128]{2,1,0:T(8,128)(2,1)}...) custom-call(bf16[512,768]{1,0:T(8,128)(2,1)} %refs_0_.3, ...), custom_call_target="tpu_custom_call" | custom-call | tf_op jit(solution)/shard_map/forward/pallas_call | solution.py:585
  95.1 119.8 %backward.1 = (f32[512,768]{1,0:T(8,128)}, f32[512,768]{1,0:T(8,128)}, bf16[3,4,96,768]{3,2,1,0:T(8,128)(2,1)}, f32[16,128]{1,0:T(8,128)}) custom-call(bf16[512,768]{1,0:T(8,128)(2,1)} %refs_0_.3, bf16[512,768]{1,0:T(8,128)(2,1)} %refs_1_.3, bf16[512,768]{1,0:T(8,128)(2,1)} %refs_2_.2, bf16[512,768]{1,0:T(8,128)(2,1)} %refs_3_.3, ...), custom_call_target="tpu_custom_call" | custom-call | tf_op jit(solution)/shard_map/backward/pallas_call | solution.py:1292
  214.9 0.0 copy-start
  214.9 1.3 slice_bitcast_fusion.6
  216.2 1.3 slice_bitcast_fusion.5
  217.5 1.5 slice_bitcast_fusion.7
  219.0 2.2 slice.78
  221.2 0.0 copy-done
  221.2 0.3 convert_element_type.7
  221.5 0.1 slice_bitcast_fusion
  221.6 1.0 slice_bitcast_fusion.1
  222.6 0.0 copy-start.4
  222.6 0.0 copy-start.3
  222.6 1.1 copy.43
  223.8 0.0 copy-start.2
  223.8 0.2 copy-done.4
  224.0 0.9 copy.49
  224.9 0.0 copy-done.3
  224.9 0.9 copy.50
  225.8 0.0 copy-done.2
  225.8 0.0 copy-start.1
  225.8 1.1 copy.51
  226.9 0.8 copy-done.1
  227.8 1.1 copy.52
  (1 shorter events, 0.0 us)
Async XLA Ops:
  214.9 6.3 %copy-start = (bf16[3,4,96,768]{3,2,1,0:T(8,128)(2,1)S(1)}, bf16[3,4,96,768]{3,2,1,0:T(8,128)(2,1)}, u32[]{:S(2)}) copy-start(bf16[3,4,96,768]{3,2,1,0:T(8,128)(2,1)} %get-tuple-element.62) | copy-start | bytes 5308420
  222.6 1.4 copy-start.4
  222.6 2.2 copy-start.3
  223.8 2.0 copy-start.2
  225.8 2.0 copy-start.1

commit v5 on v4

--- a/solution.py
+++ b/solution.py
@@ -596,230 +596,190 @@
 class Reduce:
     def __init__(self, refs, sems):
         self.g, more = refs
-        self.cr1, self.cr2, self.xr0, self.xr3, self.xr1, self.xr2, self.zr0, self.zr3, self.zr1, self.zr2 = more[:10]
-        self.tt, self.yr, self.res = (more[10], more[11]), (more[12], more[13]), more[14]
+        self.cr1, self.cr2, *more, self.res = more
+        self.big, self.cut, self.out = more[:5], more[5:10], more[10:]
         self.cs, self.cr, self.credit, self.xs, self.xd, self.zs, self.zd, self.ys, self.yd, self.as_, self.ad = sems
         self.r, self.z, self.c = places()
         self.f = 2 * self.z + self.c
         self.side = (self.r % 2, self.r // 2)
 
-
-    def part(self, u, r, z):
-        rows, cols = quarter(u, r, self.c)
-        return self.g[0].at[matrices(u), z, rows, cols]
-
-    def core0(self, u):
-        src = self.g[0].at[matrices(u), ALL, ds((1 - self.c) * 96, 96), columns(u)]
-        dst = self.cr1.at[matrices(u), ALL, :, columns(u)]
-        return remote(src, dst, self.cs.at[0, u], self.cr.at[0, u], (self.r, 2 * self.z + 1 - self.c))
-
-    def across0(self, u, m):
-        to = hop(self.r, m + 1)
-        dst = self.xr3.at[m] if isinstance(u, int) and u == PIECES else self.xr0.at[u, m]
-        return remote(self.part(u, to, ALL), dst, self.xs.at[0, 3 * u + m], self.xd.at[0, 3 * u + m], (to, self.f))
-
-    def along0(self, u, k):
-        to = hop(self.z, k + 1)
-        dst = self.zr3.at[k] if isinstance(u, int) and u == PIECES else self.zr0.at[u, k]
-        device = (self.r, 2 * to + self.c)
-        return remote(self.part(u, self.r, to), dst, self.zs.at[0, 3 * u + k], self.zd.at[0, 3 * u + k], device)
-
-    def result(self, u, r):
-        rows, cols = quarter(u, r, 0)
-        return self.res.at[0, matrices(u), rows, cols]
-
-    def spread0(self, u, m, come=False):
-        far = hop(self.r, m + 1)
-        ref = self.result(u, far if come else self.r)
-        return remote(ref, ref, self.as_.at[0, 3 * u + m], self.ad.at[0, 3 * u + m], (far, self.f))
-
-    def start0(self, u):
-        self.core0(u).start()
-
-    def cores0(self, u):
-        self.core0(u).wait_recv()
-
-        def add(i, carry):
-            rows = ds(self.c * 96, 96)
-            total = self.g[0][matrices(u), i, rows, columns(u)].astype(F32)
-            total = total + self.cr1[matrices(u), i, :, columns(u)].astype(F32)
-            self.g[0][matrices(u), i, rows, columns(u)] = total.astype(BF16)
-            return carry
-
-        lax.fori_loop(0, 4, add, 0)
-        for m in range(3):
-            self.across0(u, m).start()
-
-    def replicas0(self, u):
-        last = isinstance(u, int) and u == PIECES
-        ref = self.part(u, self.r, ALL)
-        total = ref[...].astype(F32)
-        for m in range(3):
-            self.across0(u, m).wait_recv()
-            total = total + (self.xr3[m] if last else self.xr0[u, m]).astype(F32)
-        ref[...] = total.astype(BF16)
-        for k in range(3):
-            self.along0(u, k).start()
-
-    def owners0(self, u):
-        last = isinstance(u, int) and u == PIECES
-        total = self.part(u, self.r, self.z)[...].astype(F32)
-        for k in range(3):
-            self.along0(u, k).wait_recv()
-            total = total + (self.zr3[k] if last else self.zr0[u, k]).astype(F32)
-        self.result(u, self.r)[...] = total.astype(BF16)
-        for m in range(3):
-            self.spread0(u, m).start()
-
-    def finish0(self, u):
-        for m in range(3):
-            self.spread0(u, m, True).wait_recv()
-
-
-    def part1(self, i, m, z, give=False):
+    def number(self, kind, i):
+        return {"in": 0, "square": 4, "piece": 5, "out": 8}[kind] + i
+
+    def columns(self, kind, i, side):
+        return pl.ds(pl.multiple_of(i * 256 + side * 128, 128), 128) if kind == "piece" else ds(side * 384, 384)
+
+    def half(self, kind, i, m, z, give=False):
         side = 1 - self.side[m] if give else self.side[m]
+        if kind == "out":
+            return block_of(self.g, 2, 2 * m + side, i, self.c)
         rows = pl.ds(pl.multiple_of(self.c * 96 + m * 48, 48), 48)
-        return self.g[1].at[i, z, rows, ds(side * 384, 384)]
-
-    def part2(self, m, z, give=False):
+        cols = self.columns(kind, i, side)
+        if kind == "in":
+            return self.g[1].at[i, z, rows, cols]
+        return self.g[0].at[3 if kind == "square" else slice(0, 3), z, rows, cols]
+
+    def held(self, what, kind, i, m):
+        if kind == "out":
+            return self.out[what].at[m, i] if what == 0 else self.out[what].at[m, i // 2] if what == 1 else self.out[what].at[m]
+        return self.cut[what].at[m, i] if kind == "piece" else self.big[what].at[m, 4 if kind == "square" else i]
+
+    def mine(self, kind, i):
+        rows, cols = ds(self.c * 96, 96), ds(i * 256, 256)
+        if kind == "out":
+            return self.g[2].at[i, ds(self.c * 384, 384), :], self.cr2.at[i]
+        if kind == "in":
+            return self.g[1].at[i, :, rows, :], self.cr1.at[i]
+        if kind == "square":
+            return self.g[0].at[3, :, rows, :], self.cr1.at[3]
+        return self.g[0].at[0:3, :, rows, cols], self.cr1.at[0:3, :, :, cols]
+
+    def core(self, kind, i):
+        rows, cols = ds((1 - self.c) * 96, 96), ds(i * 256, 256)
+        if kind == "out":
+            src = self.g[2].at[i, ds((1 - self.c) * 384, 384), :]
+        elif kind == "in":
+            src = self.g[1].at[i, :, rows, :]
+        elif kind == "square":
+            src = self.g[0].at[3, :, rows, :]
+        else:
+            src = self.g[0].at[0:3, :, rows, cols]
+        n = self.number(kind, i)
+        return remote(src, self.mine(kind, i)[1], self.cs.at[n], self.cr.at[n], (self.r, 2 * self.z + 1 - self.c))
+
+    def across(self, kind, i, m):
+        n = 2 * self.number(kind, i) + m
+        src, dst = self.half(kind, i, m, ALL, True), self.held(0, kind, i, m)
+        return remote(src, dst, self.xs.at[n], self.xd.at[n], (hop(self.r, m + 1), self.f))
+
+    def near(self, kind, i, m, j=0):
+        to, n = hop(self.z, 1), 4 * self.number(kind, i) + 2 * m + j
+        src, dst = self.half(kind, i, m, hop(self.z, 3) if j else to), self.held(1, kind, i, m)
+        return remote(
+            src, dst if kind == "out" else dst.at[j], self.zs.at[n], self.zd.at[n], (self.r, 2 * to + self.c)
+        )
+
+    def far(self, kind, i, m):
+        to = hop(self.z, 2)
+        if kind == "out":
+            i, n = to, 64 + m
+        else:
+            n = 48 + 2 * self.number(kind, i) + m
+        src, dst = self.half(kind, i, m, to), self.held(2, kind, i, m)
+        return remote(src, dst, self.zs.at[n], self.zd.at[n], (self.r, 2 * to + self.c))
+
+    def complete(self, kind, i, m):
+        n = 2 * (8 if kind == "out" else self.number(kind, i)) + m
+        src, dst = self.held(3, kind, i, m), self.held(4, kind, i, m)
+        return remote(src, dst, self.ys.at[n], self.yd.at[n], (hop(self.r, 2 - m), self.f))
+
+    def result(self, kind, i, m, give=False):
         side = 1 - self.side[m] if give else self.side[m]
-        return block_of(self.g, 2, 2 * m + side, z, self.c)
-
-    def core(self, t, i):
-        if t == 2:
-            src, dst = self.g[2].at[i, ds((1 - self.c) * 384, 384), :], self.cr2.at[i]
-        else:
-            src, dst = block_of(self.g, 1, i, ALL, 1 - self.c), self.cr1.at[i]
-        return remote(src, dst, self.cs.at[t, i], self.cr.at[t, i], (self.r, 2 * self.z + 1 - self.c))
-
-    def across(self, t, i, m):
-        at, device = 2 * i + m, (hop(self.r, m + 1), self.f)
-        if t == 1:
-            src, dst = self.part1(i, m, ALL, True), self.xr1.at[m, i]
-        else:
-            src, dst = self.part2(m, i, True), self.xr2.at[m, i]
-        return remote(src, dst, self.xs.at[t, at], self.xd.at[t, at], device)
-
-    def along1(self, i, k, m, come=False):
-        far = hop(self.z, k)
-        src, dst = self.part1(i, m, far), self.zr1.at[k - 1, m, i]
-        at = 8 * (k - 1) + 2 * i + m
-        return remote(src, dst, self.zs.at[1, at], self.zd.at[1, at], (self.r, 2 * far + self.c))
-
-    def along2(self, to, m):
-        src, dst = self.part2(m, to), self.zr2.at[self.z, m]
-        return remote(
-            src, dst, self.zs.at[2, 2 * to + m], self.zd.at[2, 2 * self.z + m], (self.r, 2 * to + self.c)
-        )
-
-    def along2_come(self, back, m):
-        src, dst = self.part2(m, back), self.zr2.at[back, m]
-        return remote(src, dst, self.zs.at[2, 2 * back + m], self.zd.at[2, 2 * back + m], (self.r, 2 * back + self.c))
-
-    def complete(self, t, m):
-        src, dst = self.tt[t - 1].at[m], self.yr[t - 1].at[m]
-        return remote(src, dst, self.ys.at[t - 1, m], self.yd.at[t - 1, m], (hop(self.r, 2 - m), self.f))
-
-    def result_of(self, t, m, give=False):
-        side = 1 - self.side[m] if give else self.side[m]
-        if t == 1:
-            return self.res.at[1, :, m * 48 : (m + 1) * 48, ds(side * 384, 384)]
-        return self.res.at[2, 2 * m + side]
-
-    def spread(self, t, m, come=False):
-        ref = self.result_of(t, m, come)
-        return remote(ref, ref, self.as_.at[t, m], self.ad.at[t, m], (hop(self.r, m + 1), self.f))
-
-    def start(self, i):
-        self.core(2, i).start()
-        self.core(1, i).start()
-
-    def cores(self, i):
-        rows = ds(self.c * 384, 384)
-        self.core(2, i).wait_recv()
-        self.g[2][i, rows, :] = (self.g[2][i, rows, :].astype(F32) + self.cr2[i].astype(F32)).astype(BF16)
+        if kind == "out":
+            return self.res.at[2, 2 * m + side]
+        rows, cols = slice(m * 48, (m + 1) * 48), self.columns(kind, i, side)
+        if kind == "in":
+            return self.res.at[1, i, rows, cols]
+        return self.res.at[0, 3 if kind == "square" else slice(0, 3), rows, cols]
+
+    def spread(self, kind, i, m, come=False):
+        n = 2 * (8 if kind == "out" else self.number(kind, i)) + m
+        ref = self.result(kind, i, m, come)
+        return remote(ref, ref, self.as_.at[n], self.ad.at[n], (hop(self.r, m + 1), self.f))
+
+    def start(self, kind, i=0):
+        self.core(kind, i).start()
+
+    def cores(self, kind, i=0):
+        self.core(kind, i).wait_recv()
+        ref, come = self.mine(kind, i)
+        ref[...] = (ref[...].astype(F32) + come[...].astype(F32)).astype(BF16)
         for m in range(2):
-            self.across(2, i, m).start()
-        rows = ds(self.c * 96, 96)
-        self.core(1, i).wait_recv()
-        self.g[1][i, :, rows, :] = (self.g[1][i, :, rows, :].astype(F32) + self.cr1[i].astype(F32)).astype(BF16)
-        for m in range(2):
-            self.across(1, i, m).start()
-
-    def allow0(self):
+            self.across(kind, i, m).start()
+
+    def allow(self):
         pl.semaphore_signal(
             self.credit, inc=1, device_id=(self.r, 2 * self.z + 1 - self.c), device_id_type=pl.DeviceIdType.MESH
         )
 
-    def replicas(self, i):
+    def replicas(self, kind, i=0):
         for m in range(2):
-            self.across(2, i, m).wait_recv()
-            ref = self.part2(m, i)
-            ref[...] = (ref[...].astype(F32) + self.xr2[m, i].astype(F32)).astype(BF16)
-
-            @pl.when(self.z != i)
-            def _(m=m):
-                self.along2(i, m).start()
-
+            self.across(kind, i, m).wait_recv()
+            ref = self.half(kind, i, m, ALL)
+            ref[...] = (ref[...].astype(F32) + self.held(0, kind, i, m)[...].astype(F32)).astype(BF16)
+            if kind == "out":
+                @pl.when((self.z + i) % 2 == 1)
+                def _(m=m):
+                    self.near(kind, i, m).start()
+            else:
+                for j in range(2):
+                    self.near(kind, i, m, j).start()
+
+    def pairs(self, kind, i=0):
+        if kind == "out":
+            @pl.when((self.z + i) % 2 == 0)
+            def _():
+                for m in range(2):
+                    self.near(kind, i, m).wait_recv()
+                    ref = self.half(kind, i, m, None)
+                    ref[...] = (ref[...].astype(F32) + self.held(1, kind, i, m)[...].astype(F32)).astype(BF16)
+
+                    @pl.when(self.z != i)
+                    def _(m=m):
+                        self.far(kind, i, m).start()
+            return
         for m in range(2):
-            self.across(1, i, m).wait_recv()
-            ref = self.part1(i, m, ALL)
-            ref[...] = (ref[...].astype(F32) + self.xr1[m, i].astype(F32)).astype(BF16)
-            for k in (1, 2, 3):
-                self.along1(i, k, m).start()
-
-    def owners(self, t):
+            for j in (1, 0):
+                self.near(kind, i, m, j).wait_recv()
+                ref = self.half(kind, i, m, hop(self.z, 2 * j))
+                ref[...] = (ref[...].astype(F32) + self.held(1, kind, i, m).at[j][...].astype(F32)).astype(BF16)
+                if j:
+                    self.far(kind, i, m).start()
+
+    def owners(self, kind, i=0):
         for m in range(2):
-            if t == 1:
-                for i in range(4):
-                    total = self.part1(i, m, self.z)[...].astype(F32)
-                    for k in (1, 2, 3):
-                        self.along1(i, k, m).wait_recv()
-                        total = total + self.zr1[k - 1, m, i].astype(F32)
-                    self.tt[0][m, i] = total.astype(BF16)
-            else:
-                total = self.part2(m, self.z)[...].astype(F32)
-                for k in (1, 2, 3):
-                    back = hop(self.z, k)
-                    self.along2_come(back, m).wait_recv()
-                    total = total + self.zr2[back, m].astype(F32)
-                self.tt[1][m] = total.astype(BF16)
-            self.complete(t, m).start()
-
-    def ends(self, t):
+            self.far(kind, i, m).wait_recv()
+            total = self.half(kind, self.z if kind == "out" else i, m, self.z)[...].astype(F32)
+            total = total + self.held(2, kind, i, m)[...].astype(F32)
+            self.held(3, kind, i, m)[...] = total.astype(BF16)
+            self.complete(kind, i, m).start()
+
+    def ends(self, kind, i=0):
         for m in range(2):
-            self.complete(t, m).wait_recv()
-            total = self.tt[t - 1][m].astype(F32) + self.yr[t - 1][m].astype(F32)
-            self.result_of(t, m)[...] = total.astype(BF16)
-            self.spread(t, m).start()
-
-    def finish(self, t):
+            self.complete(kind, i, m).wait_recv()
+            total = self.held(3, kind, i, m)[...].astype(F32) + self.held(4, kind, i, m)[...].astype(F32)
+            self.result(kind, i, m)[...] = total.astype(BF16)
+            self.spread(kind, i, m).start()
+
+    def finish(self, kind, i=0):
         for m in range(2):
-            self.spread(t, m, True).wait_recv()
+            self.spread(kind, i, m, True).wait_recv()
 
     def drain(self):
-        def sent(u):
-            self.core0(u).wait_send()
-            for m in range(3):
-                self.across0(u, m).wait_send()
-                self.along0(u, m).wait_send()
-                self.spread0(u, m).wait_send()
-
-        lax.fori_loop(0, PIECES, lambda u, carry: (sent(u), carry)[1], 0)
-        sent(PIECES)
+        def sent(kind, i):
+            self.core(kind, i).wait_send()
+            for m in range(2):
+                self.across(kind, i, m).wait_send()
+                if kind != "out":
+                    for j in range(2):
+                        self.near(kind, i, m, j).wait_send()
+                    self.far(kind, i, m).wait_send()
+                    self.complete(kind, i, m).wait_send()
+                    self.spread(kind, i, m).wait_send()
+
+        def several(kind, count):
+            lax.fori_loop(0, count, lambda i, carry: (sent(kind, i), carry)[1], 0)
+
+        several("in", 4)
+        several("out", 4)
+        several("piece", PIECES)
+        sent("square", 0)
         for m in range(2):
-            for t in (1, 2):
-                for i in range(4):
-                    self.across(t, i, m).wait_send()
-                self.complete(t, m).wait_send()
-                self.spread(t, m).wait_send()
-            for k in (1, 2, 3):
-                self.along2(hop(self.z, k), m).wait_send()
-                for i in range(4):
-                    self.along1(i, k, m).wait_send()
-        for t in (1, 2):
-            for i in range(4):
-                self.core(t, i).wait_send()
+            for i in (hop(self.z, 1), hop(self.z, 3)):
+                self.near("out", i, m).wait_send()
+            self.far("out", 0, m).wait_send()
+            self.complete("out", 0, m).wait_send()
+            self.spread("out", 0, m).wait_send()
 
 
 class SmallReduce:
@@ -906,12 +866,22 @@
 
 
 BACK_NETWORK = {
-    (0, 0): (("replicas", 3),),
-    (0, 1): (("replicas0", 3),),
-    (1, 1): (("cores0", 0), ("owners", 2)),
-    (2, 0): (("replicas0", 0), ("owners0", 3)),
-    (2, 1): (("cores0", 1), ("ends", 2)),
+    (0, 0): (("replicas", "out", 3), ("replicas", "in", 3), ),
+    (0, 1): (("pairs", "out", 2), ("pairs", "in", 2), ("replicas", "square"), ),
+    (1, 0): (),
+    (1, 1): (("cores", "piece", 0), ),
+    (2, 0): (("replicas", "piece", 0), ("pairs", "out", 3), ("pairs", "in", 3), ("pairs", "square"), ("owners", "in", 0), ("owners", "in", 1), ),
+    (2, 1): (("cores", "piece", 1), ),
 }
+
+LAST_NETWORK = (
+    (("cores", "piece", 2), ),
+    (("replicas", "piece", 1), ("pairs", "piece", 0), ("owners", "out"), ),
+    (("owners", "in", 2), ("owners", "square"), ("ends", "in", 0), ("ends", "in", 1), ),
+    (("replicas", "piece", 2), ("pairs", "piece", 1), ("owners", "in", 3), ("sum_middle",), ),
+    (("owners", "piece", 0), ("ends", "out"), ("ends", "in", 2), ("ends", "square"), ),
+    (("pairs", "piece", 2), ("owners", "piece", 1), ("ends", "in", 3), ("ends", "piece", 0), ("owners", "piece", 2), ("ends", "piece", 1), ("ends", "piece", 2), ),
+)
 
 
 def backward_kernel(linked, *refs):
@@ -927,7 +897,7 @@
     ctx_s, g_s, dctx_s, tr_s, l_sem, t_sem = take(6)
     ga_s, gi_s, go_s = grads = take(3)
     if linked:
-        gvec_ref, *more = take(16)
+        gvec_ref, *more = take(19)
         sum_refs = take(3)
         sems = take(11)
         sum_sems = take(4)
@@ -1008,11 +978,18 @@
             if linked:
                 @pl.when((t % 3 == 1) & (t >= 4))
                 def _():
-                    net.cores(t // 3 - 1)
+                    for kind in ("out", "in"):
+                        net.cores(kind, t // 3 - 1)
 
                 @pl.when((t % 3 == 1) & (t >= 7))
                 def _():
-                    net.replicas(t // 3 - 2)
+                    for kind in ("out", "in"):
+                        net.replicas(kind, t // 3 - 2)
+
+                @pl.when(t == 11)
+                def _():
+                    for kind in ("out", "in"):
+                        net.pairs(kind, 0)
 
             db = db_s[...]
             di = (mm_nt(db, wo_s[slot]) * slope_s[slot].astype(F32)).astype(BF16)
@@ -1025,7 +1002,8 @@
             if linked:
                 @pl.when(t % 3 == 2)
                 def _():
-                    net.start(i)
+                    net.start("out", i)
+                    net.start("in", i)
 
             return carry
 
@@ -1050,18 +1028,22 @@
         wload.wait()
         cload.wait()
         if linked:
-            net.cores(3)
-            net.allow0()
-            net.replicas(2)
+            for kind in ("out", "in"):
+                net.cores(kind, 3)
+            net.allow()
+            for kind in ("out", "in"):
+                net.replicas(kind, 2)
         tr_s[...] = ctx_s[...].T
         ga_s[3] = mm(tr_s[...], db_s[...]).astype(BF16).reshape(4, 192, D)
         if linked:
             pl.semaphore_wait(net.credit, 1)
-            net.start0(PIECES)
+            net.start("square")
         for j in range(4):
             dctx_s[j * 256 : (j + 1) * 256, :] = mm_nt(db_s[j * 256 : (j + 1) * 256, :], wt_s[...].reshape(D, D)).astype(BF16)
         if linked:
-            net.cores0(PIECES)
+            for kind in ("out", "in"):
+                net.pairs(kind, 1)
+            net.cores("square")
         for copy in xyloads:
             copy.wait()
         tr_s[...] = nl_s[...].T
@@ -1100,8 +1082,8 @@
                 if when == part:
                     @pl.when(p == at)
                     def _(moves=moves):
-                        for name, u in moves:
-                            getattr(net, name)(u)
+                        for name, *unit in moves:
+                            getattr(net, name)(*unit)
 
         def step(p, carry):
             for part in range(2):
@@ -1123,7 +1105,7 @@
             for w, left, grad in ((1, slice(0, SEQ), dk_s), (2, slice(0, SEQ), dv_s), (0, slice(0, ROWS), dq_s)):
                 ga_s[w, :, :, cols] = mm(tr_s[:, left], grad[:, cols]).astype(BF16).reshape(4, 192, 256)
             if linked:
-                net.start0(p)
+                net.start("piece", p)
             return carry
 
         def attend_back(hp, slot):
@@ -1194,23 +1176,25 @@
         )
         add_vec(0, dq_s[...].astype(F32))
         add_vec(1, dv_s[...].astype(F32))
+        def run(names):
+            if linked:
+                for name, *args in names:
+                    (getattr(sums, name[4:]) if name.startswith("sum_") else getattr(net, name))(*args)
+
+        run(LAST_NETWORK[0])
         if linked:
-            net.cores0(2)
             sums.start(gvec_ref, table)
-            net.replicas0(1)
-            net.owners0(0)
         else:
             gtab_ref[...] = table
 
         wload.wait()
+        run(LAST_NETWORK[1])
         g_s[0:SEQ, :] += mm_nt(dq_s[0:SEQ, :], square(wa_s, 0))
+        run(LAST_NETWORK[2])
         g_s[0:SEQ, :] += mm_nt(dk_s[...], square(wa_s, 1))
-        if linked:
-            net.replicas0(2)
-            net.owners0(1)
-            net.owners(1)
-            sums.middle()
+        run(LAST_NETWORK[3])
         g_s[0:SEQ, :] += mm_nt(dv_s[...], square(wa_s, 2))
+        run(LAST_NETWORK[4])
         g_s[SEQ:, :] += mm_nt(dq_s[SEQ:, :], square(wa_s, 0))
         outs = [
             pltpu.make_async_copy(g_s.at[s * SEQ : (s + 1) * SEQ, :], ref, l_sem.at[2 + s])
@@ -1218,16 +1202,17 @@
         ]
         for copy in outs:
             copy.start()
+        run(LAST_NETWORK[5])
         if linked:
-            net.ends(1)
-            net.owners0(2)
-            net.finish(2)
-            net.finish(1)
+            net.finish("out")
+            for i in range(4):
+                net.finish("in", i)
             small_ref[...] = sums.finish()
             res_ref[1] = res_s[1]
             res_ref[2] = res_s[2]
-            for u in range(PIECES + 1):
-                net.finish0(u)
+            net.finish("square")
+            for i in range(PIECES):
+                net.finish("piece", i)
             res_ref[0] = res_s[0]
             net.drain()
             sums.drain()
@@ -1274,15 +1259,17 @@
         scratch += [pltpu.VMEM((16, D), F32)] + [
             pltpu.VMEM(s, BF16)
             for s in (
-                (4, 4, 96, D), (4, 384, D), (3, 3, 3, 4, 48, 128), (3, 4, 48, 384), (2, 4, 4, 48, 384), (2, 4, 96, D),
-                (3, 3, 3, 48, 128), (3, 48, 384), (3, 2, 4, 48, 384), (4, 2, 96, D), (2, 4, 48, 384), (2, 96, D),
-                (2, 4, 48, 384), (2, 96, D), (3, 4, 96, D),
+                (4, 4, 96, D), (4, 384, D),
+                (2, 5, 4, 48, 384), (2, 5, 2, 48, 384), (2, 5, 48, 384), (2, 5, 48, 384), (2, 5, 48, 384),
+                (2, 3, 3, 4, 48, 128), (2, 3, 2, 3, 48, 128), (2, 3, 3, 48, 128), (2, 3, 3, 48, 128), (2, 3, 3, 48, 128),
+                (2, 4, 96, D), (2, 2, 96, D), (2, 96, D), (2, 96, D), (2, 96, D),
+                (3, 4, 96, D),
             )
         ]
         scratch += [pltpu.VMEM((n, 16, 128), F32) for n in (8, 8, 4)]
         scratch += [
-            dma((3, 4)), dma((3, 4)), pltpu.SemaphoreType.REGULAR, dma((3, 12)), dma((3, 12)), dma((3, 24)), dma((3, 24)),
-            dma((2, 2)), dma((2, 2)), dma((3, 12)), dma((3, 12)), dma((7,)), dma((7,)), dma((3,)), dma((3,)),
+            dma((12,)), dma((12,)), pltpu.SemaphoreType.REGULAR, dma((24,)), dma((24,)), dma((66,)), dma((66,)),
+            dma((18,)), dma((18,)), dma((18,)), dma((18,)), dma((7,)), dma((7,)), dma((3,)), dma((3,)),
         ]
         params = pltpu.CompilerParams(vmem_limit_bytes=VMEM_LIMIT, collective_id=2, has_side_effects=True)
     else:
@@ -1298,6 +1285,57 @@
         compiler_params=params,
         name="backward",
     )(x, y, cc, cq, vecs, wa, wi, wo, *saved)
+
+
+def finish_kernel(oc_h, oq_h, gc_h, gq_h, res_ref, small_ref, oc_o, oq_o, gc_o, gq_o, wq, wk, wv, wo, wi, wf, *rest):
+    *vectors, low_s, high_s, in_sem, out_sem = rest
+    moves = []
+    for i, (src, dst) in enumerate(((gc_h, gc_o), (gq_h, gq_o), (oc_h, oc_o), (oq_h, oq_o))):
+        held = (high_s if i < 2 else low_s).at[i % 2]
+        for part in range(2):
+            rows = slice(part * SEQ // 2, (part + 1) * SEQ // 2)
+            n = len(moves)
+            moves.append((
+                pltpu.make_async_copy(src.at[rows, :], held.at[rows, :], in_sem.at[n]),
+                pltpu.make_async_copy(held.at[rows, :], dst.at[rows, :], out_sem.at[n]),
+            ))
+    for move, _ in moves:
+        move.start()
+    small = small_ref[...]
+    for i in range(8):
+        vectors[i][...] = small[i, :96]
+    for j in range(3):
+        vectors[8][j * 128 : (j + 1) * 128] = small[8 + j]
+    vectors[9][...] = small[11, :48]
+    for q in range(4):
+        (wq, wk, wv, wo)[q][...] = res_ref[0, q].astype(F32)
+        wi[:, q * D : (q + 1) * D] = res_ref[1, q].astype(F32)
+        wf[q * 96 : (q + 1) * 96, :] = res_ref[2, q].astype(F32)
+    for move, onward in moves:
+        move.wait()
+        onward.start()
+    for _, onward in moves:
+        onward.wait()
+
+
+def call_finish(oc, oq, gc, gq, res, small):
+    hbm = pl.BlockSpec(memory_space=pl.ANY)
+    vmem = pl.BlockSpec(memory_space=pltpu.VMEM)
+    shape = jax.ShapeDtypeStruct
+    outs = [shape(a.shape, a.dtype) for a in (oc, oq, gc, gq)] + [shape((96, D), F32)] * 4
+    outs += [shape((96, FF), F32), shape((384, D), F32)]
+    outs += [shape((96,), F32)] * 8 + [shape((384,), F32), shape((48,), F32)]
+    return pl.pallas_call(
+        finish_kernel,
+        out_shape=outs,
+        in_specs=[hbm] * 4 + [vmem] * 2,
+        out_specs=[hbm] * 4 + [vmem] * 16,
+        scratch_shapes=[
+            pltpu.VMEM((2, SEQ, D), BF16), pltpu.VMEM((2, SEQ, D), F32),
+            pltpu.SemaphoreType.DMA((8,)), pltpu.SemaphoreType.DMA((8,)),
+        ],
+        name="finish",
+    )(oc, oq, gc, gq, res, small)
 
 
 def shards(
@@ -1332,12 +1370,8 @@
     streams = (content_stream, query_stream, content_cotangent, query_cotangent)
     gc, gq, *grads = call_backward(linked, *streams, vecs, wa, wi, wo, saved)
     if linked:
-        res, flat = grads
-        res = res.astype(F32)
-        ga, go = res[0], res[2].reshape(4 * width, D)
-        gi = res[1].transpose(1, 0, 2).reshape(width, FF)
-        v = [flat[i, :width] for i in range(8)]
-        inner, table = flat[8:11].reshape(4 * width), flat[11, : bucket_bias.shape[0]]
+        out_c, out_q, gc, gq, *rest = call_finish(out_c, out_q, gc, gq, *grads)
+        ga, gi, go, v, inner, table = rest[:4], rest[4], rest[5], rest[6:14], rest[14], rest[15]
     else:
         def reduce(a, axis=0):
             a = lax.psum_scatter(a, "fsdp", scatter_dimension=axis, tiled=True)

time: 230 us -> 213 us (0.926)
  local copies, waits for them, and re-layouts: 15.2 us -> 1.54 us
  Pallas kernels: 211 us -> 208 us
    pallas_call x1, Pallas kernels: 120 us -> 110 us  [call_backward(): pl.pallas_call(functools.partial(backward_kernel, linked), out_shape=outs...]
    pallas_call x0 -> x1, Pallas kernels: none -> 7.16 us  [call_finish(): pl.pallas_call(finish_kernel, out_shape=outs, in_specs=[hbm] * 4 + [vmem]...]
    unnamed x15 -> x0, local copies, waits for them, and re-layouts: 5.21 us -> none
    squeeze x3 -> x0, local copies, waits for them, and re-layouts: 3.87 us -> none  [the longest x1 1.52 us: shards(): v = [flat[i, :width] for i in range(8)]]
    reshape x2 -> x0, local copies, waits for them, and re-layouts: 2.39 us -> none  [the longest x1 1.26 us: shards(): flat[8:11].reshape(4 * width)]
where the time goes in v5:
time: 213 us; the launch traced here: 212 us
  Pallas kernels  208 us (98%)
    pallas_call x1, Pallas kernels, call_backward(): pl.pallas_call(functools.partial(backward_kernel, linked), out_shape=outs...  110 us
    pallas_call x1, Pallas kernels, call_forward(): pl.pallas_call(functools.partial(forward_kernel, linked), out_shape=outs,...  90.9 us
    pallas_call x1, Pallas kernels, call_finish(): pl.pallas_call(finish_kernel, out_shape=outs, in_specs=[hbm] * 4 + [vmem]...  7.16 us

profile of v5, /device:TPU:0, one launch (start us, length us, event | category | flops | bytes accessed | tf_op | source)
XLA Modules:
  0.0 212.2 jit_solution(1582831262420085679)
XLA Ops:
  1.3 0.7 pad_bitcast_fusion
  2.0 0.1 pad.13.clone
  2.0 0.8 stack.35
  2.8 1.3 fusion.3.refs_4_
  4.2 90.9 %forward.1 = (bf16[512,768]{1,0:T(8,128)(2,1)}, bf16[512,768]{1,0:T(8,128)(2,1)}, bf16[2,6,512,128]{3,2,1,0:T(8,128)(2,1)}, bf16[6,512,128]{2,1,0:T(8,128)(2,1)}...) custom-call(bf16[512,768]{1,0:T(8,128)(2,1)} %refs_0_.3, ...), custom_call_target="tpu_custom_call" | custom-call | tf_op jit(solution)/shard_map/forward/pallas_call | solution.py:585
  95.1 109.8 %backward.1 = (f32[512,768]{1,0:T(8,128)}, f32[512,768]{1,0:T(8,128)}, bf16[3,4,96,768]{3,2,1,0:T(8,128)(2,1)}, f32[16,128]{1,0:T(8,128)}) custom-call(bf16[512,768]{1,0:T(8,128)(2,1)} %refs_0_.3, bf16[512,768]{1,0:T(8,128)(2,1)} %refs_1_.3, bf16[512,768]{1,0:T(8,128)(2,1)} %refs_2_.2, bf16[512,768]{1,0:T(8,128)(2,1)} %refs_3_.3, ...), custom_call_target="tpu_custom_call" | custom-call | tf_op jit(solution)/shard_map/backward/pallas_call | solution.py:1279
  204.9 7.2 %finish.1 = (bf16[512,768]{1,0:T(8,128)(2,1)}, bf16[512,768]{1,0:T(8,128)(2,1)}, f32[512,768]{1,0:T(8,128)}, f32[512,768]{1,0:T(8,128)}, f32[96,768]{1,0:T(8,128...) custom-call(bf16[512,768]{1,0:T(8,128)(2,1)} %get-tuple-element.62.o, ...), custom_call_target="tpu_custom_call" | custom-call | tf_op jit(solution)/shard_map/finish/pallas_call | solution.py:1328
  (1 shorter events, 0.0 us)

commit v6 on v5

--- a/solution.py
+++ b/solution.py
@@ -161,6 +161,57 @@
         f = (2 * self.z + self.c + 8 - k) % 8
         return remote(self.small.at[f], self.small.at[f], self.vs.at[k - 1], self.vr.at[k - 1], (self.r, f))
 
+    def z_half(self, u, k, m, come=False):
+        q = 2 * m + (self.r % 2, self.r // 2)[m]
+        ref = self.block(u, q, hop(self.z, k if come else 2 * (k == 3)), self.c)
+        n = 2 * (k - 1) + m
+        return remote(ref, ref, self.zs.at[u, n], self.zr.at[u, n], (self.r, 2 * hop(self.z, 1 + (k == 2)) + self.c))
+
+    def x_half(self, u, k, m, come=False):
+        side = (self.r % 2, self.r // 2)[m]
+        ref = self.block(u, 2 * m + (1 - side if come else side), hop(self.z, k), self.c)
+        n = 2 * (k - 1) + m
+        return remote(ref, ref, self.xs.at[u, n], self.xr.at[u, n], (hop(self.r, m + 1), 2 * self.z + self.c))
+
+    def c_inner(self, n, come=False):
+        m, other = n % 2, n // 2
+        side = (self.r % 2, self.r // 2)[m]
+        ref = self.block(4, 2 * m + (1 - side if other else side), ALL, 1 - self.c if come else self.c)
+        return remote(ref, ref, self.cs.at[4, n], self.cr.at[4, n], (self.r, 2 * self.z + 1 - self.c))
+
+    def c_outer(self, k, come=False):
+        ref = self.w[2].at[hop(self.z, k), ds((1 - self.c if come else self.c) * 384, 384), :]
+        return remote(ref, ref, self.cs.at[5, k], self.cr.at[5, k], (self.r, 2 * self.z + 1 - self.c))
+
+    def start_half(self, u):
+        for k in (2, 1):
+            for m in range(2):
+                self.z_half(u, k, m).start()
+
+    def pass_half(self, u, k):
+        for m in range(2):
+            self.z_half(u, k, m, True).wait_recv()
+            if k == 2:
+                self.z_half(u, 3, m).start()
+            self.x_half(u, k, m).start()
+
+    def share_inner(self, n):
+        for k in (1, 2, 3) if n >= 2 else ():
+            self.x_half(4, k, n % 2, True).wait_recv()
+        self.c_inner(n).start()
+
+    def finish_inner(self):
+        for n in range(4):
+            self.c_inner(n, True).wait_recv()
+
+    def share_outer(self, k):
+        for m in range(2 if k else 0):
+            self.x_half(5, k, m, True).wait_recv()
+        self.c_outer(k).start()
+
+    def finish_outer(self, k):
+        self.c_outer(k, True).wait_recv()
+
     def z_copy(self, u, k, come=False):
         far = hop(self.z, k)
         ref = self.block(u, self.r, far if come else self.z, self.c)
@@ -172,16 +223,10 @@
         at = 3 * (k - 1) + m - 1
         return remote(ref, ref, self.xs.at[u, at], self.xr.at[u, at], (far, 2 * self.z + self.c))
 
-    def c_copy(self, u, m, come=False):
+    def c_copy(self, u, come=False):
         c = 1 - self.c if come else self.c
-        if isinstance(u, int) and u > PIECES:
-            ref = self.block(u, hop(self.r, m), ALL, c)
-        else:
-            ref = self.w[0].at[matrices(u), ALL, ds(c * 96, 96), columns(u)]
-        return remote(ref, ref, self.cs.at[u, m], self.cr.at[u, m], (self.r, 2 * self.z + 1 - self.c))
-
-    def parts(self, u):
-        return 4 if isinstance(u, int) and u > PIECES else 1
+        ref = self.w[0].at[matrices(u), ALL, ds(c * 96, 96), columns(u)]
+        return remote(ref, ref, self.cs.at[u, 0], self.cr.at[u, 0], (self.r, 2 * self.z + 1 - self.c))
 
     def start_z(self, u):
         for k in (1, 2, 3):
@@ -194,19 +239,13 @@
                 self.x_copy(u, k, m).start()
 
     def share(self, u):
-        parts = self.parts(u)
-        for m in range(4):
-            if m:
-                for k in (1, 2, 3):
-                    self.x_copy(u, k, m, True).wait_recv()
-            if parts == 4:
-                self.c_copy(u, m).start()
-        if parts == 1:
-            self.c_copy(u, 0).start()
+        for m in (1, 2, 3):
+            for k in (1, 2, 3):
+                self.x_copy(u, k, m, True).wait_recv()
+        self.c_copy(u).start()
 
     def finish(self, u):
-        for m in range(self.parts(u)):
-            self.c_copy(u, m, True).wait_recv()
+        self.c_copy(u, True).wait_recv()
 
     def drain(self):
         for k in range(1, 8):
@@ -217,20 +256,27 @@
                 self.z_copy(u, k).wait_send()
                 for m in (1, 2, 3):
                     self.x_copy(u, k, m).wait_send()
-            for m in range(self.parts(u)):
-                self.c_copy(u, m).wait_send()
+            self.c_copy(u).wait_send()
 
         lax.fori_loop(0, PIECES, lambda u, carry: (sent(u), carry)[1], 0)
-        for u in (3, 4, 5):
-            sent(u)
+        sent(3)
+        for k in range(4):
+            self.c_inner(k).wait_send()
+            self.c_outer(k).wait_send()
+            for u, m in ((4, 0), (4, 1), (5, 0), (5, 1)) if k else ():
+                self.z_half(u, k, m).wait_send()
+                self.x_half(u, k, m).wait_send()
 
 
 def unpack_small(small_s, vec_s):
     blocks = [small_s[f] for f in range(8)]
-    at = lax.broadcasted_iota(jnp.int32, (1024, D), 0)
-    want = lax.broadcasted_iota(jnp.int32, (1024, D), 1)
-    spread = jnp.where((at % 128 < 96) & (want == (at // 128) * 96 + at % 128), 1.0, 0.0).astype(BF16)
-    vec_s[...] = mm(jnp.concatenate(blocks, axis=1), spread)
+    at = lax.broadcasted_iota(jnp.int32, (128, D), 0)
+    shift = jnp.where(at < 96, lax.broadcasted_iota(jnp.int32, (128, D), 1) - at, -1)
+    total = None
+    for f in range(8):
+        part = mm(blocks[f], jnp.where(shift == 96 * f, 1.0, 0.0).astype(BF16))
+        total = part if total is None else total + part
+    vec_s[...] = total
     wide = [b.astype(F32) for b in blocks]
     for m in range(4):
         for j in range(6):
@@ -239,7 +285,7 @@
 
 
 def lines_of(rows):
-    bucket = bucket_of(lax.broadcasted_iota(jnp.int32, (128, 1024), 1) - 512)
+    bucket = jnp.broadcast_to(bucket_of(lax.broadcasted_iota(jnp.int32, (1, 1024), 1) - 512), (128, 1024))
     entry = lax.broadcasted_iota(jnp.int32, (128, 1024), 0)
 
     def pick(first, shift):
@@ -277,10 +323,13 @@
     return [line[h : h + 1] for h in range(HEADS)]
 
 
-def build_strip(lines, strip_s):
-    for h in range(HEADS):
-        wide = jnp.broadcast_to(lines[h], (128, 1024))
-        strip_s[h] = pltpu.roll(wide, 0, 1, stride=1, stride_axis=0)[:, 128:]
+def build_strip(lines, strip_s, heads):
+    for h in heads:
+        line = lines[h]
+        wide = jnp.broadcast_to(line[:, 256:768], (128, 512))
+        strip_s[h, :, 0:256] = jnp.broadcast_to(line[:, 0:1], (128, 256))
+        strip_s[h, :, 256:640] = pltpu.roll(wide, 0, 1, stride=1, stride_axis=0)[:, 128:]
+        strip_s[h, :, 640:896] = jnp.broadcast_to(line[:, 1023:1024], (128, 256))
 
 
 def square(w_s, m, cols=slice(None)):
@@ -307,11 +356,12 @@
                 ref[s, 2 * p + e] = piece
 
 
-def attend(q_s, k_s, v_s, strip_s, mask_s, p_st, ctx_s, hp, slot):
+def attend(q_s, k_s, v_s, strip_s, mask_s, p_st, ctx_s, hp, slot, ahead):
     lane = lax.broadcasted_iota(jnp.int32, (SEQ, 128), 1)
     k = k_s[hp]
     v = v_s[hp]
     for s in range(2):
+        ahead(s)
         q = q_s[s, hp]
         outs = []
         for e in range(2):
@@ -342,12 +392,18 @@
 
 
 NETWORK = {
-    (0, 0): (("pass_on", 2), ("start_z", 3), ("start_z", 4)),
+    (0, 0): (("pass_on", 2),),
     (0, 1): (("share", 1),),
-    (1, 0): (("pass_on", 3), ("start_z", 5)),
-    (1, 1): (("share", 2), ("pass_on", 4)),
-    (2, 0): (("share", 3),),
-    (2, 1): (("pass_on", 5),),
+    (1, 0): (("share", 2),),
+    (1, 3): (("pass_half", 4, 2), ("pass_half", 4, 1)),
+    (2, 0): (("pass_on", 3), ("start_half", 5)),
+}
+
+
+FEED_NETWORK = {
+    4: (("share_outer", 1), ("share_outer", 2)),
+    6: (("pass_half", 5, 3),),
+    9: (("share_outer", 3),),
 }
 
 
@@ -382,8 +438,8 @@
             net.small_copy(k).start()
         for copy in own[0]:
             copy.wait()
-        for u in range(PIECES):
-            net.start_z(u)
+        net.start_z(0)
+        net.start_z(1)
     else:
         loads = [pltpu.make_async_copy(src, dst, w_sem.at[i, 0]) for i, (src, dst) in enumerate(zip(weights, copies))]
         for copy in loads:
@@ -397,17 +453,23 @@
     def attention(strip_s, mask_s, p_st):
         build_masks(len_ref, rank_ref, mask_s)
         if linked:
+            net.pass_on(0)
+            net.start_z(2)
             for k in range(1, 8):
                 net.small_come(k).wait_recv()
-            build_strip(lines_of(unpack_small(small_s, vec_ref)), strip_s)
-            net.pass_on(0)
+            lines = lines_of(unpack_small(small_s, vec_ref))
             net.pass_on(1)
             for copy in own[1] + own[2]:
                 copy.wait()
+            net.start_half(4)
+            net.start_z(3)
+            build_strip(lines, strip_s, range(0, 4))
             net.share(0)
+            net.share_outer(0)
+            build_strip(lines, strip_s, range(4, HEADS))
             keep(vec_ref, vec_h)
         else:
-            build_strip(lines_of_table(tab_ref), strip_s)
+            build_strip(lines_of_table(tab_ref), strip_s, range(HEADS))
             loads[0].wait()
 
         def store(hp, slot):
@@ -418,22 +480,23 @@
                 if when == part:
                     @pl.when(p == at)
                     def _(moves=moves):
-                        for name, u in moves:
-                            getattr(net, name)(u)
+                        for name, *unit in moves:
+                            getattr(net, name)(*unit)
 
         def step(p, carry):
             if linked:
                 net.finish(p)
             project(x_ref, y_ref, vec_ref, wa_s, q_s, k_s, v_s, p)
             for part in range(2):
-                if linked:
-                    hooks(p, part)
-
                 @pl.when(p >= 1)
                 def _():
                     store(2 * p - 2 + part, part).wait()
 
-                attend(q_s, k_s, v_s, strip_s, mask_s, p_st, ctx_s, 2 * p + part, part)
+                def ahead(s, part=part):
+                    if linked:
+                        hooks(p, 2 * part + s)
+
+                attend(q_s, k_s, v_s, strip_s, mask_s, p_st, ctx_s, 2 * p + part, part, ahead)
                 store(2 * p + part, part).start()
             return carry
 
@@ -452,6 +515,10 @@
     )
     keep(ctx_s, ctx_h)
     if linked:
+        net.share(3)
+        net.pass_half(4, 3)
+        net.share_inner(0)
+        net.share_inner(1)
         net.finish(3)
         keep(wa_s, weights[0])
 
@@ -472,8 +539,11 @@
     keep(nl_s, nl_h)
 
     if linked:
-        net.share(4)
-        net.finish(4)
+        net.share_inner(2)
+        net.share_inner(3)
+        net.pass_half(5, 2)
+        net.pass_half(5, 1)
+        net.finish_inner()
         keep(wi_s, weights[1])
     else:
         loads[1].wait()
@@ -498,9 +568,11 @@
                     c.wait()
 
             if linked:
-                @pl.when(t == 9)
-                def _():
-                    net.share(5)
+                for at, moves in FEED_NETWORK.items():
+                    @pl.when(t == at)
+                    def _(moves=moves):
+                        for name, *unit in moves:
+                            getattr(net, name)(*unit)
 
             cols = ds((t % 3) * TILE, TILE)
             inner = mm(nl_s[...], square(wi_s, t // 3, cols)) + vec_ref[pl.ds(8 + (t // 3), 1), cols]
@@ -512,16 +584,21 @@
             return carry
 
         lax.fori_loop(0, TILES, step, 0)
+        z = places()[1] if linked else 0
+        for k in range(4):
+            if linked:
+                net.finish_outer(k)
+            far = hop(z, k)
+
+            def outer(i, carry, k=k, far=far):
+                rows = ds(i * 512, 512)
+                part = mm(act_s[rows, ds(far * D, D)], wo_s[far])
+                br_s[rows, :] = part + br_s[rows, :] if k else part
+                return carry
+
+            lax.fori_loop(0, ROWS // 512, outer, 0)
         if linked:
-            net.finish(5)
             keep(wo_s, weights[2])
-
-        def outer(i, carry):
-            rows = ds(i * 256, 256)
-            br_s[rows, :] = mm(act_s[rows, :], wo_s[...].reshape(FF, D))
-            return carry
-
-        lax.fori_loop(0, ROWS // 256, outer, 0)
         for t in (TILES - 2, TILES - 1):
             for c in pair(t, t % 2):
                 c.wait()
@@ -576,7 +653,7 @@
         outs += [shape((16, D), F32)] + [shape(w, BF16) for w in WEIGHTS]
         scratch += [
             pltpu.VMEM((8, 16, 128), BF16), pltpu.VMEM((16, D), F32),
-            dma((6, 3)), dma((6, 3)), dma((6, 9)), dma((6, 9)), dma((6, 4)), dma((6, 4)), dma((7,)), dma((7,)),
+            dma((6, 6)), dma((6, 6)), dma((6, 9)), dma((6, 9)), dma((6, 4)), dma((6, 4)), dma((7,)), dma((7,)),
         ]
         params = pltpu.CompilerParams(vmem_limit_bytes=VMEM_LIMIT, collective_id=1, has_side_effects=True)
     else:
@@ -693,7 +770,7 @@
     def cores(self, kind, i=0):
         self.core(kind, i).wait_recv()
         ref, come = self.mine(kind, i)
-        ref[...] = (ref[...].astype(F32) + come[...].astype(F32)).astype(BF16)
+        ref[...] = ref[...] + come[...]
         for m in range(2):
             self.across(kind, i, m).start()
 
@@ -706,7 +783,7 @@
         for m in range(2):
             self.across(kind, i, m).wait_recv()
             ref = self.half(kind, i, m, ALL)
-            ref[...] = (ref[...].astype(F32) + self.held(0, kind, i, m)[...].astype(F32)).astype(BF16)
+            ref[...] = ref[...] + self.held(0, kind, i, m)[...]
             if kind == "out":
                 @pl.when((self.z + i) % 2 == 1)
                 def _(m=m):
@@ -722,7 +799,7 @@
                 for m in range(2):
                     self.near(kind, i, m).wait_recv()
                     ref = self.half(kind, i, m, None)
-                    ref[...] = (ref[...].astype(F32) + self.held(1, kind, i, m)[...].astype(F32)).astype(BF16)
+                    ref[...] = ref[...] + self.held(1, kind, i, m)[...]
 
                     @pl.when(self.z != i)
                     def _(m=m):
@@ -732,7 +809,7 @@
             for j in (1, 0):
                 self.near(kind, i, m, j).wait_recv()
                 ref = self.half(kind, i, m, hop(self.z, 2 * j))
-                ref[...] = (ref[...].astype(F32) + self.held(1, kind, i, m).at[j][...].astype(F32)).astype(BF16)
+                ref[...] = ref[...] + self.held(1, kind, i, m).at[j][...]
                 if j:
                     self.far(kind, i, m).start()
 
@@ -834,17 +911,16 @@
 
 
 def pack_small(vec_ref, table, out_ref):
-    want = lax.broadcasted_iota(jnp.int32, (D, 1024), 0)
-    at = lax.broadcasted_iota(jnp.int32, (D, 1024), 1)
-    gathered = jnp.where((at % 128 < 96) & (want == (at // 128) * 96 + at % 128), 1.0, 0.0)
     vec = vec_ref[...]
-    rows = lax.dot_general(
-        vec[0:8], gathered, (((1,), (0,)), ((), ())), precision=lax.Precision.HIGHEST, preferred_element_type=F32
-    )
+    at = lax.broadcasted_iota(jnp.int32, (D, 128), 1)
+    shift = jnp.where(at < 96, lax.broadcasted_iota(jnp.int32, (D, 128), 0) - at, -1)
     lane = lax.broadcasted_iota(jnp.int32, (1, 128), 1)
     for f in range(8):
         m = f // 2
-        out_ref[f, 0:8, :] = rows[:, f * 128 : (f + 1) * 128]
+        out_ref[f, 0:8, :] = lax.dot_general(
+            vec[0:8], jnp.where(shift == 96 * f, 1.0, 0.0), (((1,), (0,)), ((), ())),
+            precision=lax.Precision.HIGHEST, preferred_element_type=F32,
+        )
         for j in range(3):
             col = (f % 2) * 384 + j * 128
             out_ref[f, 8 + j : 9 + j, :] = vec[8 + m : 9 + m, col : col + 128]
@@ -868,7 +944,6 @@
 BACK_NETWORK = {
     (0, 0): (("replicas", "out", 3), ("replicas", "in", 3), ),
     (0, 1): (("pairs", "out", 2), ("pairs", "in", 2), ("replicas", "square"), ),
-    (1, 0): (),
     (1, 1): (("cores", "piece", 0), ),
     (2, 0): (("replicas", "piece", 0), ("pairs", "out", 3), ("pairs", "in", 3), ("pairs", "square"), ("owners", "in", 0), ("owners", "in", 1), ),
     (2, 1): (("cores", "piece", 1), ),
@@ -876,11 +951,11 @@
 
 LAST_NETWORK = (
     (("cores", "piece", 2), ),
-    (("replicas", "piece", 1), ("pairs", "piece", 0), ("owners", "out"), ),
-    (("owners", "in", 2), ("owners", "square"), ("ends", "in", 0), ("ends", "in", 1), ),
-    (("replicas", "piece", 2), ("pairs", "piece", 1), ("owners", "in", 3), ("sum_middle",), ),
-    (("owners", "piece", 0), ("ends", "out"), ("ends", "in", 2), ("ends", "square"), ),
-    (("pairs", "piece", 2), ("owners", "piece", 1), ("ends", "in", 3), ("ends", "piece", 0), ("owners", "piece", 2), ("ends", "piece", 1), ("ends", "piece", 2), ),
+    (("replicas", "piece", 1), ("pairs", "piece", 0), ("owners", "out"), ("owners", "in", 2), ),
+    (("replicas", "piece", 2), ("owners", "square"), ("ends", "in", 0), ("ends", "in", 1), ),
+    (("pairs", "piece", 1), ("owners", "in", 3), ("ends", "out"), ("ends", "in", 2), ("sum_middle",), ),
+    (("pairs", "piece", 2), ("owners", "piece", 0), ("ends", "square"), ("ends", "in", 3), ),
+    (("owners", "piece", 1), ("ends", "piece", 0), ("owners", "piece", 2), ("ends", "piece", 1), ("ends", "piece", 2), ),
 )
 
 

time: 213 us -> 205 us (0.962)
  Pallas kernels: 208 us -> 200 us
    pallas_call x1, Pallas kernels: 110 us -> 105 us  [call_backward(): pl.pallas_call(functools.partial(backward_kernel, linked), out_shape=outs...]
    pallas_call x1, Pallas kernels: 90.9 us -> 88.2 us  [call_forward(): pl.pallas_call(functools.partial(forward_kernel, linked), out_shape=outs,...]
where the time goes in v6:
time: 205 us
  Pallas kernels  200 us (98%)
    pallas_call x1, Pallas kernels, call_backward(): pl.pallas_call(functools.partial(backward_kernel, linked), out_shape=outs...  105 us
    pallas_call x1, Pallas kernels, call_forward(): pl.pallas_call(functools.partial(forward_kernel, linked), out_shape=outs,...  88.2 us
    pallas_call x1, Pallas kernels, call_finish(): pl.pallas_call(finish_kernel, out_shape=outs, in_specs=[hbm] * 4 + [vmem]...  7.16 us

profile of v6, /device:TPU:0, one launch (start us, length us, event | category | flops | bytes accessed | tf_op | source)
XLA Modules:
  0.0 204.6 jit_solution(1063597837519598375)
XLA Ops:
  1.3 0.7 pad_bitcast_fusion
  2.0 0.1 pad.13.clone
  2.0 0.8 stack.35
  2.8 1.3 fusion.3.refs_4_
  4.2 88.2 %forward.1 = (bf16[512,768]{1,0:T(8,128)(2,1)}, bf16[512,768]{1,0:T(8,128)(2,1)}, bf16[2,6,512,128]{3,2,1,0:T(8,128)(2,1)}, bf16[6,512,128]{2,1,0:T(8,128)(2,1)}...) custom-call(bf16[512,768]{1,0:T(8,128)(2,1)} %refs_0_.3, ...), custom_call_target="tpu_custom_call" | custom-call | tf_op jit(solution)/shard_map/forward/pallas_call | solution.py:662
  92.4 104.8 %backward.1 = (f32[512,768]{1,0:T(8,128)}, f32[512,768]{1,0:T(8,128)}, bf16[3,4,96,768]{3,2,1,0:T(8,128)(2,1)}, f32[16,128]{1,0:T(8,128)}) custom-call(bf16[512,768]{1,0:T(8,128)(2,1)} %refs_0_.3, bf16[512,768]{1,0:T(8,128)(2,1)} %refs_1_.3, bf16[512,768]{1,0:T(8,128)(2,1)} %refs_2_.2, bf16[512,768]{1,0:T(8,128)(2,1)} %refs_3_.3, ...), custom_call_target="tpu_custom_call" | custom-call | tf_op jit(solution)/shard_map/backward/pallas_call | solution.py:1354
  197.2 7.2 %finish.1 = (bf16[512,768]{1,0:T(8,128)(2,1)}, bf16[512,768]{1,0:T(8,128)(2,1)}, f32[512,768]{1,0:T(8,128)}, f32[512,768]{1,0:T(8,128)}, f32[96,768]{1,0:T(8,128...) custom-call(bf16[512,768]{1,0:T(8,128)(2,1)} %get-tuple-element.62.o, ...), custom_call_target="tpu_custom_call" | custom-call | tf_op jit(solution)/shard_map/finish/pallas_call | solution.py:1403
  (1 shorter events, 0.0 us)

commit v7 on v6

--- a/solution.py
+++ b/solution.py
@@ -401,9 +401,9 @@
 
 
 FEED_NETWORK = {
-    4: (("share_outer", 1), ("share_outer", 2)),
-    6: (("pass_half", 5, 3),),
-    9: (("share_outer", 3),),
+    5: (("share_outer", 1), ("share_outer", 2)),
+    7: (("pass_half", 5, 3),),
+    11: (("share_outer", 3),),
 }
 
 
@@ -523,6 +523,10 @@
         keep(wa_s, weights[0])
 
     for s, in_ref in ((0, x_ref), (1, y_ref)):
+        if linked and s:
+            net.share_inner(2)
+            net.share_inner(3)
+
         def first(i, carry, s=s, in_ref=in_ref):
             own = ds(i * 256, 256)
             rows = ds(s * SEQ + i * 256, 256)
@@ -539,8 +543,6 @@
     keep(nl_s, nl_h)
 
     if linked:
-        net.share_inner(2)
-        net.share_inner(3)
         net.pass_half(5, 2)
         net.pass_half(5, 1)
         net.finish_inner()
@@ -1109,7 +1111,12 @@
             for kind in ("out", "in"):
                 net.replicas(kind, 2)
         tr_s[...] = ctx_s[...].T
-        ga_s[3] = mm(tr_s[...], db_s[...]).astype(BF16).reshape(4, 192, D)
+
+        def square_grad(j, carry):
+            ga_s[3, j] = mm(tr_s[pl.ds(pl.multiple_of(j * 192, 192), 192), :], db_s[...]).astype(BF16)
+            return carry
+
+        lax.fori_loop(0, 4, square_grad, 0)
         if linked:
             pl.semaphore_wait(net.credit, 1)
             net.start("square")
@@ -1362,35 +1369,51 @@
     )(x, y, cc, cq, vecs, wa, wi, wo, *saved)
 
 
-def finish_kernel(oc_h, oq_h, gc_h, gq_h, res_ref, small_ref, oc_o, oq_o, gc_o, gq_o, wq, wk, wv, wo, wi, wf, *rest):
-    *vectors, low_s, high_s, in_sem, out_sem = rest
+def finish_kernel(oc_h, oq_h, gc_h, gq_h, res_h, small_ref, oc_o, oq_o, gc_o, gq_o, *rest):
+    *weights, low_s, high_s, res_s, square_s, inner_s, outer_s, in_sem, out_sem = rest
+    weights, vectors = weights[:6], weights[6:]
+    held = [square_s.at[q] for q in range(4)] + [inner_s, outer_s]
+    grads = [pltpu.make_async_copy(res_h.at[t], res_s.at[t], in_sem.at[8 + t]) for t in (2, 1, 0)]
     moves = []
     for i, (src, dst) in enumerate(((gc_h, gc_o), (gq_h, gq_o), (oc_h, oc_o), (oq_h, oq_o))):
-        held = (high_s if i < 2 else low_s).at[i % 2]
+        room = (high_s if i < 2 else low_s).at[i % 2]
         for part in range(2):
             rows = slice(part * SEQ // 2, (part + 1) * SEQ // 2)
             n = len(moves)
             moves.append((
-                pltpu.make_async_copy(src.at[rows, :], held.at[rows, :], in_sem.at[n]),
-                pltpu.make_async_copy(held.at[rows, :], dst.at[rows, :], out_sem.at[n]),
+                pltpu.make_async_copy(src.at[rows, :], room.at[rows, :], in_sem.at[n]),
+                pltpu.make_async_copy(room.at[rows, :], dst.at[rows, :], out_sem.at[n]),
             ))
+    for copy in grads:
+        copy.start()
     for move, _ in moves:
         move.start()
+    writes = [pltpu.make_async_copy(src, dst, out_sem.at[8 + i]) for i, (src, dst) in enumerate(zip(held, weights))]
     small = small_ref[...]
     for i in range(8):
         vectors[i][...] = small[i, :96]
     for j in range(3):
         vectors[8][j * 128 : (j + 1) * 128] = small[8 + j]
     vectors[9][...] = small[11, :48]
+    grads[0].wait()
     for q in range(4):
-        (wq, wk, wv, wo)[q][...] = res_ref[0, q].astype(F32)
-        wi[:, q * D : (q + 1) * D] = res_ref[1, q].astype(F32)
-        wf[q * 96 : (q + 1) * 96, :] = res_ref[2, q].astype(F32)
+        outer_s[q * 96 : (q + 1) * 96, :] = res_s[2, q].astype(F32)
+    writes[5].start()
+    grads[1].wait()
+    for q in range(4):
+        inner_s[:, q * D : (q + 1) * D] = res_s[1, q].astype(F32)
+    writes[4].start()
+    grads[2].wait()
+    for q in range(4):
+        square_s[q] = res_s[0, q].astype(F32)
+        writes[q].start()
     for move, onward in moves:
         move.wait()
         onward.start()
     for _, onward in moves:
         onward.wait()
+    for copy in writes:
+        copy.wait()
 
 
 def call_finish(oc, oq, gc, gq, res, small):
@@ -1403,12 +1426,14 @@
     return pl.pallas_call(
         finish_kernel,
         out_shape=outs,
-        in_specs=[hbm] * 4 + [vmem] * 2,
-        out_specs=[hbm] * 4 + [vmem] * 16,
+        in_specs=[hbm] * 5 + [vmem],
+        out_specs=[hbm] * 10 + [vmem] * 10,
         scratch_shapes=[
-            pltpu.VMEM((2, SEQ, D), BF16), pltpu.VMEM((2, SEQ, D), F32),
-            pltpu.SemaphoreType.DMA((8,)), pltpu.SemaphoreType.DMA((8,)),
+            pltpu.VMEM((2, SEQ, D), BF16), pltpu.VMEM((2, SEQ, D), F32), pltpu.VMEM((3, 4, 96, D), BF16),
+            pltpu.VMEM((4, 96, D), F32), pltpu.VMEM((96, FF), F32), pltpu.VMEM((384, D), F32),
+            pltpu.SemaphoreType.DMA((11,)), pltpu.SemaphoreType.DMA((14,)),
         ],
+        compiler_params=pltpu.CompilerParams(vmem_limit_bytes=VMEM_LIMIT),
         name="finish",
     )(oc, oq, gc, gq, res, small)
 

time: 205 us -> 203 us (level)
  no operation moved by 1% of the time
where the time goes in v7:
time: 203 us
  Pallas kernels  199 us (98%)
    pallas_call x1, Pallas kernels, call_backward(): pl.pallas_call(functools.partial(backward_kernel, linked), out_shape=outs...  104 us
    pallas_call x1, Pallas kernels, call_forward(): pl.pallas_call(functools.partial(forward_kernel, linked), out_shape=outs,...  87.7 us
    pallas_call x1, Pallas kernels, call_finish(): pl.pallas_call(finish_kernel, out_shape=outs, in_specs=[hbm] * 5 + [vmem]...  7.02 us

profile of v7, /device:TPU:0, one launch (start us, length us, event | category | flops | bytes accessed | tf_op | source)
XLA Modules:
  0.0 202.9 jit_solution(1878750312290563213)
XLA Ops:
  1.3 0.7 pad_bitcast_fusion
  2.0 0.1 pad.13.clone
  2.0 0.8 stack.35
  2.8 1.3 fusion.3.refs_4_
  4.2 87.7 %forward.1 = (bf16[512,768]{1,0:T(8,128)(2,1)}, bf16[512,768]{1,0:T(8,128)(2,1)}, bf16[2,6,512,128]{3,2,1,0:T(8,128)(2,1)}, bf16[6,512,128]{2,1,0:T(8,128)(2,1)}...) custom-call(bf16[512,768]{1,0:T(8,128)(2,1)} %refs_0_.3, ...), custom_call_target="tpu_custom_call" | custom-call | tf_op jit(solution)/shard_map/forward/pallas_call | solution.py:664
  91.9 103.9 %backward.1 = (f32[512,768]{1,0:T(8,128)}, f32[512,768]{1,0:T(8,128)}, bf16[3,4,96,768]{3,2,1,0:T(8,128)(2,1)}, f32[16,128]{1,0:T(8,128)}) custom-call(bf16[512,768]{1,0:T(8,128)(2,1)} %refs_0_.3, bf16[512,768]{1,0:T(8,128)(2,1)} %refs_1_.3, bf16[512,768]{1,0:T(8,128)(2,1)} %refs_2_.2, bf16[512,768]{1,0:T(8,128)(2,1)} %refs_3_.3, ...), custom_call_target="tpu_custom_call" | custom-call | tf_op jit(solution)/shard_map/backward/pallas_call | solution.py:1361
  195.8 7.0 %finish.1 = (bf16[512,768]{1,0:T(8,128)(2,1)}, bf16[512,768]{1,0:T(8,128)(2,1)}, f32[512,768]{1,0:T(8,128)}, f32[512,768]{1,0:T(8,128)}, f32[96,768]{1,0:T(8,128...) custom-call(bf16[512,768]{1,0:T(8,128)(2,1)} %get-tuple-element.62.o, ...), custom_call_target="tpu_custom_call" | custom-call | tf_op jit(solution)/shard_map/finish/pallas_call | solution.py:1426
  (1 shorter events, 0.0 us)

commit v8 on v7

--- a/solution.py
+++ b/solution.py
@@ -412,7 +412,7 @@
     take = lambda n: [refs.pop(0) for _ in range(n)]
     x_ref, y_ref, len_ref, rank_ref = take(4)
     if linked:
-        (small_ref,) = take(1)
+        rows_ref, inner_ref, table_ref = take(3)
         shards = take(6)
     else:
         vec_ref, tab_ref, *weights = take(5)
@@ -430,7 +430,11 @@
         for batch in own:
             for copy in batch:
                 copy.start()
-        small_s[f] = small_ref[...]
+        vec_ref[:, 0:128] = jnp.zeros((16, 128), F32)
+        vec_ref[0:8, 0:96] = rows_ref[...].astype(F32)
+        vec_ref[8:11, 0:128] = inner_ref[...].astype(F32)
+        vec_ref[11:12, 0:48] = table_ref[...].astype(F32)
+        small_s[f] = vec_ref[:, 0:128].astype(BF16)
         greet(
             [(hop(r, m), f) for m in (1, 2, 3)] + [(r, (f + k) % 8) for k in range(1, 8)]
         )
@@ -651,7 +655,7 @@
     ]
     in_specs = [vmem, vmem, smem, vmem]
     if linked:
-        in_specs += [vmem] + [hbm] * 6
+        in_specs += [vmem] * 3 + [hbm] * 6
         outs += [shape((16, D), F32)] + [shape(w, BF16) for w in WEIGHTS]
         scratch += [
             pltpu.VMEM((8, 16, 128), BF16), pltpu.VMEM((16, D), F32),
@@ -1448,11 +1452,9 @@
     linked = width * 8 == D and lax.axis_size("rep") == 4
     front = (content_stream, query_stream, lengths, ranking)
     if linked:
-        rows = jnp.pad(jnp.stack(small), ((0, 0), (0, 128 - width)))
-        rest = jnp.pad(bucket_bias, (0, 128 - bucket_bias.shape[0])).reshape(1, 128)
-        packed = jnp.concatenate([rows, inner_bias.reshape(3, 128), rest, jnp.zeros((4, 128), BF16)])
+        packed = (jnp.stack(small), inner_bias.reshape(3, 128), bucket_bias.reshape(1, -1))
         out_c, out_q, *saved, vecs, wa, wi, wo = call_forward(
-            True, *front, packed, query_weight, key_weight, value_weight, output_weight, inner_weight, outer_weight
+            True, *front, *packed, query_weight, key_weight, value_weight, output_weight, inner_weight, outer_weight
         )
     else:
         def gather(a, axis=0):

time: 203 us -> 202 us (level)
  no operation moved by 1% of the time
where the time goes in v8:
time: 202 us; the launch traced here: 201 us
  Pallas kernels  199 us (99%)
    pallas_call x1, Pallas kernels, call_backward(): pl.pallas_call(functools.partial(backward_kernel, linked), out_shape=outs...  104 us
    pallas_call x1, Pallas kernels, call_forward(): pl.pallas_call(functools.partial(forward_kernel, linked), out_shape=outs,...  87.7 us
    pallas_call x1, Pallas kernels, call_finish(): pl.pallas_call(finish_kernel, out_shape=outs, in_specs=[hbm] * 5 + [vmem]...  7.02 us

profile of v8, /device:TPU:0, one launch (start us, length us, event | category | flops | bytes accessed | tf_op | source)
XLA Modules:
  0.0 201.5 jit_solution(18339212187107853078)
XLA Ops:
  1.3 1.4 stack.35.refs_4_
  2.7 87.7 %forward.1 = (bf16[512,768]{1,0:T(8,128)(2,1)}, bf16[512,768]{1,0:T(8,128)(2,1)}, bf16[2,6,512,128]{3,2,1,0:T(8,128)(2,1)}, bf16[6,512,128]{2,1,0:T(8,128)(2,1)}...) custom-call(bf16[512,768]{1,0:T(8,128)(2,1)} %refs_0_.3, ...), custom_call_target="tpu_custom_call" | custom-call | tf_op jit(solution)/shard_map/forward/pallas_call | solution.py:668
  90.4 103.9 %backward.1 = (f32[512,768]{1,0:T(8,128)}, f32[512,768]{1,0:T(8,128)}, bf16[3,4,96,768]{3,2,1,0:T(8,128)(2,1)}, f32[16,128]{1,0:T(8,128)}) custom-call(bf16[512,768]{1,0:T(8,128)(2,1)} %refs_0_.3, bf16[512,768]{1,0:T(8,128)(2,1)} %refs_1_.3, bf16[512,768]{1,0:T(8,128)(2,1)} %refs_2_.2, bf16[512,768]{1,0:T(8,128)(2,1)} %refs_3_.3, ...), custom_call_target="tpu_custom_call" | custom-call | tf_op jit(solution)/shard_map/backward/pallas_call | solution.py:1365
  194.3 7.0 %finish.1 = (bf16[512,768]{1,0:T(8,128)(2,1)}, bf16[512,768]{1,0:T(8,128)(2,1)}, f32[512,768]{1,0:T(8,128)}, f32[512,768]{1,0:T(8,128)}, f32[96,768]{1,0:T(8,128...) custom-call(bf16[512,768]{1,0:T(8,128)(2,1)} %get-tuple-element.62.o, ...), custom_call_target="tpu_custom_call" | custom-call | tf_op jit(solution)/shard_map/finish/pallas_call | solution.py:1430
